TPU v7x, 128 devices: a whole 4x4x4 slice. The times are simulated.
128 devices in a mesh: space: 32 (over x, z_lo, y), member: 4 (over z_hi, core).
Axes of the slice: x: 4, y: 4, z: 4 (z_hi: 2, z_lo: 2; z = z_hi * 2 + z_lo), core: 2. Of those that a mesh axis runs over, the one named last changes fastest.
Arguments:
- latent: bfloat16 [8, 768, 4096], P('member', None, 'space'), may hold values from -6 to 6
- send_rows: int32 [2, 512], P(None, 'space'), may hold values from 0 to 127, as said below
- neighbours: int32 [8, 4096], P(None, 'space'), may hold values from 0 to 159, as said below
- degree: int32 [4096], P('space'), may hold values from 4 to 8
- dec_nodes: int32 [3, 32768], P(None, 'space'), may hold values from 0 to 127, as said below
- counts: int32 [32], replicated, may hold values from 512 to 1024, as said below
- targets: float32 [83, 32768], P(None, 'space')
- member_noise: float32 [8, 32], P('member'), may hold values from -5 to 5
- w_qkv: bfloat16 [768, 2304], replicated, may hold values from -0.21875 to 0.21875
- w_out: bfloat16 [768, 768], replicated, may hold values from -0.21875 to 0.21875
- w_noise: float32 [32, 768], replicated, may hold values from -0.5 to 0.5
- decoder_hidden_weight: bfloat16 [768, 768], replicated, may hold values from -0.21875 to 0.21875
- decoder_output_weight: bfloat16 [83, 768], replicated, may hold values from -0.21875 to 0.21875
Outputs:
- mean_fair_crps: float32 [], replicated
- d_latent: float32 [8, 768, 4096], P('member', None, 'space')
- grad_qkv: float32 [768, 2304], replicated
- grad_out: float32 [768, 768], replicated
- grad_noise: float32 [32, 768], replicated
- grad_dec1: float32 [768, 768], replicated
- grad_dec2: float32 [83, 768], replicated
Inputs may be any that keep to these rules, and one draw needn't show every extreme that they name: `neighbours`: entries index a shard's extended rows; slot 0 is the node itself, every entry lies within 16 rows of it. The first degree slots of a node are live. `send_rows`: local node indices; within each row of a shard distinct. `dec_nodes`: local node indices of the shard that holds the grid point; for the point at place p of its shard each entry lies from p * 128 // 1024 to 3 more. `counts`: the live points of a shard are its first ones.
All inputs are finite; a program needn't handle non-finite values.
Results may differ from a plain program's by a relative error of at most 0.024.
Values may be sent and summed in bfloat16 or wider, within the bound.
No kernel may reach another device: no remote copies, remote signals or barrier semaphores. Data moves between devices by JAX's collectives and lax.ppermute only.
A program may use at most 128 MiB of HBM per device.

v0:
```python
import jax
import jax.numpy as jnp
from jax import lax
from jax.experimental import pallas as pl
from jax.experimental.pallas import tpu as pltpu
from jax.sharding import PartitionSpec as P

HEADS = 6
HEAD = 128
EPS = 1e-5
F32 = jnp.float32
BF16 = jnp.bfloat16
NN = (((1,), (0,)), ((), ()))
NT = (((1,), (1,)), ((), ()))
TN = (((0,), (0,)), ((), ()))
VMEM = pl.BlockSpec(memory_space=pltpu.VMEM)
SMEM = pl.BlockSpec(memory_space=pltpu.SMEM)
PARAMS = pltpu.CompilerParams(vmem_limit_bytes=48 * 1024 * 1024)


def mm(a, b, dims=NN):
    return lax.dot_general(a, b, dims, preferred_element_type=F32)


def call(body, out_shape, *args, smem=(), flops=0, scratch=()):
    out_shape = [jax.ShapeDtypeStruct(s, d) for s, d in out_shape]
    size = sum(a.size * a.dtype.itemsize for a in args)
    size += sum(o.size * o.dtype.itemsize for o in out_shape)
    return pl.pallas_call(
        body,
        out_shape=out_shape,
        in_specs=[SMEM if i in smem else VMEM for i in range(len(args))],
        out_specs=[VMEM] * len(out_shape),
        scratch_shapes=list(scratch),
        compiler_params=PARAMS,
        cost_estimate=pl.CostEstimate(flops=flops, bytes_accessed=size, transcendentals=0),
    )(*args)


def gains(noise, w_noise):
    return 1.0 + lax.dot_general(
        noise, w_noise, NN, precision=lax.Precision.HIGHEST, preferred_element_type=F32
    )


def normalise(rows):
    centre = rows - jnp.mean(rows, axis=1, keepdims=True)
    inverse = lax.rsqrt(jnp.mean(centre * centre, axis=1, keepdims=True) + EPS)
    return centre * inverse, inverse


def norm_back(cotangent, gain, hat, inverse):
    d_hat = cotangent * gain
    mean = jnp.mean(d_hat, axis=1, keepdims=True)
    along = jnp.mean(d_hat * hat, axis=1, keepdims=True)
    return inverse * (d_hat - mean - hat * along)


def send_body(latent, rows, sent):
    nodes = latent.shape[2]
    rim = rows.shape[1]
    both = jnp.concatenate([rows[0:1, :], rows[1:2, :]], axis=1)
    table = lax.broadcasted_iota(jnp.int32, (nodes, 2 * rim), 0) == both
    table = table.astype(F32).T.astype(BF16)
    for m in range(latent.shape[0]):
        picked = mm(table, latent[m], NT).astype(BF16)
        sent[0, m] = picked[:rim]
        sent[1, m] = picked[rim:]


def local_body(latent, noise, w_noise, w_qkv, own, normed, proj):
    gain = gains(noise[...], w_noise[...])
    members, _, nodes = latent.shape
    for m in range(members):
        rows = latent[m].astype(F32).T
        own[m] = rows.astype(BF16)
        hat, _ = normalise(rows)
        normed[m * nodes : (m + 1) * nodes] = (hat * gain[m : m + 1]).astype(BF16)
    proj[...] = mm(normed[...], w_qkv[...]).astype(BF16)


def slot_mask(nbr, degree, rows):
    slots, nodes = nbr.shape
    index = lax.broadcasted_iota(jnp.int32, (rows, nodes), 0)
    total = jnp.zeros((rows, nodes), F32)
    for j in range(slots):
        live = (index == nbr[j : j + 1, :]) & (degree[...] > j)
        total = total + live.astype(F32)
    return total / degree[...].astype(F32)


def point_table(dec_nodes, nodes):
    points = dec_nodes.shape[1]
    index = lax.broadcasted_iota(jnp.int32, (nodes, points), 0)
    total = jnp.zeros((nodes, points), F32)
    for j in range(dec_nodes.shape[0]):
        total = total + (index == dec_nodes[j : j + 1, :]).astype(F32)
    return total.astype(BF16)


def extend(own, low, high):
    return jnp.concatenate([low, own, high], axis=0)


def forward_body(
    own, proj, low, high, noise, w_noise, w_qkv, w_out, w_hid, w_pred, nbr, degree, dec_nodes,
    normed_rim, proj_rim, attended, stored, hidden, slope, forecast, table,
):
    members, nodes, width = own.shape
    rim = low.shape[1]
    gain = gains(noise[...], w_noise[...])
    for m in range(members):
        rows = jnp.concatenate([low[m], high[m]], axis=0).astype(F32)
        hat, _ = normalise(rows)
        normed_rim[2 * rim * m : 2 * rim * (m + 1)] = (hat * gain[m : m + 1]).astype(BF16)
    proj_rim[...] = mm(normed_rim[...], w_qkv[:, width:]).astype(BF16)
    mask = slot_mask(nbr, degree, nodes + 2 * rim)
    for m in range(members):
        here = slice(m * nodes, (m + 1) * nodes)
        lo = slice(2 * rim * m, 2 * rim * m + rim)
        hi = slice(2 * rim * m + rim, 2 * rim * (m + 1))
        for h in range(HEADS):
            at = [slice(k * width + h * HEAD, k * width + (h + 1) * HEAD) for k in range(3)]
            rim_at = [slice(a.start - width, a.stop - width) for a in at]
            key = extend(proj[here, at[1]], proj_rim[lo, rim_at[1]], proj_rim[hi, rim_at[1]])
            value = extend(proj[here, at[2]], proj_rim[lo, rim_at[2]], proj_rim[hi, rim_at[2]])
            score = mm(key, proj[here, at[0]], NT) * HEAD**-0.5
            weight = (jax.nn.sigmoid(score) * mask).astype(BF16)
            attended[here, at[0]] = mm(weight, value, TN).astype(BF16)
    branch = mm(attended[...], w_out[...])
    for m in range(members):
        here = slice(m * nodes, (m + 1) * nodes)
        stored[here] = (own[m].astype(F32) + branch[here]).astype(BF16)
    table[...] = point_table(dec_nodes, nodes)
    mixed = mm(stored[...], w_hid[...]).astype(BF16)
    block = 256
    for m in range(members):
        part = mixed[m * nodes : (m + 1) * nodes]
        for g in range(0, dec_nodes.shape[1], block):
            pre = mm(part, table[:, g : g + block], TN) * (1.0 / 3.0)
            sig = 0.5 * jnp.tanh(0.5 * pre) + 0.5
            hid = pre * sig
            hidden[m, :, g : g + block] = hid.astype(BF16)
            slope[m, :, g : g + block] = (sig + hid * (1.0 - sig)).astype(BF16)
            forecast[m, :, g : g + block] = mm(
                w_pred[...], hidden[m, :, g : g + block]
            ).astype(BF16)


def smooth(v):
    square = v * v + 0.25
    inverse = lax.rsqrt(square)
    return square * inverse - 0.5, v * inverse


def crps_body(
    live_count, mine, *rest
):
    (*others, targets, hidden, slope, table, stored, attended, w_out, w_hid, w_pred,
     d_updated, d_attended, g_out, g_hid, g_pred, loss, d_pre, d_cast) = rest
    members, channels, points = mine.shape
    total = members * (1 + len(others))
    block = 256
    nodes = table.shape[0]
    scale = 0.5 / (total * (total - 1))
    losses = []
    for g in range(0, points, block):
        at = slice(g, g + block)
        live = lax.broadcasted_iota(jnp.int32, (1, block), 1) + g < live_count[0]
        live = live.astype(F32)
        own = [mine[m, :, at].astype(F32) for m in range(members)]
        aim = targets[:, at]
        near = jnp.zeros((channels, block), F32)
        far = jnp.zeros((channels, block), F32)
        slopes = []
        for m in range(members):
            value, grad = smooth(own[m] - aim)
            near = near + value
            slopes.append([grad, jnp.zeros((channels, block), F32)])
        for a in range(members):
            for b in range(a + 1, members):
                value, grad = smooth(own[a] - own[b])
                far = far + 2.0 * value
                slopes[a][1] = slopes[a][1] + grad
                slopes[b][1] = slopes[b][1] - grad
        for other in others:
            for k in range(members):
                theirs = other[k, :, at].astype(F32)
                for m in range(members):
                    value, grad = smooth(own[m] - theirs)
                    far = far + value
                    slopes[m][1] = slopes[m][1] + grad
        for m in range(members):
            grad = slopes[m][0] * (1.0 / total) - slopes[m][1] * (2.0 * scale)
            d_cast[m, :, at] = (grad * live).astype(BF16)
        column = jnp.sum(near * (1.0 / total) - far * scale, axis=0, keepdims=True) * live
        losses.append(column)
    loss[...] = losses[0] + losses[1] + losses[2] + losses[3]
    back = w_pred[...].astype(F32).T.astype(BF16)
    grad = jnp.zeros((channels, hidden.shape[1]), F32)
    for m in range(members):
        grad = grad + mm(d_cast[m], hidden[m], NT)
        for g in range(0, points, block):
            at = slice(g, g + block)
            d_hid = mm(back, d_cast[m, :, at])
            d_pre[m, :, at] = (d_hid * slope[m, :, at].astype(F32)).astype(BF16)
    g_pred[...] = grad.astype(BF16)
    pooled = [
        (mm(table[...], d_pre[m], NT) * (1.0 / 3.0)).astype(BF16) for m in range(members)
    ]
    pooled = jnp.concatenate(pooled, axis=0)
    g_hid[...] = mm(stored[...], pooled, TN).astype(BF16)
    d_updated[...] = mm(pooled, w_hid[...], NT).astype(BF16)
    g_out[...] = mm(attended[...], d_updated[...], TN).astype(BF16)
    d_attended[...] = mm(d_updated[...], w_out[...], NT).astype(BF16)


def back_body(
    own, proj, low, high, noise, w_noise, w_qkv, normed, normed_rim, proj_rim, nbr, degree,
    d_updated, d_attended,
    d_own, d_low, d_high, g_qkv, g_noise, d_proj, d_rim,
):
    members, nodes, width = own.shape
    rim = low.shape[1]
    noises = noise[...]
    gain = gains(noises, w_noise[...])
    mask = slot_mask(nbr, degree, nodes + 2 * rim)
    for m in range(members):
        here = slice(m * nodes, (m + 1) * nodes)
        lo = slice(2 * rim * m, 2 * rim * m + rim)
        hi = slice(2 * rim * m + rim, 2 * rim * (m + 1))
        for h in range(HEADS):
            at = [slice(k * width + h * HEAD, k * width + (h + 1) * HEAD) for k in range(3)]
            rim_at = [slice(a.start - width, a.stop - width) for a in at]
            query = proj[here, at[0]]
            key = extend(proj[here, at[1]], proj_rim[lo, rim_at[1]], proj_rim[hi, rim_at[1]])
            value = extend(proj[here, at[2]], proj_rim[lo, rim_at[2]], proj_rim[hi, rim_at[2]])
            out = d_attended[here, at[0]]
            sig = jax.nn.sigmoid(mm(key, query, NT) * HEAD**-0.5)
            weight = sig * mask
            d_value = mm(weight.astype(BF16), out).astype(BF16)
            d_weight = mm(value, out, NT)
            d_score = (d_weight * weight * (1.0 - sig) * HEAD**-0.5).astype(BF16)
            d_key = mm(d_score, query).astype(BF16)
            d_proj[here, at[0]] = mm(d_score, key, TN).astype(BF16)
            for k, d in ((1, d_key), (2, d_value)):
                d_rim[lo, rim_at[k]] = d[:rim]
                d_proj[here, at[k]] = d[rim : rim + nodes]
                d_rim[hi, rim_at[k]] = d[rim + nodes :]
    g_qkv[:, :width] = mm(normed[...], d_proj[:, :width], TN).astype(BF16)
    g_qkv[:, width:] = (
        mm(normed[...], d_proj[:, width:], TN) + mm(normed_rim[...], d_rim[...], TN)
    ).astype(BF16)
    d_normed = mm(d_proj[...], w_qkv[...], NT)
    d_normed_rim = mm(d_rim[...], w_qkv[:, width:], NT)
    d_noise = jnp.zeros(g_noise.shape, F32)
    noise_columns = jnp.concatenate([noises] * (8 // members), axis=0).T
    for m in range(members):
        here = slice(m * nodes, (m + 1) * nodes)
        rims = slice(2 * rim * m, 2 * rim * (m + 1))
        hat, inverse = normalise(own[m].astype(F32))
        d_gain = jnp.sum(d_normed[here] * hat, axis=0, keepdims=True)
        rows = norm_back(d_normed[here], gain[m : m + 1], hat, inverse)
        d_own[m] = (rows + d_updated[here].astype(F32)).T
        hat, inverse = normalise(jnp.concatenate([low[m], high[m]], axis=0).astype(F32))
        d_gain = d_gain + jnp.sum(d_normed_rim[rims] * hat, axis=0, keepdims=True)
        rows = norm_back(d_normed_rim[rims], gain[m : m + 1], hat, inverse)
        d_low[m] = rows[:rim].astype(BF16)
        d_high[m] = rows[rim:].astype(BF16)
        d_noise = d_noise + noise_columns[:, m : m + 1] * d_gain
    g_noise[...] = d_noise.astype(g_noise.dtype)


def join_body(d_own, rows, from_next, from_prev, d_latent):
    nodes = d_own.shape[2]
    rim = rows.shape[1]
    index = lax.broadcasted_iota(jnp.int32, (nodes, 2 * rim), 0)
    both = jnp.concatenate([rows[0:1, :], rows[1:2, :]], axis=1)
    table = (index == both).astype(F32).T.astype(BF16)
    for m in range(d_own.shape[0]):
        back = jnp.concatenate([from_next[m], from_prev[m]], axis=0)
        d_latent[m] = d_own[m] + mm(back, table, TN)


def on_device(
    latent, send_rows, neighbours, degree, dec_nodes, counts, targets, member_noise,
    w_qkv, w_out, w_noise, w_hid, w_pred,
):
    members, width, nodes = latent.shape
    rim = send_rows.shape[1]
    points = dec_nodes.shape[1]
    channels = targets.shape[0]
    rows = members * nodes
    rims = members * 2 * rim
    degree = degree[None, :]
    size = lax.axis_size("space")
    up = [(i, i + 1) for i in range(size - 1)]
    down = [(i + 1, i) for i in range(size - 1)]

    (sent,) = call(send_body, [((2, members, rim, width), BF16)], latent, send_rows)
    low = lax.ppermute(sent[0], "space", up)
    high = lax.ppermute(sent[1], "space", down)
    own, normed, proj = call(
        local_body,
        [((members, nodes, width), BF16), ((rows, width), BF16), ((rows, 3 * width), BF16)],
        latent, member_noise, w_noise, w_qkv,
        flops=2 * rows * width * 3 * width,
    )
    normed_rim, proj_rim, attended, stored, hidden, slope, forecast, table = call(
        forward_body,
        [
            ((rims, width), BF16), ((rims, 2 * width), BF16), ((rows, width), BF16),
            ((rows, width), BF16), ((members, width, points), BF16),
            ((members, width, points), BF16), ((members, channels, points), BF16),
            ((nodes, points), BF16),
        ],
        own, proj, low, high, member_noise, w_noise, w_qkv, w_out, w_hid, w_pred,
        neighbours, degree, dec_nodes,
        flops=3 * 10**9,
    )
    gathered = gather_members(forecast)
    live_count = lax.dynamic_slice_in_dim(counts, lax.axis_index("space"), 1)
    d_updated, d_attended, g_out, g_hid, g_pred, loss = call(
        crps_body,
        [
            ((rows, width), BF16), ((rows, width), BF16), ((width, width), BF16),
            ((width, width), BF16), ((channels, width), BF16), ((1, 256), F32),
        ],
        live_count, forecast, *gathered, targets, hidden, slope, table, stored, attended,
        w_out, w_hid, w_pred,
        smem=(0,),
        scratch=[
            pltpu.VMEM((members, width, points), BF16),
            pltpu.VMEM((members, channels, points), BF16),
        ],
        flops=6 * 10**9,
    )
    d_own, d_low, d_high, g_qkv, g_noise = call(
        back_body,
        [
            ((members, width, nodes), F32), ((members, rim, width), BF16),
            ((members, rim, width), BF16), ((width, 3 * width), BF16), ((32, width), F32),
        ],
        own, proj, low, high, member_noise, w_noise, w_qkv, normed, normed_rim, proj_rim,
        neighbours, degree, d_updated, d_attended,
        scratch=[pltpu.VMEM((rows, 3 * width), BF16), pltpu.VMEM((rims, 2 * width), BF16)],
        flops=6 * 10**9,
    )
    everywhere = ("space", "member")
    g_out, g_hid, g_pred = lax.psum((g_out, g_hid, g_pred), everywhere)
    g_qkv, g_noise, loss = lax.psum((g_qkv, g_noise, loss), everywhere)
    from_next = lax.ppermute(d_low, "space", down)
    from_prev = lax.ppermute(d_high, "space", up)
    (d_latent,) = call(
        join_body, [((members, width, nodes), F32)], d_own, send_rows, from_next, from_prev
    )
    mean = jnp.sum(loss) / (channels * jnp.sum(counts).astype(F32))
    return (
        mean, d_latent, g_qkv.astype(F32), g_out.astype(F32), g_noise, g_hid.astype(F32),
        g_pred.astype(F32),
    )


def gather_members(forecast):
    size = lax.axis_size("member")
    return [
        lax.ppermute(forecast, "member", [(i, (i + s) % size) for i in range(size)])
        for s in range(1, size)
    ]


def solution(mesh):
    in_specs = (
        P("member", None, "space"), P(None, "space"), P(None, "space"), P("space"),
        P(None, "space"), P(), P(None, "space"), P("member", None), P(), P(), P(), P(), P(),
    )
    out_specs = (P(), P("member", None, "space"), P(), P(), P(), P(), P())
    return jax.shard_map(
        on_device, mesh=mesh, in_specs=in_specs, out_specs=out_specs, check_vma=False
    )
```

profile of v0, /device:TPU:2, one launch (start us, length us, event | category | flops | bytes accessed | tf_op | source)
XLA Modules:
  0.0 391.9 jit_solution(8859468316669009838)
XLA Ops:
  9.3 3.5 collective-permute-start
  12.8 5.4 %collective-permute-start.1 = (bf16[2,16,768]{2,1,0:T(8,128)(2,1)S(1)}, bf16[2,16,768]{2,1,0:T(8,128)(2,1)S(1)}, u32[]{:S(2)}, u32[]{:S(2)}) collective-permute-start(bf16[2,16,768]{2,1,0:T(8,128)(2,1)S(1)} %get-tuple-element.55), channel_id=1, source_target_pairs={{4,0},{8,4},{12,8},{16,12},{20,16},{24,20},{28,24},{32,28},{36,32}... | collective-permute-start | bytes 147464 | tf_op jit(solution)/shard_map/ppermute | solution.py:302
  18.2 2.0 copy-done
  21.7 1.5 shard_map.180
  24.1 10.7 %shard_map.182 = (bf16[64,768]{1,0:T(8,128)(2,1)S(1)}, bf16[64,1536]{1,0:T(8,128)(2,1)S(1)}, bf16[256,768]{1,0:T(8,128)(2,1)S(1)}, bf16[256,768]{1,0:T(8,128)(2,...) custom-call(bf16[2,128,768]{2,1,0:T(8,128)(2,1)S(1)} %get-tuple-elem, ...), custom_call_target="tpu_custom_call" | custom-call | flops 3000000000 | bytes 15787264 | tf_op jit(solution)/shard_map/pallas_call | solution.py:29
  38.3 3.9 collective-permute-start.3
  42.2 2.9 collective-permute-start.4
  45.7 3.9 collective-permute-done.2.rest_0_
  49.6 1.8 collective-permute-done.3.rest_1_
  51.4 6.7 %collective-permute-done.4.rest_2_ = bf16[2,83,1024]{2,1,0:T(8,128)(2,1)S(1)} collective-permute-done((bf16[2,83,1024]{2,1,0:T(8,128)(2,1)S(1)}, bf16[2,83,1024]{2,1,0:T(8,128)(2,1)S(1)}, u32[]{:S(2)}, u32[]{:S(2)}) %collective-permute-start.4) | collective-permute-done | bytes 340000 | tf_op jit(solution)/shard_map/ppermute | solution.py:367
  58.1 1.0 copy-done.22
  59.1 1.0 copy-done.24
  61.1 10.6 %shard_map.183 = (bf16[256,768]{1,0:T(8,128)(2,1)S(1)}, bf16[256,768]{1,0:T(8,128)(2,1)S(1)}, bf16[768,768]{1,0:T(8,128)(2,1)}, bf16[768,768]{1,0:T(8,128)(2,1)}...) custom-call(s32[1]{0:T(128)} %dynamic_slice.3.live_count, bf16[2,83,1024]{2,1,0:T(8,128)(2,1)S(1)} %get-tuple-element.31.mine, ...), custom_call_target="tpu_custom_call" | custom-call | flops 6000000000 | bytes 14800900 | tf_op jit(solution)/shard_map/pallas_call | solution.py:29
  71.8 9.5 %shard_map.184 = (f32[2,768,128]{2,1,0:T(8,128)S(1)}, bf16[2,16,768]{2,1,0:T(8,128)(2,1)S(1)}, bf16[2,16,768]{2,1,0:T(8,128)(2,1)S(1)}, bf16[768,2304]{1,0:T(8,128)(2,1)}, f32[32,768]{1,0:T(8,128)}) custom-call(bf16[2,128,768]{2,1,0:T(8,128)(2,1)S(1)} %copy-done.13, bf16[256,2304]{1,0:T(8,128)(2,1)S(1)} %copy-done.11, ...), custom_call_target="tpu_custom_call" | custom-call | flops 6000000000 | bytes 11309824 | tf_op jit(solution)/shard_map/pallas_call | solution.py:29
  81.4 2.3 collective-permute-start.5
  83.7 3.5 collective-permute-start.6
  88.5 67.1 %psum.42 = f32[1,256]{1,0:T(1,128)S(1)} all-reduce(f32[1,256]{1,0:T(1,128)S(1)} %get-tuple-element.37), channel_id=1, replica_groups=mesh['space'=32,'member'=4] {'space','member'}, use_global_device_ids=true, to_apply=%region_0.0 | all-reduce | flops 256 | bytes 2048 | tf_op jit(solution)/shard_map/psum | solution.py:351
  156.9 1.3 shard_map.185
  158.2 80.9 %all-reduce.6.cloned.1.call-done = (bf16[768,2304]{1,0:T(8,128)(2,1)}, bf16[768,768]{1,0:T(8,128)(2,1)}, bf16[768,768]{1,0:T(8,128)(2,1)}, bf16[83,768]{1,0:T(8,128)(2,1)}) async-done(((bf16[768,2304]{1,0:T(8,128)(2,1)}, bf16[768,768]{1,0:T(8,128)(2,1)}, bf16[768,768]{1,0:T(8,128)(2,1)}, bf16[83,768]{1,0:T(8,128)(2,1)}), (bf16[768,2304]{1,0:T(8,128)(2,1)}, bf16[768,768]{1,0:T(8,128)(2,1)}, ...) | async-done | bytes 6025744 | tf_op jit(solution)/shard_map/psum | solution.py:351
  239.1 5.6 %convert_element_type.16 = f32[768,2304]{1,0:T(8,128)} convert(bf16[768,2304]{1,0:T(8,128)(2,1)} %get-tuple-element.51) | non-fusion elementwise | flops 1769472 | bytes 10616832 | tf_op jit(solution)/shard_map/convert_element_type | solution.py:359
  244.7 1.6 convert_element_type.17
  246.4 1.6 convert_element_type.18
  248.7 133.7 %all-reduce.4.cloned.1.call-done = f32[32,768]{1,0:T(8,128)} async-done(((f32[32,768]{1,0:T(8,128)}), f32[32,768]{1,0:T(8,128)}) %all-reduce.4.cloned.1.call-update) | async-done | bytes 98320 | tf_op jit(solution)/shard_map/psum | solution.py:351
  382.4 1.5 copy.25
  (82 shorter events, 11.6 us)
Async XLA Ops:
  7.2 231.9 %all-reduce.6.cloned.1.call-start = ((), (), s32[]{:S(2)}) async-start(), calls=%async_computation.1 | async-start | bytes 12066816 | tf_op jit(solution)/shard_map/psum | solution.py:351
  8.9 15.1 %copy-start.3 = (f32[32,768]{1,0:T(8,128)S(1)}, f32[32,768]{1,0:T(8,128)}, u32[]{:S(2)}) copy-start(f32[32,768]{1,0:T(8,128)} %w_noise.5) | copy-start | bytes 294916
  8.9 15.1 %copy-start.7 = (f32[2,32]{1,0:T(2,128)S(1)}, f32[2,32]{1,0:T(2,128)}, u32[]{:S(2)}) copy-start(f32[2,32]{1,0:T(2,128)} %noise.5) | copy-start | bytes 772
  8.9 15.1 %copy-start.17 = (bf16[83,768]{1,0:T(8,128)(2,1)S(1)}, bf16[83,768]{1,0:T(8,128)(2,1)}, u32[]{:S(2)}) copy-start(bf16[83,768]{1,0:T(8,128)(2,1)} %rest_11_.1) | copy-start | bytes 382468
  8.9 15.1 %copy-start.18 = (s32[3,1024]{1,0:T(4,128)S(1)}, s32[3,1024]{1,0:T(4,128)}, u32[]{:S(2)}) copy-start(s32[3,1024]{1,0:T(4,128)} %dec_nodes.1) | copy-start | bytes 36868
  8.9 15.1 %copy-start.19 = (s32[8,128]{1,0:T(8,128)S(1)}, s32[8,128]{1,0:T(8,128)}, u32[]{:S(2)}) copy-start(s32[8,128]{1,0:T(8,128)} %nbr.3) | copy-start | bytes 12292
  8.9 15.1 %copy-start.20 = (s32[128]{0:T(128)S(1)}, s32[128]{0:T(128)}, u32[]{:S(2)}) copy-start(s32[128]{0:T(128)} %param.16) | copy-start | bytes 1540
  9.3 14.7 %collective-permute-start = (bf16[2,16,768]{2,1,0:T(8,128)(2,1)S(1)}, bf16[2,16,768]{2,1,0:T(8,128)(2,1)S(1)}, u32[]{:S(2)}, u32[]{:S(2)}) collective-permute-start(bf16[2,16,768]{2,1,0:T(8,128)(2,1)S(1)} %get-tuple-element.56), channel_id=1, source_target_pairs={{0,4},{4,8},{8,12},{12,16},{16,20},{20,24},{24,28},{28,32},{32,36}... | collective-permute-start | bytes 147464 | tf_op jit(solution)/shard_map/ppermute | solution.py:301
  12.8 11.2 %collective-permute-start.1 = (bf16[2,16,768]{2,1,0:T(8,128)(2,1)S(1)}, bf16[2,16,768]{2,1,0:T(8,128)(2,1)S(1)}, u32[]{:S(2)}, u32[]{:S(2)}) collective-permute-start(bf16[2,16,768]{2,1,0:T(8,128)(2,1)S(1)} %get-tuple-element.55), channel_id=1, source_target_pairs={{4,0},{8,4},{12,8},{16,12},{20,16},{24,20},{28,24},{32,28},{36,32}... | collective-permute-start | bytes 147464 | tf_op jit(solution)/shard_map/ppermute | solution.py:302
  24.0 10.8 %copy-start.10 = (bf16[256,2304]{1,0:T(8,128)(2,1)}, bf16[256,2304]{1,0:T(8,128)(2,1)S(1)}, u32[]{:S(2)}) copy-start(bf16[256,2304]{1,0:T(8,128)(2,1)S(1)} %get-tuple-element.30.proj) | copy-start | bytes 3538948
  24.0 10.8 %copy-start.12 = (bf16[2,128,768]{2,1,0:T(8,128)(2,1)}, bf16[2,128,768]{2,1,0:T(8,128)(2,1)S(1)}, u32[]{:S(2)}) copy-start(bf16[2,128,768]{2,1,0:T(8,128)(2,1)S(1)} %get-tuple-element.29.own) | copy-start | bytes 1179652
  24.1 21.1 %copy-start.34 = (s32[32]{0:T(128)S(1)}, s32[32]{0:T(128)}, u32[]{:S(2)}) copy-start(s32[32]{0:T(128)} %param.18) | copy-start | bytes 388
  24.1 34.0 %copy-start.16 = (f32[83,1024]{1,0:T(8,128)S(1)}, f32[83,1024]{1,0:T(8,128)}, u32[]{:S(2)}) copy-start(f32[83,1024]{1,0:T(8,128)} %rest_3_.1) | copy-start | bytes 1019908
  38.3 11.3 %collective-permute-start.2 = (bf16[2,83,1024]{2,1,0:T(8,128)(2,1)S(1)}, bf16[2,83,1024]{2,1,0:T(8,128)(2,1)S(1)}, u32[]{:S(2)}, u32[]{:S(2)}) collective-permute-start(bf16[2,83,1024]{2,1,0:T(8,128)(2,1)S(1)} %get-tuple-element.31.mine), channel_id=1, source_target_pairs={{0,1},{1,2},{2,3},{3,0},{4,5},{5,6},{6,7},{7,4},{8,9},{9,10},{10,1... | collective-permute-start | bytes 1019912 | tf_op jit(solution)/shard_map/ppermute | solution.py:367
  38.3 13.1 %collective-permute-start.3 = (bf16[2,83,1024]{2,1,0:T(8,128)(2,1)S(1)}, bf16[2,83,1024]{2,1,0:T(8,128)(2,1)S(1)}, u32[]{:S(2)}, u32[]{:S(2)}) collective-permute-start(bf16[2,83,1024]{2,1,0:T(8,128)(2,1)S(1)} %get-tuple-element.31.mine), channel_id=1, source_target_pairs={{0,2},{1,3},{2,0},{3,1},{4,6},{5,7},{6,4},{7,5},{8,10},{9,11},{10,... | collective-permute-start | bytes 1019912 | tf_op jit(solution)/shard_map/ppermute | solution.py:367
  42.2 15.9 %collective-permute-start.4 = (bf16[2,83,1024]{2,1,0:T(8,128)(2,1)S(1)}, bf16[2,83,1024]{2,1,0:T(8,128)(2,1)S(1)}, u32[]{:S(2)}, u32[]{:S(2)}) collective-permute-start(bf16[2,83,1024]{2,1,0:T(8,128)(2,1)S(1)} %get-tuple-element.31.mine), channel_id=1, source_target_pairs={{0,3},{1,0},{2,1},{3,2},{4,7},{5,4},{6,5},{7,6},{8,11},{9,8},{10,9... | collective-permute-start | bytes 1019912 | tf_op jit(solution)/shard_map/ppermute | solution.py:367
  61.1 10.6 %copy-start.13 = (bf16[2,128,768]{2,1,0:T(8,128)(2,1)S(1)}, bf16[2,128,768]{2,1,0:T(8,128)(2,1)}, u32[]{:S(2)}) copy-start(bf16[2,128,768]{2,1,0:T(8,128)(2,1)} %copy-done.12) | copy-start | bytes 1179652
  61.1 10.6 %copy-start.15 = (bf16[256,768]{1,0:T(8,128)(2,1)S(1)}, bf16[256,768]{1,0:T(8,128)(2,1)}, u32[]{:S(2)}) copy-start(bf16[256,768]{1,0:T(8,128)(2,1)} %copy-done.14) | copy-start | bytes 1179652
  61.1 10.7 %copy-start.28 = (bf16[64,1536]{1,0:T(8,128)(2,1)S(1)}, bf16[64,1536]{1,0:T(8,128)(2,1)}, u32[]{:S(2)}) copy-start(bf16[64,1536]{1,0:T(8,128)(2,1)} %copy-done.27) | copy-start | bytes 589828
  61.1 10.7 %copy-start.30 = (bf16[64,768]{1,0:T(8,128)(2,1)S(1)}, bf16[64,768]{1,0:T(8,128)(2,1)}, u32[]{:S(2)}) copy-start(bf16[64,768]{1,0:T(8,128)(2,1)} %copy-done.29) | copy-start | bytes 294916
  81.3 75.6 %copy-start.5 = (s32[2,16]{1,0:T(2,128)S(1)}, s32[2,16]{1,0:T(2,128)}, u32[]{:S(2)}) copy-start(s32[2,16]{1,0:T(2,128)} %rows.3) | copy-start | bytes 388
  81.3 301.1 %all-reduce.4.cloned.1.call-start = ((), (), s32[]{:S(2)}) async-start(), calls=%async_computation | async-start | bytes 196608 | tf_op jit(solution)/shard_map/psum | solution.py:351
  81.4 75.5 %collective-permute-start.5 = (bf16[2,16,768]{2,1,0:T(8,128)(2,1)S(1)}, bf16[2,16,768]{2,1,0:T(8,128)(2,1)S(1)}, u32[]{:S(2)}, u32[]{:S(2)}) collective-permute-start(bf16[2,16,768]{2,1,0:T(8,128)(2,1)S(1)} %get-tuple-element.44), channel_id=1, source_target_pairs={{4,0},{8,4},{12,8},{16,12},{20,16},{24,20},{28,24},{32,28},{36,32}... | collective-permute-start | bytes 147464 | tf_op jit(solution)/shard_map/ppermute | solution.py:352
  83.7 73.2 %collective-permute-start.6 = (bf16[2,16,768]{2,1,0:T(8,128)(2,1)S(1)}, bf16[2,16,768]{2,1,0:T(8,128)(2,1)S(1)}, u32[]{:S(2)}, u32[]{:S(2)}) collective-permute-start(bf16[2,16,768]{2,1,0:T(8,128)(2,1)S(1)} %get-tuple-element.45), channel_id=1, source_target_pairs={{0,4},{4,8},{8,12},{12,16},{16,20},{20,24},{24,28},{28,32},{32,36}... | collective-permute-start | bytes 147464 | tf_op jit(solution)/shard_map/ppermute | solution.py:353
  (20 other events, 36.7 us)
Sparse Core Ops, SparseCore 0:
  81.4 157.6 all-reduce.5
  245.2 137.2 all-reduce.3
where the time goes:
time: 393 us; the launch traced here: 392 us
  waiting for transfers between devices  227 us (58%)
  blocking collectives  67.1 us (17%)
  Pallas kernels  33.9 us (9%)
  starting transfers between devices  21.6 us (5%)
  between operations  16.8 us (4%)
  local copies, waits for them, and re-layouts  14.8 us (4%)
  other arithmetic  10.7 us (3%)
    psum x2, waiting for transfers between devices, on_device(): g_qkv, g_noise, loss = lax.psum((g_qkv, g_noise, loss), everywhere)  215 us
    psum x1, blocking collectives, on_device(): g_qkv, g_noise, loss = lax.psum((g_qkv, g_noise, loss), everywhere)  67.1 us
    pallas_call x6, Pallas kernels, call(): pl.pallas_call(body, out_shape=out_shape, in_specs=[SMEM if i in smem els...  33.9 us
    unnamed x71, local copies, waits for them, and re-layouts  14.1 us
    ppermute x3, waiting for transfers between devices, gather_members(): lax.ppermute(forecast, 'member', [(i, (i + s) % size) for i in range(size)])  12.4 us
  transfers between devices with their start and end apart: 9, of which 5 were waited for; matrix products, arithmetic and copies ran while one was open for 3% of the time, Pallas kernels for 1%

commit v1 on v0

--- a/solution.py
+++ b/solution.py
@@ -7,6 +7,11 @@
 
 HEADS = 6
 HEAD = 128
+TILE = 128
+GROUPS = 16
+SLOTS_A = 5
+SLOTS_B = 7
+CHUNKS = 4 * GROUPS
 EPS = 1e-5
 F32 = jnp.float32
 BF16 = jnp.bfloat16
@@ -154,10 +159,10 @@
 
 
 def crps_body(
-    live_count, mine, *rest
+    core, live_count, mine, *rest
 ):
     (*others, targets, hidden, slope, table, stored, attended, w_out, w_hid, w_pred,
-     d_updated, d_attended, g_out, g_hid, g_pred, loss, d_pre, d_cast) = rest
+     d_updated, d_attended, keep, send, loss, d_pre, d_cast, halves) = rest
     members, channels, points = mine.shape
     total = members * (1 + len(others))
     block = 256
@@ -195,7 +200,10 @@
             d_cast[m, :, at] = (grad * live).astype(BF16)
         column = jnp.sum(near * (1.0 / total) - far * scale, axis=0, keepdims=True) * live
         losses.append(column)
-    loss[...] = losses[0] + losses[1] + losses[2] + losses[3]
+    for i in range(16):
+        at = i % 2
+        piece = losses[i // 2 % 4][:, TILE * at : TILE * (at + 1)]
+        loss[i : i + 1] = piece.astype(BF16) if i < 8 else jnp.zeros((1, TILE), BF16)
     back = w_pred[...].astype(F32).T.astype(BF16)
     grad = jnp.zeros((channels, hidden.shape[1]), F32)
     for m in range(members):
@@ -204,27 +212,53 @@
             at = slice(g, g + block)
             d_hid = mm(back, d_cast[m, :, at])
             d_pre[m, :, at] = (d_hid * slope[m, :, at].astype(F32)).astype(BF16)
-    g_pred[...] = grad.astype(BF16)
+    g_pred = jnp.zeros((96 - channels, grad.shape[1]), F32)
+    g_pred = jnp.concatenate([grad, g_pred], axis=0).astype(BF16)
     pooled = [
         (mm(table[...], d_pre[m], NT) * (1.0 / 3.0)).astype(BF16) for m in range(members)
     ]
     pooled = jnp.concatenate(pooled, axis=0)
-    g_hid[...] = mm(stored[...], pooled, TN).astype(BF16)
+    g_hid = mm(stored[...], pooled, TN).astype(BF16)
     d_updated[...] = mm(pooled, w_hid[...], NT).astype(BF16)
-    g_out[...] = mm(attended[...], d_updated[...], TN).astype(BF16)
+    g_out = mm(attended[...], d_updated[...], TN).astype(BF16)
     d_attended[...] = mm(d_updated[...], w_out[...], NT).astype(BF16)
-
-
-def back_body(
-    own, proj, low, high, noise, w_noise, w_qkv, normed, normed_rim, proj_rim, nbr, degree,
-    d_updated, d_attended,
-    d_own, d_low, d_high, g_qkv, g_noise, d_proj, d_rim,
-):
-    members, nodes, width = own.shape
-    rim = low.shape[1]
-    noises = noise[...]
-    gain = gains(noises, w_noise[...])
-    mask = slot_mask(nbr, degree, nodes + 2 * rim)
+    half = g_hid.shape[1] // 2
+    for c in range(2):
+        for k in range(GROUPS):
+            for slot in range(SLOTS_A * 4):
+                chunk, lane = 4 * k + slot // SLOTS_A, TILE * (slot % SLOTS_A)
+                grad, row, column = tile_of_first(k, slot, (g_hid, g_out, g_pred))
+                if grad is None:
+                    piece = jnp.zeros((16, TILE), BF16)
+                else:
+                    column = c * half + TILE * column
+                    piece = grad[16 * row : 16 * row + 16, column : column + TILE]
+                halves[c, chunk, :, lane : lane + TILE] = piece
+    keep[...] = halves[core[0]]
+    send[...] = halves[1 - core[0]]
+
+
+def tile_of_first(k, slot, grads):
+    if slot < 18:
+        part = slot % 9
+        return grads[slot // 9], 3 * k + part // 3, part % 3
+    tile = k + GROUPS * (slot - 18)
+    if tile < 18:
+        return grads[2], tile // 3, tile % 3
+    return None, 0, 0
+
+
+def attend_back_body(
+    core, proj, proj_rim, nbr, degree, d_attended,
+    d_proj, d_rim, send, mask,
+):
+    nodes = nbr.shape[1]
+    members = proj.shape[0] // nodes
+    width = HEADS * HEAD
+    rim = proj_rim.shape[0] // (2 * members)
+    per_half = HEADS // 2
+    part = width // 2
+    mask[...] = slot_mask(nbr, degree, nodes + 2 * rim)
     for m in range(members):
         here = slice(m * nodes, (m + 1) * nodes)
         lo = slice(2 * rim * m, 2 * rim * m + rim)
@@ -237,22 +271,44 @@
             value = extend(proj[here, at[2]], proj_rim[lo, rim_at[2]], proj_rim[hi, rim_at[2]])
             out = d_attended[here, at[0]]
             sig = jax.nn.sigmoid(mm(key, query, NT) * HEAD**-0.5)
-            weight = sig * mask
+            weight = sig * mask[...]
             d_value = mm(weight.astype(BF16), out).astype(BF16)
             d_weight = mm(value, out, NT)
             d_score = (d_weight * weight * (1.0 - sig) * HEAD**-0.5).astype(BF16)
             d_key = mm(d_score, query).astype(BF16)
-            d_proj[here, at[0]] = mm(d_score, key, TN).astype(BF16)
+            c, j = h // per_half, h % per_half
+            spot = [slice(k * part + j * HEAD, k * part + (j + 1) * HEAD) for k in range(3)]
+            d_proj[c, here, spot[0]] = mm(d_score, key, TN).astype(BF16)
             for k, d in ((1, d_key), (2, d_value)):
-                d_rim[lo, rim_at[k]] = d[:rim]
-                d_proj[here, at[k]] = d[rim : rim + nodes]
-                d_rim[hi, rim_at[k]] = d[rim + nodes :]
-    g_qkv[:, :width] = mm(normed[...], d_proj[:, :width], TN).astype(BF16)
-    g_qkv[:, width:] = (
-        mm(normed[...], d_proj[:, width:], TN) + mm(normed_rim[...], d_rim[...], TN)
-    ).astype(BF16)
-    d_normed = mm(d_proj[...], w_qkv[...], NT)
-    d_normed_rim = mm(d_rim[...], w_qkv[:, width:], NT)
+                d_rim[c, lo, spot[k - 1]] = d[:rim]
+                d_proj[c, here, spot[k]] = d[rim : rim + nodes]
+                d_rim[c, hi, spot[k - 1]] = d[rim + nodes :]
+    rows = members * nodes
+    send[:rows] = d_proj[1 - core[0]]
+    send[rows:, : 2 * part] = d_rim[1 - core[0]]
+    send[rows:, 2 * part :] = jnp.zeros((2 * rim * members, part), BF16)
+
+
+def norm_back_body(
+    own, low, high, noise, w_noise, w_qkv, d_proj, d_rim, d_updated,
+    d_own, d_low, d_high, g_noise,
+):
+    members, nodes, width = own.shape
+    rim = low.shape[1]
+    part = width // 2
+    noises = noise[...]
+    gain = gains(noises, w_noise[...])
+    d_normed = jnp.zeros((members * nodes, width), F32)
+    d_normed_rim = jnp.zeros((members * 2 * rim, width), F32)
+    for c in range(2):
+        for k in range(3):
+            column = k * width + c * part
+            weight = w_qkv[:, column : column + part]
+            d_normed = d_normed + mm(d_proj[c, :, k * part : (k + 1) * part], weight, NT)
+            if k:
+                d_normed_rim = d_normed_rim + mm(
+                    d_rim[c, :, (k - 1) * part : k * part], weight, NT
+                )
     d_noise = jnp.zeros(g_noise.shape, F32)
     noise_columns = jnp.concatenate([noises] * (8 // members), axis=0).T
     for m in range(members):
@@ -268,7 +324,110 @@
         d_low[m] = rows[:rim].astype(BF16)
         d_high[m] = rows[rim:].astype(BF16)
         d_noise = d_noise + noise_columns[:, m : m + 1] * d_gain
-    g_noise[...] = d_noise.astype(g_noise.dtype)
+    g_noise[...] = d_noise.astype(BF16)
+
+
+def pack_body(
+    core, normed, normed_rim, normed_theirs, d_proj, d_rim, d_theirs, keep, came, g_noise, loss,
+    packed, g_half,
+):
+    rows = normed.shape[0]
+    wide = 2 * d_proj.shape[2] // 3
+    width = normed.shape[1]
+    mine = d_proj[core[0]]
+    rim = d_rim[core[0]]
+    for r in range(0, width, 256):
+        at = slice(r, r + 256)
+        total = mm(normed[:, at], mine, TN) + mm(normed_theirs[:rows, at], d_theirs[:rows], TN)
+        g_half[at, : wide // 2] = total[:, : wide // 2].astype(BF16)
+        edge = mm(normed_rim[:, at], rim, TN)
+        edge = edge + mm(normed_theirs[rows:, at], d_theirs[rows:, :wide], TN)
+        g_half[at, wide // 2 :] = (total[:, wide // 2 :] + edge).astype(BF16)
+    first = TILE * SLOTS_A
+    packed[:, :, :first] = (keep[...].astype(F32) + came[...].astype(F32)).astype(BF16)
+    for k in range(GROUPS):
+        for slot in range(SLOTS_B * 4):
+            chunk, lane = 4 * k + slot // SLOTS_B, first + TILE * (slot % SLOTS_B)
+            if slot < 27:
+                row, column = 48 * k + 16 * (slot // 9), TILE * (slot % 9)
+                piece = g_half[row : row + 16, column : column + TILE]
+            elif k < 12:
+                row, column = 16 * (k // 6), TILE * (k % 6)
+                piece = g_noise[row : row + 16, column : column + TILE]
+            elif k == 12:
+                piece = loss[...]
+            else:
+                piece = jnp.zeros((16, TILE), BF16)
+            packed[chunk, :, lane : lane + TILE] = piece
+
+
+def sum_body(came, spread):
+    chips, chunks = came.shape[0], came.shape[1]
+    for j in range(chunks):
+        total = came[0, j].astype(F32)
+        for i in range(1, chips):
+            total = total + came[i, j].astype(F32)
+        total = total.astype(BF16)
+        for i in range(chips):
+            spread[i, j] = total
+
+
+def unpack_body(
+    core, counts, own, other, g_qkv, g_out, g_noise, g_hid, g_pred, mean, pred_rows
+):
+    k = pl.program_id(0)
+    first_core = core[0] == 0
+    width = g_hid.shape[1]
+    half = width // 2
+    for c in range(2):
+        def tile(chunk, lane):
+            at = (chunk, slice(None), slice(lane, lane + TILE))
+            mine, theirs = own[at].astype(F32), other[at].astype(F32)
+            return jnp.where(first_core == (c == 0), mine, theirs)
+
+        for slot in range(18):
+            target = (g_hid, g_out)[slot // 9]
+            row, column = 16 * (slot % 9 // 3), c * half + TILE * (slot % 3)
+            target[row : row + 16, column : column + TILE] = tile(
+                slot // SLOTS_A, TILE * (slot % SLOTS_A)
+            )
+        for slot in range(27):
+            row, column = 16 * (slot // 9), slot % 9
+            column = width * (column // 3) + c * half + TILE * (column % 3)
+            g_qkv[row : row + 16, column : column + TILE] = tile(
+                slot // SLOTS_B, TILE * (SLOTS_A + slot % SLOTS_B)
+            )
+        for slot in (18, 19):
+            index = k + GROUPS * (slot - 18)
+
+            @pl.when(index < 18)
+            def _(slot=slot, index=index, c=c, tile=tile):
+                row = pl.multiple_of(16 * (index // 3), 16)
+                column = pl.multiple_of(c * half + TILE * (index % 3), TILE)
+                pred_rows[pl.ds(row, 16), pl.ds(column, TILE)] = tile(
+                    slot // SLOTS_A, TILE * (slot % SLOTS_A)
+                )
+
+    spare = (3, slice(None), slice(TILE * (SLOTS_A + 6), TILE * (SLOTS_A + 7)))
+
+    @pl.when(k < 12)
+    def _():
+        row = pl.multiple_of(16 * (k // 6), 16)
+        column = pl.multiple_of(TILE * (k % 6), TILE)
+        g_noise[pl.ds(row, 16), pl.ds(column, TILE)] = own[spare].astype(F32) + other[
+            spare
+        ].astype(F32)
+
+    @pl.when(k == 12)
+    def _():
+        channels = g_pred.shape[0]
+        total = jnp.sum(own[spare].astype(F32) + other[spare].astype(F32), keepdims=True)
+        live = jnp.sum(counts[...].astype(F32), keepdims=True)
+        mean[...] = total / (channels * live)
+
+    @pl.when(k == GROUPS - 1)
+    def _():
+        g_pred[...] = pred_rows[: g_pred.shape[0]]
 
 
 def join_body(d_own, rows, from_next, from_prev, d_latent):
@@ -319,62 +478,117 @@
         flops=3 * 10**9,
     )
     gathered = gather_members(forecast)
+    packed_shape = (CHUNKS, 16, TILE * (SLOTS_A + SLOTS_B))
+    first_shape = (CHUNKS, 16, TILE * SLOTS_A)
+    core = lax.axis_index("core").astype(jnp.int32)[None]
+    swap = [(0, 1), (1, 0)]
+    normed_theirs = lax.ppermute(jnp.concatenate([normed, normed_rim], axis=0), "core", swap)
     live_count = lax.dynamic_slice_in_dim(counts, lax.axis_index("space"), 1)
-    d_updated, d_attended, g_out, g_hid, g_pred, loss = call(
+    d_updated, d_attended, keep, send, loss = call(
         crps_body,
         [
-            ((rows, width), BF16), ((rows, width), BF16), ((width, width), BF16),
-            ((width, width), BF16), ((channels, width), BF16), ((1, 256), F32),
-        ],
-        live_count, forecast, *gathered, targets, hidden, slope, table, stored, attended,
+            ((rows, width), BF16), ((rows, width), BF16), (first_shape, BF16),
+            (first_shape, BF16), ((16, TILE), BF16),
+        ],
+        core, live_count, forecast, *gathered, targets, hidden, slope, table, stored, attended,
         w_out, w_hid, w_pred,
-        smem=(0,),
+        smem=(0, 1),
         scratch=[
             pltpu.VMEM((members, width, points), BF16),
             pltpu.VMEM((members, channels, points), BF16),
+            pltpu.VMEM((2,) + first_shape, BF16),
         ],
         flops=6 * 10**9,
     )
-    d_own, d_low, d_high, g_qkv, g_noise = call(
-        back_body,
+    came = lax.ppermute(send, "core", swap)
+    d_proj, d_rim, d_send = call(
+        attend_back_body,
+        [
+            ((2, rows, 3 * width // 2), BF16), ((2, rims, width), BF16),
+            ((rows + rims, 3 * width // 2), BF16),
+        ],
+        core, proj, proj_rim, neighbours, degree, d_attended,
+        smem=(0,),
+        scratch=[pltpu.VMEM((nodes + 2 * rim, nodes), F32)],
+        flops=2 * 10**9,
+    )
+    d_theirs = lax.ppermute(d_send, "core", swap)
+    d_own, d_low, d_high, g_noise = call(
+        norm_back_body,
         [
             ((members, width, nodes), F32), ((members, rim, width), BF16),
-            ((members, rim, width), BF16), ((width, 3 * width), BF16), ((32, width), F32),
-        ],
-        own, proj, low, high, member_noise, w_noise, w_qkv, normed, normed_rim, proj_rim,
-        neighbours, degree, d_updated, d_attended,
-        scratch=[pltpu.VMEM((rows, 3 * width), BF16), pltpu.VMEM((rims, 2 * width), BF16)],
-        flops=6 * 10**9,
-    )
-    everywhere = ("space", "member")
-    g_out, g_hid, g_pred = lax.psum((g_out, g_hid, g_pred), everywhere)
-    g_qkv, g_noise, loss = lax.psum((g_qkv, g_noise, loss), everywhere)
+            ((members, rim, width), BF16), ((32, width), BF16),
+        ],
+        own, low, high, member_noise, w_noise, w_qkv, d_proj, d_rim, d_updated,
+        flops=2 * 10**9,
+    )
+    (packed,) = call(
+        pack_body,
+        [(packed_shape, BF16)],
+        core, normed, normed_rim, normed_theirs, d_proj, d_rim, d_theirs, keep, came, g_noise,
+        loss,
+        smem=(0,),
+        scratch=[pltpu.VMEM((width, 3 * width // 2), BF16)],
+        flops=2 * 10**9,
+    )
+    chips = ("space", "zhi")
+    count = lax.axis_size(chips)
+    parts = lax.all_to_all(packed, chips, 0, 0, tiled=True)
+    (spread,) = call(
+        sum_body,
+        [((count, CHUNKS // count) + packed_shape[1:], BF16)],
+        parts.reshape((count, CHUNKS // count) + packed_shape[1:]),
+    )
+    half = lax.all_to_all(spread.reshape(packed_shape), chips, 0, 0, tiled=True)
+    other = lax.ppermute(half, "core", swap)
     from_next = lax.ppermute(d_low, "space", down)
     from_prev = lax.ppermute(d_high, "space", up)
     (d_latent,) = call(
         join_body, [((members, width, nodes), F32)], d_own, send_rows, from_next, from_prev
     )
-    mean = jnp.sum(loss) / (channels * jnp.sum(counts).astype(F32))
-    return (
-        mean, d_latent, g_qkv.astype(F32), g_out.astype(F32), g_noise, g_hid.astype(F32),
-        g_pred.astype(F32),
-    )
+    block = pl.BlockSpec((4,) + packed_shape[1:], lambda k: (k, 0, 0))
+    whole = lambda shape: pl.BlockSpec(shape, lambda k: (0, 0))
+    g_qkv, g_out, g_noise, g_hid, g_pred, mean = pl.pallas_call(
+        unpack_body,
+        grid=(GROUPS,),
+        out_shape=[
+            jax.ShapeDtypeStruct(shape, F32)
+            for shape in (
+                (width, 3 * width), (width, width), (32, width), (width, width),
+                (channels, width), (1, 1),
+            )
+        ],
+        in_specs=[SMEM, whole((1, counts.shape[0])), block, block],
+        out_specs=[
+            pl.BlockSpec((48, 3 * width), lambda k: (k, 0)),
+            pl.BlockSpec((48, width), lambda k: (k, 0)),
+            whole((32, width)),
+            pl.BlockSpec((48, width), lambda k: (k, 0)),
+            whole((channels, width)),
+            whole((1, 1)),
+        ],
+        scratch_shapes=[pltpu.VMEM((96, width), F32)],
+        compiler_params=PARAMS,
+    )(core, counts[None, :], half, other)
+    return mean[0, 0], d_latent, g_qkv, g_out, g_noise, g_hid, g_pred
 
 
 def gather_members(forecast):
-    size = lax.axis_size("member")
+    axes = ("zhi", "core")
     return [
-        lax.ppermute(forecast, "member", [(i, (i + s) % size) for i in range(size)])
-        for s in range(1, size)
+        lax.ppermute(forecast, axes, [(i, i ^ step) for i in range(4)]) for step in (1, 2, 3)
     ]
 
 
 def solution(mesh):
+    space = mesh.shape["space"]
+    mesh = jax.sharding.Mesh(mesh.devices.reshape(space, 2, 2), ("space", "zhi", "core"))
+    member = ("zhi", "core")
     in_specs = (
-        P("member", None, "space"), P(None, "space"), P(None, "space"), P("space"),
-        P(None, "space"), P(), P(None, "space"), P("member", None), P(), P(), P(), P(), P(),
-    )
-    out_specs = (P(), P("member", None, "space"), P(), P(), P(), P(), P())
+        P(member, None, "space"), P(None, "space"), P(None, "space"), P("space"),
+        P(None, "space"), P(), P(None, "space"), P(member, None), P(), P(), P(), P(), P(),
+    )
+    out_specs = (P(), P(member, None, "space"), P(), P(), P(), P(), P())
     return jax.shard_map(
         on_device, mesh=mesh, in_specs=in_specs, out_specs=out_specs, check_vma=False
     )

time: 393 us -> 207 us (0.53)
  waiting for transfers between devices: 227 us -> 25 us
  blocking collectives: 67.1 us -> 96.1 us
  Pallas kernels: 33.9 us -> 51.1 us
  between operations: 16.8 us -> 1.04 us
  other arithmetic: 10.7 us -> 0.03 us
    psum x2 -> x0, waiting for transfers between devices: 215 us -> none  [on_device(): g_qkv, g_noise, loss = lax.psum((g_qkv, g_noise, loss), everywhere)]
    all_to_all x0 -> x2, blocking collectives: none -> 96.1 us  [the longest x1 50.6 us: on_device(): parts = lax.all_to_all(packed, chips, 0, 0, tiled=True)]
    psum x1 -> x0, blocking collectives: 67.1 us -> none  [on_device(): g_qkv, g_noise, loss = lax.psum((g_qkv, g_noise, loss), everywhere)]
    pallas_call x0 -> x1, Pallas kernels: none -> 12.1 us  [on_device(): pl.pallas_call(unpack_body, grid=(GROUPS,), out_shape=[jax.ShapeDtypeStru...]
    convert_element_type x4 -> x0, other arithmetic: 9.45 us -> none  [the longest x1 5.57 us: on_device(): g_qkv.astype(F32)]
    ppermute x1, waiting for transfers between devices: 0.01 us -> 6.91 us  [on_device(): from_prev = lax.ppermute(d_high, 'space', up)]
    pallas_call x6 -> x9, Pallas kernels: 33.9 us -> 39 us  [call(): pl.pallas_call(body, out_shape=out_shape, in_specs=[SMEM if i in smem els...]
    ppermute x3 -> x7, waiting for transfers between devices: 12.4 us -> 16 us  [the longest x3 16 us: gather_members(): lax.ppermute(forecast, axes, [(i, i ^ step) for i in range(4)])]
  transfers between devices with their start and end apart: 9 -> 11, of which waited for: 5 -> 5; matrix products, arithmetic and copies ran while one was open for 3% -> 0% of each run, Pallas kernels for 1% -> 5%
where the time goes in v1:
time: 207 us; the launch traced here: 206 us
  blocking collectives  96.1 us (46%)
  Pallas kernels  51.1 us (25%)
  waiting for transfers between devices  25 us (12%)
  starting transfers between devices  18.6 us (9%)
  local copies, waits for them, and re-layouts  14.3 us (7%)
    all_to_all x1, blocking collectives, on_device(): parts = lax.all_to_all(packed, chips, 0, 0, tiled=True)  50.6 us
    all_to_all x1, blocking collectives, on_device(): half = lax.all_to_all(spread.reshape(packed_shape), chips, 0, 0, tiled=True)  45.6 us
    pallas_call x9, Pallas kernels, call(): pl.pallas_call(body, out_shape=out_shape, in_specs=[SMEM if i in smem els...  39 us
    ppermute x3, waiting for transfers between devices, gather_members(): lax.ppermute(forecast, axes, [(i, i ^ step) for i in range(4)])  16 us
    unnamed x60, local copies, waits for them, and re-layouts  13.7 us
    pallas_call x1, Pallas kernels, on_device(): pl.pallas_call(unpack_body, grid=(GROUPS,), out_shape=[jax.ShapeDtypeStru...  12.1 us
    ppermute x1, waiting for transfers between devices, on_device(): from_prev = lax.ppermute(d_high, 'space', up)  6.91 us
    ppermute x1, starting transfers between devices, on_device(): high = lax.ppermute(sent[1], 'space', down)  6.25 us
  transfers between devices with their start and end apart: 11, of which 5 were waited for; matrix products, arithmetic and copies ran while one was open for 0% of the time, Pallas kernels for 5%

profile of v1, /device:TPU:2, one launch (start us, length us, event | category | flops | bytes accessed | tf_op | source)
XLA Modules:
  0.0 206.3 jit_solution(5478150917581884699)
XLA Ops:
  2.7 6.2 %collective-permute-start.1 = (bf16[2,16,768]{2,1,0:T(8,128)(2,1)S(1)}, bf16[2,16,768]{2,1,0:T(8,128)(2,1)S(1)}, u32[]{:S(2)}, u32[]{:S(2)}) collective-permute-start(bf16[2,16,768]{2,1,0:T(8,128)(2,1)S(1)} %get-tuple-element.65), channel_id=1, source_target_pairs={{4,0},{8,4},{12,8},{16,12},{20,16},{24,20},{28,24},{32,28},{36,32}... | collective-permute-start | bytes 147464 | tf_op jit(solution)/shard_map/ppermute | solution.py:461
  9.0 1.9 collective-permute-start
  10.9 2.0 copy-done
  14.5 1.5 shard_map.180
  16.0 2.0 collective-permute-done.low
  18.0 10.3 %shard_map.182 = (bf16[64,768]{1,0:T(8,128)(2,1)S(1)}, bf16[64,1536]{1,0:T(8,128)(2,1)S(1)}, bf16[256,768]{1,0:T(8,128)(2,1)S(1)}, bf16[256,768]{1,0:T(8,128)(2,...) custom-call(bf16[2,128,768]{2,1,0:T(8,128)(2,1)S(1)} %get-tuple-elem, ...), custom_call_target="tpu_custom_call" | custom-call | flops 3000000000 | bytes 15787264 | tf_op jit(solution)/shard_map/pallas_call | solution.py:34
  31.2 1.6 collective-permute-start.5
  32.8 2.0 collective-permute-start.4
  35.5 7.7 %collective-permute-done.5.rest_2_ = bf16[2,83,1024]{2,1,0:T(8,128)(2,1)} collective-permute-done((bf16[2,83,1024]{2,1,0:T(8,128)(2,1)}, bf16[2,83,1024]{2,1,0:T(8,128)(2,1)}, u32[]{:S(2)}, u32[]{:S(2)}) %collective-permute-start.5) | collective-permute-done | bytes 340000 | tf_op jit(solution)/shard_map/ppermute | solution.py:579
  43.1 8.3 %collective-permute-done.4.rest_1_ = bf16[2,83,1024]{2,1,0:T(8,128)(2,1)} collective-permute-done((bf16[2,83,1024]{2,1,0:T(8,128)(2,1)}, bf16[2,83,1024]{2,1,0:T(8,128)(2,1)}, u32[]{:S(2)}, u32[]{:S(2)}) %collective-permute-start.4) | collective-permute-done | bytes 340000 | tf_op jit(solution)/shard_map/ppermute | solution.py:579
  53.4 1.0 copy-done.24
  55.4 11.2 %shard_map.183 = (bf16[256,768]{1,0:T(8,128)(2,1)S(1)}, bf16[256,768]{1,0:T(8,128)(2,1)S(1)}, bf16[64,16,640]{2,1,0:T(8,128)(2,1)}, bf16[64,16,640]{2,1,0:T(8,128)(2,1)}, bf16[16,128]{1,0:T(8,128)(2,1)S(1)}) custom-call(s32[1]{0:T(128)} %bitcast.core, s32[1]{0:T(128)} %dynamic_slice.3.live_count, bf16[2,83,1024]{2,1,0:T(8,128)(2,1)} %get-tuple-element.41.mine, ...), custom_call_target="tpu_custom_call" | custom-call | flops 6000000000 | bytes 14938632 | tf_op jit(solution)/shard_map/pallas_call | solution.py:34
  66.7 2.7 %shard_map.184 = (bf16[2,256,1152]{2,1,0:T(8,128)(2,1)S(1)}, bf16[2,64,768]{2,1,0:T(8,128)(2,1)S(1)}, bf16[320,1152]{1,0:T(8,128)(2,1)S(1)}) custom-call(s32[1]{0:T(128)} %bitcast.core, bf16[256,2304]{1,0:T(8,128)(2,1)S(1)} %copy-done.13, bf16[64,1536]{1,0:T(8,128)(2,1)S(1)} %copy-done.28, s32[8,128]{1,0:T(8,128)S(1)} %copy-done.19, s32[1,128]{1,0:T(1,128)S(1)} %bitcast.13, ...), custom_call_target="tpu_custom_call" | custom-call | flops 2000000000 | bytes 3887620 | tf_op jit(solution)/shard_map/pallas_call | solution.py:34
  70.3 4.7 %shard_map.185 = (f32[2,768,128]{2,1,0:T(8,128)S(1)}, bf16[2,16,768]{2,1,0:T(8,128)(2,1)S(1)}, bf16[2,16,768]{2,1,0:T(8,128)(2,1)S(1)}, bf16[32,768]{1,0:T(8,128)(2,1)S(1)}) custom-call(bf16[2,128,768]{2,1,0:T(8,128)(2,1)S(1)} %get-tuple-element.37.own, bf16[2,16,768]{2,1,0:T(8,128)(2,1)S(1)} %copy-done.17, ...), custom_call_target="tpu_custom_call" | custom-call | flops 2000000000 | bytes 6832384 | tf_op jit(solution)/shard_map/pallas_call | solution.py:34
  75.0 4.4 %shard_map.186 = bf16[64,16,1536]{2,1,0:T(8,128)(2,1)} custom-call(s32[1]{0:T(128)} %bitcast.core, bf16[256,768]{1,0:T(8,128)(2,1)S(1)} %get-tuple-element.36.normed, bf16[64,768]{1,0:T(8,128)(2,1)S(1)} %get-tuple-element.39.normed_rim, bf16[320,768]{1,0:T(8,128)(2,1)S(1)} %collective-permute-done.2.normed_theirs, ...), custom_call_target="tpu_custom_call" | custom-call | flops 2000000000 | bytes 8916996 | tf_op jit(solution)/shard_map/pallas_call | solution.py:34
  79.5 50.6 %all_to_all.10 = bf16[64,16,1536]{2,1,0:T(8,128)(2,1)} all-to-all(bf16[64,16,1536]{2,1,0:T(8,128)(2,1)} %shard_map.186), channel_id=1, replica_groups=mesh['space'=32,'zhi'=2,'core'=2] {'space','zhi'}, dimensions={0} | all-to-all | bytes 6291456 | tf_op jit(solution)/shard_map/all_to_all | solution.py:536
  130.0 2.6 %shard_map.187 = bf16[64,1,16,1536]{3,2,1,0:T(8,128)(2,1)S(1)} custom-call(bf16[64,1,16,1536]{3,2,1,0:T(8,128)(2,1)} %bitcast.14), custom_call_target="tpu_custom_call" | custom-call | bytes 6291456 | tf_op jit(solution)/shard_map/pallas_call | solution.py:34
  132.6 45.6 %all_to_all.11.own = bf16[64,16,1536]{2,1,0:T(8,128)(2,1)S(1)} all-to-all(bf16[64,16,1536]{2,1,0:T(8,128)(2,1)S(1)} %bitcast.10), channel_id=1, replica_groups=mesh['space'=32,'zhi'=2,'core'=2] {'space','zhi'}, dimensions={0} | all-to-all | bytes 6291456 | tf_op jit(solution)/shard_map/all_to_all | solution.py:542
  178.2 4.0 %collective-permute-start.9 = (bf16[2,16,768]{2,1,0:T(8,128)(2,1)S(1)}, bf16[2,16,768]{2,1,0:T(8,128)(2,1)S(1)}, u32[]{:S(2)}, u32[]{:S(2)}) collective-permute-start(bf16[2,16,768]{2,1,0:T(8,128)(2,1)S(1)} %get-tuple-element.58), channel_id=1, source_target_pairs={{4,0},{8,4},{12,8},{16,12},{20,16},{24,20},{28,24},{32,28},{36,32}... | collective-permute-start | bytes 147464 | tf_op jit(solution)/shard_map/ppermute | solution.py:544
  182.2 1.9 collective-permute-start.10
  184.3 6.9 %collective-permute-done.10.from_prev = bf16[2,16,768]{2,1,0:T(8,128)(2,1)S(1)} collective-permute-done((bf16[2,16,768]{2,1,0:T(8,128)(2,1)S(1)}, bf16[2,16,768]{2,1,0:T(8,128)(2,1)S(1)}, u32[]{:S(2)}, u32[]{:S(2)}) %collective-permute-start.10) | collective-permute-done | bytes 49184 | tf_op jit(solution)/shard_map/ppermute | solution.py:545
  191.2 1.3 shard_map.189
  192.4 1.6 copy-done.29
  194.1 12.1 %shard_map.188 = (f32[768,2304]{1,0:T(8,128)}, f32[768,768]{1,0:T(8,128)}, f32[32,768]{1,0:T(8,128)}, f32[768,768]{1,0:T(8,128)}, f32[83,768]{1,0:T(8,128)}, /*index=5*/f32[1,1]{1,0:T(1,128)}) custom-call(s32[1]{0:T(128)} %bitcast.core, s32[1,32]{1,0:T(1,128)S(1)} %bitcast.11, bf16[64,16,1536]{2,1,0:T(8,128)(2,1)S(1)} %all_to_all.11.own, ...), custom_call_target="tpu_custom_call" | custom-call | tf_op jit(solution)/shard_map/pallas_call | solution.py:551
  (73 shorter events, 11.2 us)
Async XLA Ops:
  2.3 15.6 %copy-start.4 = (f32[32,768]{1,0:T(8,128)S(1)}, f32[32,768]{1,0:T(8,128)}, u32[]{:S(2)}) copy-start(f32[32,768]{1,0:T(8,128)} %w_noise.5) | copy-start | bytes 294916
  2.3 15.6 %copy-start.8 = (f32[2,32]{1,0:T(2,128)S(1)}, f32[2,32]{1,0:T(2,128)}, u32[]{:S(2)}) copy-start(f32[2,32]{1,0:T(2,128)} %noise.5) | copy-start | bytes 772
  2.3 15.6 %copy-start.15 = (bf16[83,768]{1,0:T(8,128)(2,1)S(1)}, bf16[83,768]{1,0:T(8,128)(2,1)}, u32[]{:S(2)}) copy-start(bf16[83,768]{1,0:T(8,128)(2,1)} %rest_11_.1) | copy-start | bytes 382468
  2.3 15.6 %copy-start.18 = (s32[3,1024]{1,0:T(4,128)S(1)}, s32[3,1024]{1,0:T(4,128)}, u32[]{:S(2)}) copy-start(s32[3,1024]{1,0:T(4,128)} %dec_nodes.1) | copy-start | bytes 36868
  2.3 15.7 %copy-start.19 = (s32[8,128]{1,0:T(8,128)S(1)}, s32[8,128]{1,0:T(8,128)}, u32[]{:S(2)}) copy-start(s32[8,128]{1,0:T(8,128)} %nbr.3) | copy-start | bytes 12292
  2.3 15.7 %copy-start.20 = (s32[128]{0:T(128)S(1)}, s32[128]{0:T(128)}, u32[]{:S(2)}) copy-start(s32[128]{0:T(128)} %param.16) | copy-start | bytes 1540
  2.7 13.3 %collective-permute-start.1 = (bf16[2,16,768]{2,1,0:T(8,128)(2,1)S(1)}, bf16[2,16,768]{2,1,0:T(8,128)(2,1)S(1)}, u32[]{:S(2)}, u32[]{:S(2)}) collective-permute-start(bf16[2,16,768]{2,1,0:T(8,128)(2,1)S(1)} %get-tuple-element.65), channel_id=1, source_target_pairs={{4,0},{8,4},{12,8},{16,12},{20,16},{24,20},{28,24},{32,28},{36,32}... | collective-permute-start | bytes 147464 | tf_op jit(solution)/shard_map/ppermute | solution.py:461
  9.0 9.0 %collective-permute-start = (bf16[2,16,768]{2,1,0:T(8,128)(2,1)S(1)}, bf16[2,16,768]{2,1,0:T(8,128)(2,1)S(1)}, u32[]{:S(2)}, u32[]{:S(2)}) collective-permute-start(bf16[2,16,768]{2,1,0:T(8,128)(2,1)S(1)} %get-tuple-element.66), channel_id=1, source_target_pairs={{0,4},{4,8},{8,12},{12,16},{16,20},{20,24},{24,28},{28,32},{32,36}... | collective-permute-start | bytes 147464 | tf_op jit(solution)/shard_map/ppermute | solution.py:460
  16.0 12.4 %copy-start.12 = (bf16[256,2304]{1,0:T(8,128)(2,1)}, bf16[256,2304]{1,0:T(8,128)(2,1)S(1)}, u32[]{:S(2)}) copy-start(bf16[256,2304]{1,0:T(8,128)(2,1)S(1)} %get-tuple-element.38.proj) | copy-start | bytes 3538948
  17.9 10.4 %copy-start.16 = (bf16[2,16,768]{2,1,0:T(8,128)(2,1)}, bf16[2,16,768]{2,1,0:T(8,128)(2,1)S(1)}, u32[]{:S(2)}) copy-start(bf16[2,16,768]{2,1,0:T(8,128)(2,1)S(1)} %collective-permute-done.low) | copy-start | bytes 147460
  18.0 16.9 %copy-start.9 = (s32[32]{0:T(128)S(1)}, s32[32]{0:T(128)}, u32[]{:S(2)}) copy-start(s32[32]{0:T(128)} %param.18) | copy-start | bytes 388
  31.2 12.0 %collective-permute-start.5 = (bf16[2,83,1024]{2,1,0:T(8,128)(2,1)}, bf16[2,83,1024]{2,1,0:T(8,128)(2,1)}, u32[]{:S(2)}, u32[]{:S(2)}) collective-permute-start(bf16[2,83,1024]{2,1,0:T(8,128)(2,1)} %get-tuple-element.41.mine), channel_id=1, source_target_pairs={{0,3},{1,2},{2,1},{3,0},{4,7},{5,6},{6,5},{7,4},{8,11},{9,10},{10,... | collective-permute-start | bytes 1019912 | tf_op jit(solution)/shard_map/ppermute | solution.py:579
  32.8 18.7 %collective-permute-start.4 = (bf16[2,83,1024]{2,1,0:T(8,128)(2,1)}, bf16[2,83,1024]{2,1,0:T(8,128)(2,1)}, u32[]{:S(2)}, u32[]{:S(2)}) collective-permute-start(bf16[2,83,1024]{2,1,0:T(8,128)(2,1)} %get-tuple-element.41.mine), channel_id=1, source_target_pairs={{0,2},{1,3},{2,0},{3,1},{4,6},{5,7},{6,4},{7,5},{8,10},{9,11},{10,... | collective-permute-start | bytes 1019912 | tf_op jit(solution)/shard_map/ppermute | solution.py:579
  34.8 16.6 %collective-permute-start.3 = (bf16[2,83,1024]{2,1,0:T(8,128)(2,1)}, bf16[2,83,1024]{2,1,0:T(8,128)(2,1)}, u32[]{:S(2)}, u32[]{:S(2)}) collective-permute-start(bf16[2,83,1024]{2,1,0:T(8,128)(2,1)} %get-tuple-element.41.mine), channel_id=1, source_target_pairs={{0,1},{1,0},{2,3},{3,2},{4,5},{5,4},{6,7},{7,6},{8,9},{9,8},{10,11... | collective-permute-start | bytes 1019912 | tf_op jit(solution)/shard_map/ppermute | solution.py:579
  55.4 11.2 %copy-start.13 = (bf16[256,2304]{1,0:T(8,128)(2,1)S(1)}, bf16[256,2304]{1,0:T(8,128)(2,1)}, u32[]{:S(2)}) copy-start(bf16[256,2304]{1,0:T(8,128)(2,1)} %copy-done.12) | copy-start | bytes 3538948
  55.4 11.2 %copy-start.28 = (bf16[64,1536]{1,0:T(8,128)(2,1)S(1)}, bf16[64,1536]{1,0:T(8,128)(2,1)}, u32[]{:S(2)}) copy-start(bf16[64,1536]{1,0:T(8,128)(2,1)} %copy-done.27) | copy-start | bytes 589828
  66.6 8.4 %collective-permute-start.7 = (bf16[64,16,640]{2,1,0:T(8,128)(2,1)}, bf16[64,16,640]{2,1,0:T(8,128)(2,1)S(1)}, u32[]{:S(2)}, u32[]{:S(2)}) collective-permute-start(bf16[64,16,640]{2,1,0:T(8,128)(2,1)} %get-tuple-element.52), channel_id=1, source_target_pairs={{0,1},{1,0},{2,3},{3,2},{4,5},{5,4},{6,7},{7,6},{8,9},{9,8},{10,11... | collective-permute-start | bytes 3932168 | tf_op jit(solution)/shard_map/ppermute | solution.py:503
  69.4 5.7 %collective-permute-start.6 = (bf16[320,1152]{1,0:T(8,128)(2,1)S(1)}, bf16[320,1152]{1,0:T(8,128)(2,1)S(1)}, u32[]{:S(2)}, u32[]{:S(2)}) collective-permute-start(bf16[320,1152]{1,0:T(8,128)(2,1)S(1)} %get-tuple-element.50), channel_id=1, source_target_pairs={{0,1},{1,0},{2,3},{3,2},{4,5},{5,4},{6,7},{7,6},{8,9},{9,8},{10,11... | collective-permute-start | bytes 2211848 | tf_op jit(solution)/shard_map/ppermute | solution.py:515
  70.0 5.0 %collective-permute-start.2 = (bf16[320,768]{1,0:T(8,128)(2,1)S(1)}, bf16[320,768]{1,0:T(8,128)(2,1)S(1)}, u32[]{:S(2)}, u32[]{:S(2)}) collective-permute-start(bf16[320,768]{1,0:T(8,128)(2,1)S(1)} %pad_maximum_fusion), channel_id=1, source_target_pairs={{0,1},{1,0},{2,3},{3,2},{4,5},{5,4},{6,7},{7,6},{8,9},{9,8},{10,11... | collective-permute-start | bytes 1474568 | tf_op jit(solution)/shard_map/ppermute | solution.py:485
  70.3 4.7 %copy-start.2 = (bf16[64,16,640]{2,1,0:T(8,128)(2,1)S(1)}, bf16[64,16,640]{2,1,0:T(8,128)(2,1)}, u32[]{:S(2)}) copy-start(bf16[64,16,640]{2,1,0:T(8,128)(2,1)} %get-tuple-element.51.keep) | copy-start | bytes 3932164
  132.6 58.5 %copy-start.6 = (s32[2,16]{1,0:T(2,128)S(1)}, s32[2,16]{1,0:T(2,128)}, u32[]{:S(2)}) copy-start(s32[2,16]{1,0:T(2,128)} %rows.3) | copy-start | bytes 388
  178.2 14.2 %collective-permute-start.8 = (bf16[64,16,1536]{2,1,0:T(8,128)(2,1)S(1)}, bf16[64,16,1536]{2,1,0:T(8,128)(2,1)S(1)}, u32[]{:S(2)}, u32[]{:S(2)}) collective-permute-start(bf16[64,16,1536]{2,1,0:T(8,128)(2,1)S(1)} %all_to_all.11.own), channel_id=1, source_target_pairs={{0,1},{1,0},{2,3},{3,2},{4,5},{5,4},{6,7},{7,6},{8,9},{9,8},{10,11... | collective-permute-start | bytes 9437192 | tf_op jit(solution)/shard_map/ppermute | solution.py:543
  178.2 6.0 %collective-permute-start.9 = (bf16[2,16,768]{2,1,0:T(8,128)(2,1)S(1)}, bf16[2,16,768]{2,1,0:T(8,128)(2,1)S(1)}, u32[]{:S(2)}, u32[]{:S(2)}) collective-permute-start(bf16[2,16,768]{2,1,0:T(8,128)(2,1)S(1)} %get-tuple-element.58), channel_id=1, source_target_pairs={{4,0},{8,4},{12,8},{16,12},{20,16},{24,20},{28,24},{32,28},{36,32}... | collective-permute-start | bytes 147464 | tf_op jit(solution)/shard_map/ppermute | solution.py:544
  182.2 9.0 %collective-permute-start.10 = (bf16[2,16,768]{2,1,0:T(8,128)(2,1)S(1)}, bf16[2,16,768]{2,1,0:T(8,128)(2,1)S(1)}, u32[]{:S(2)}, u32[]{:S(2)}) collective-permute-start(bf16[2,16,768]{2,1,0:T(8,128)(2,1)S(1)} %get-tuple-element.59), channel_id=1, source_target_pairs={{0,4},{4,8},{8,12},{12,16},{16,20},{20,24},{24,28},{28,32},{32,36}... | collective-permute-start | bytes 147464 | tf_op jit(solution)/shard_map/ppermute | solution.py:545
  (17 other events, 24.4 us)

commit v2 on v1

--- a/solution.py
+++ b/solution.py
@@ -9,6 +9,7 @@
 HEAD = 128
 TILE = 128
 GROUPS = 16
+BLOCKS = 4
 SLOTS_A = 5
 SLOTS_B = 7
 CHUNKS = 4 * GROUPS
@@ -20,14 +21,14 @@
 TN = (((0,), (0,)), ((), ()))
 VMEM = pl.BlockSpec(memory_space=pltpu.VMEM)
 SMEM = pl.BlockSpec(memory_space=pltpu.SMEM)
-PARAMS = pltpu.CompilerParams(vmem_limit_bytes=48 * 1024 * 1024)
+MIB = 1024 * 1024
 
 
 def mm(a, b, dims=NN):
     return lax.dot_general(a, b, dims, preferred_element_type=F32)
 
 
-def call(body, out_shape, *args, smem=(), flops=0, scratch=()):
+def call(body, out_shape, *args, smem=(), flops=0, scratch=(), vmem=16):
     out_shape = [jax.ShapeDtypeStruct(s, d) for s, d in out_shape]
     size = sum(a.size * a.dtype.itemsize for a in args)
     size += sum(o.size * o.dtype.itemsize for o in out_shape)
@@ -37,7 +38,7 @@
         in_specs=[SMEM if i in smem else VMEM for i in range(len(args))],
         out_specs=[VMEM] * len(out_shape),
         scratch_shapes=list(scratch),
-        compiler_params=PARAMS,
+        compiler_params=pltpu.CompilerParams(vmem_limit_bytes=vmem * MIB),
         cost_estimate=pl.CostEstimate(flops=flops, bytes_accessed=size, transcendentals=0),
     )(*args)
 
@@ -373,61 +374,98 @@
 
 
 def unpack_body(
-    core, counts, own, other, g_qkv, g_out, g_noise, g_hid, g_pred, mean, pred_rows
+    core, half, *rest
 ):
-    k = pl.program_id(0)
-    first_core = core[0] == 0
-    width = g_hid.shape[1]
-    half = width // 2
-    for c in range(2):
-        def tile(chunk, lane):
-            at = (chunk, slice(None), slice(lane, lane + TILE))
-            mine, theirs = own[at].astype(F32), other[at].astype(F32)
-            return jnp.where(first_core == (c == 0), mine, theirs)
-
-        for slot in range(18):
-            target = (g_hid, g_out)[slot // 9]
-            row, column = 16 * (slot % 9 // 3), c * half + TILE * (slot % 3)
-            target[row : row + 16, column : column + TILE] = tile(
-                slot // SLOTS_A, TILE * (slot % SLOTS_A)
-            )
-        for slot in range(27):
-            row, column = 16 * (slot // 9), slot % 9
-            column = width * (column // 3) + c * half + TILE * (column % 3)
-            g_qkv[row : row + 16, column : column + TILE] = tile(
-                slot // SLOTS_B, TILE * (SLOTS_A + slot % SLOTS_B)
-            )
-        for slot in (18, 19):
-            index = k + GROUPS * (slot - 18)
-
-            @pl.when(index < 18)
-            def _(slot=slot, index=index, c=c, tile=tile):
-                row = pl.multiple_of(16 * (index // 3), 16)
-                column = pl.multiple_of(c * half + TILE * (index % 3), TILE)
-                pred_rows[pl.ds(row, 16), pl.ds(column, TILE)] = tile(
-                    slot // SLOTS_A, TILE * (slot % SLOTS_A)
-                )
-
-    spare = (3, slice(None), slice(TILE * (SLOTS_A + 6), TILE * (SLOTS_A + 7)))
-
-    @pl.when(k < 12)
+    (g_qkv, g_out, g_hid, g_pred, g_noise, loss, pred_rows) = rest[-7:]
+    before = rest[:-7]
+    r, section = pl.program_id(0), pl.program_id(1)
+    per_block = GROUPS // BLOCKS
+
+    def tile(group, slot, first=0, size=SLOTS_A):
+        lane = first + TILE * (slot % size)
+        return half[4 * group + slot // size, :, lane : lane + TILE].astype(F32)
+
+    for group in range(per_block):
+        for row in range(3):
+            at = slice(48 * group + 16 * row, 48 * group + 16 * row + 16)
+            for s in range(3):
+
+                @pl.when(section == s)
+                def _(group=group, row=row, at=at, s=s):
+                    for j in range(3):
+                        g_qkv[at, TILE * j : TILE * (j + 1)] = tile(
+                            group, 9 * row + 3 * s + j, TILE * SLOTS_A, SLOTS_B
+                        )
+
+    @pl.when(section == 0)
     def _():
-        row = pl.multiple_of(16 * (k // 6), 16)
-        column = pl.multiple_of(TILE * (k % 6), TILE)
-        g_noise[pl.ds(row, 16), pl.ds(column, TILE)] = own[spare].astype(F32) + other[
-            spare
-        ].astype(F32)
-
-    @pl.when(k == 12)
-    def _():
-        channels = g_pred.shape[0]
-        total = jnp.sum(own[spare].astype(F32) + other[spare].astype(F32), keepdims=True)
-        live = jnp.sum(counts[...].astype(F32), keepdims=True)
-        mean[...] = total / (channels * live)
-
-    @pl.when(k == GROUPS - 1)
-    def _():
-        g_pred[...] = pred_rows[: g_pred.shape[0]]
+        for group in range(per_block):
+            for slot in range(18):
+                target = (g_hid, g_out)[slot // 9]
+                row, column = 48 * group + 16 * (slot % 9 // 3), TILE * (slot % 3)
+                target[row : row + 16, column : column + TILE] = tile(group, slot)
+            k = per_block * r + group
+            for slot in (18, 19):
+                index = k + GROUPS * (slot - 18)
+
+                @pl.when(index < 18)
+                def _(slot=slot, index=index, group=group):
+                    row = pl.multiple_of(16 * (index // 3), 16)
+                    column = pl.multiple_of(TILE * (index % 3), TILE)
+                    pred_rows[pl.ds(row, 16), pl.ds(column, TILE)] = tile(group, slot)
+
+            spare = tile(group, 27, TILE * SLOTS_A, SLOTS_B)
+
+            @pl.when(k < 12)
+            def _(k=k, spare=spare):
+                row = pl.multiple_of(16 * (k // 6), 16)
+                column = pl.multiple_of(TILE * (k % 6), TILE)
+                here = (pl.ds(row, 16), pl.ds(column, TILE))
+                g_noise[here] = spare + before[-2][here] if before else spare
+
+            @pl.when(k == 12)
+            def _(spare=spare):
+                total = jnp.sum(spare, keepdims=True)
+                loss[...] = total + before[-1][...] if before else total
+
+        @pl.when(r == BLOCKS - 1)
+        def _():
+            g_pred[...] = pred_rows[: g_pred.shape[0]]
+
+
+def unpack(which, half, width, channels, before=()):
+    wide = width // 2
+    rows = width // BLOCKS
+    const = lambda r, s, c: (0, 0)
+    spec = lambda shape, at: pl.BlockSpec(shape, at)
+    in_specs = [spec((CHUNKS // BLOCKS,) + half.shape[1:], lambda r, s, c: (r, 0, 0))]
+    if before:
+        in_specs += [pl.BlockSpec(memory_space=pl.ANY)] * 4
+        in_specs += [spec((32, width), const), spec((1, 1), const)]
+    shapes = (
+        (width, 3 * width), (width, width), (width, width), (channels, width), (32, width), (1, 1),
+    )
+    return pl.pallas_call(
+        unpack_body,
+        grid_spec=pltpu.PrefetchScalarGridSpec(
+            num_scalar_prefetch=1,
+            grid=(BLOCKS, 3),
+            in_specs=in_specs,
+            out_specs=[
+                spec((rows, wide), lambda r, s, c: (r, 2 * s + c[0])),
+                spec((rows, wide), lambda r, s, c: (r, c[0])),
+                spec((rows, wide), lambda r, s, c: (r, c[0])),
+                spec((channels, wide), lambda r, s, c: (0, c[0])),
+                spec((32, width), const),
+                spec((1, 1), const),
+            ],
+            scratch_shapes=[pltpu.VMEM((96, wide), F32)],
+        ),
+        out_shape=[jax.ShapeDtypeStruct(shape, F32) for shape in shapes],
+        input_output_aliases={2 + i: i for i in range(4)} if before else {},
+        compiler_params=pltpu.CompilerParams(vmem_limit_bytes=16 * MIB),
+        cost_estimate=pl.CostEstimate(flops=0, bytes_accessed=9 * 10**6, transcendentals=0),
+    )(which, half, *before)
 
 
 def join_body(d_own, rows, from_next, from_prev, d_latent):
@@ -533,6 +571,9 @@
     )
     chips = ("space", "zhi")
     count = lax.axis_size(chips)
+    from_next = lax.ppermute(d_low, "space", down)
+    from_prev = lax.ppermute(d_high, "space", up)
+    packed, from_next, from_prev = lax.optimization_barrier((packed, from_next, from_prev))
     parts = lax.all_to_all(packed, chips, 0, 0, tiled=True)
     (spread,) = call(
         sum_body,
@@ -541,43 +582,20 @@
     )
     half = lax.all_to_all(spread.reshape(packed_shape), chips, 0, 0, tiled=True)
     other = lax.ppermute(half, "core", swap)
-    from_next = lax.ppermute(d_low, "space", down)
-    from_prev = lax.ppermute(d_high, "space", up)
     (d_latent,) = call(
         join_body, [((members, width, nodes), F32)], d_own, send_rows, from_next, from_prev
     )
-    block = pl.BlockSpec((4,) + packed_shape[1:], lambda k: (k, 0, 0))
-    whole = lambda shape: pl.BlockSpec(shape, lambda k: (0, 0))
-    g_qkv, g_out, g_noise, g_hid, g_pred, mean = pl.pallas_call(
-        unpack_body,
-        grid=(GROUPS,),
-        out_shape=[
-            jax.ShapeDtypeStruct(shape, F32)
-            for shape in (
-                (width, 3 * width), (width, width), (32, width), (width, width),
-                (channels, width), (1, 1),
-            )
-        ],
-        in_specs=[SMEM, whole((1, counts.shape[0])), block, block],
-        out_specs=[
-            pl.BlockSpec((48, 3 * width), lambda k: (k, 0)),
-            pl.BlockSpec((48, width), lambda k: (k, 0)),
-            whole((32, width)),
-            pl.BlockSpec((48, width), lambda k: (k, 0)),
-            whole((channels, width)),
-            whole((1, 1)),
-        ],
-        scratch_shapes=[pltpu.VMEM((96, width), F32)],
-        compiler_params=PARAMS,
-    )(core, counts[None, :], half, other)
-    return mean[0, 0], d_latent, g_qkv, g_out, g_noise, g_hid, g_pred
+    mine = unpack(core, half, width, channels)
+    g_qkv, g_out, g_hid, g_pred, g_noise, loss = unpack(1 - core, other, width, channels, mine)
+    mean = loss[0, 0] / (channels * jnp.sum(counts).astype(F32))
+    return mean, d_latent, g_qkv, g_out, g_noise, g_hid, g_pred
 
 
 def gather_members(forecast):
-    axes = ("zhi", "core")
-    return [
-        lax.ppermute(forecast, axes, [(i, i ^ step) for i in range(4)]) for step in (1, 2, 3)
-    ]
+    swap = [(0, 1), (1, 0)]
+    far = lax.ppermute(forecast, "zhi", swap)
+    near = lax.ppermute(forecast, "core", swap)
+    return near, far, lax.ppermute(far, "core", swap)
 
 
 def solution(mesh):

time: 207 us -> 207 us (level); the launches traced: 206 us -> 204 us
  local copies, waits for them, and re-layouts: 14.3 us -> 29.7 us
  waiting for transfers between devices: 25 us -> 12.3 us
  Pallas kernels: 51.1 us -> 43.8 us
  between operations: 1.04 us -> 3.44 us
    unnamed x60 -> x92, local copies, waits for them, and re-layouts: 13.7 us -> 29.1 us
    pallas_call x9, Pallas kernels: 39 us -> 26.3 us  [call(): pl.pallas_call(body, out_shape=out_shape, in_specs=[SMEM if i in smem els...]
    ppermute x3, waiting for transfers between devices: 16 us -> 9.56 us  [the longest x1 8.15 us: gather_members(): far = lax.ppermute(forecast, 'zhi', swap)]
    pallas_call x1 -> x2, Pallas kernels: 12.1 us -> 17.5 us  [unpack(): pl.pallas_call(unpack_body, grid_spec=pltpu.PrefetchScalarGridSpec(num_sc...]
    ppermute x1, waiting for transfers between devices: 6.91 us -> 2.74 us  [on_device(): from_prev = lax.ppermute(d_high, 'space', up)]
    all_to_all x1, blocking collectives: 50.6 us -> 48.1 us  [on_device(): parts = lax.all_to_all(packed, chips, 0, 0, tiled=True)]
  transfers between devices with their start and end apart: 11 -> 11, of which waited for: 5 -> 3; matrix products, arithmetic and copies ran while one was open for 0% -> 1% of each run, Pallas kernels for 5% -> 8%
where the time goes in v2:
time: 207 us; the launch traced here: 204 us
  blocking collectives  94.2 us (46%)
  Pallas kernels  43.8 us (21%)
  local copies, waits for them, and re-layouts  29.7 us (14%)
  starting transfers between devices  19.7 us (10%)
  waiting for transfers between devices  12.3 us (6%)
  between operations  3.44 us (2%)
    all_to_all x1, blocking collectives, on_device(): parts = lax.all_to_all(packed, chips, 0, 0, tiled=True)  48.1 us
    all_to_all x1, blocking collectives, on_device(): half = lax.all_to_all(spread.reshape(packed_shape), chips, 0, 0, tiled=True)  46.1 us
    unnamed x92, local copies, waits for them, and re-layouts  29.1 us
    pallas_call x9, Pallas kernels, call(): pl.pallas_call(body, out_shape=out_shape, in_specs=[SMEM if i in smem els...  26.3 us
    pallas_call x2, Pallas kernels, unpack(): pl.pallas_call(unpack_body, grid_spec=pltpu.PrefetchScalarGridSpec(num_sc...  17.5 us
    ppermute x1, waiting for transfers between devices, gather_members(): far = lax.ppermute(forecast, 'zhi', swap)  8.15 us
    ppermute x1, starting transfers between devices, on_device(): high = lax.ppermute(sent[1], 'space', down)  5.37 us
  transfers between devices with their start and end apart: 11, of which 3 were waited for; matrix products, arithmetic and copies ran while one was open for 1% of the time, Pallas kernels for 8%

profile of v2, /device:TPU:2, one launch (start us, length us, event | category | flops | bytes accessed | tf_op | source)
XLA Modules:
  0.0 203.8 jit_solution(15699102436484932119)
XLA Ops:
  2.7 3.5 %collective-permute-start = (bf16[2,16,768]{2,1,0:T(8,128)(2,1)S(1)}, bf16[2,16,768]{2,1,0:T(8,128)(2,1)S(1)}, u32[]{:S(2)}, u32[]{:S(2)}) collective-permute-start(bf16[2,16,768]{2,1,0:T(8,128)(2,1)S(1)} %get-tuple-element.84), channel_id=1, source_target_pairs={{0,4},{4,8},{8,12},{12,16},{16,20},{20,24},{24,28},{28,32},{32,36}... | collective-permute-start | bytes 147464 | tf_op jit(solution)/shard_map/ppermute | solution.py:498
  6.2 5.4 %collective-permute-start.1 = (bf16[2,16,768]{2,1,0:T(8,128)(2,1)S(1)}, bf16[2,16,768]{2,1,0:T(8,128)(2,1)S(1)}, u32[]{:S(2)}, u32[]{:S(2)}) collective-permute-start(bf16[2,16,768]{2,1,0:T(8,128)(2,1)S(1)} %get-tuple-element.83), channel_id=1, source_target_pairs={{4,0},{8,4},{12,8},{16,12},{20,16},{24,20},{28,24},{32,28},{36,32}... | collective-permute-start | bytes 147464 | tf_op jit(solution)/shard_map/ppermute | solution.py:499
  11.6 2.0 copy-done
  15.1 1.5 shard_map.180
  17.5 1.8 copy-done.15
  20.6 6.4 %shard_map.182 = (bf16[64,768]{1,0:T(8,128)(2,1)S(1)}, bf16[64,1536]{1,0:T(8,128)(2,1)S(1)}, bf16[256,768]{1,0:T(8,128)(2,1)S(1)}, bf16[256,768]{1,0:T(8,128)(2,...) custom-call(bf16[2,128,768]{2,1,0:T(8,128)(2,1)S(1)} %get-tuple-elem, ...), custom_call_target="tpu_custom_call" | custom-call | flops 3000000000 | bytes 15787264 | tf_op jit(solution)/shard_map/pallas_call | solution.py:35
  27.6 1.7 copy-done.33
  29.3 1.6 copy-done.35
  33.8 3.9 %collective-permute-start.4 = (bf16[2,83,1024]{2,1,0:T(8,128)(2,1)}, bf16[2,83,1024]{2,1,0:T(8,128)(2,1)}, u32[]{:S(2)}, u32[]{:S(2)}) collective-permute-start(bf16[2,83,1024]{2,1,0:T(8,128)(2,1)} %get-tuple-element.50.mine), channel_id=1, source_target_pairs={{0,2},{2,0},{1,3},{3,1},{4,6},{6,4},{5,7},{7,5},{8,10},{10,8},{9,1... | collective-permute-start | bytes 1019912 | tf_op jit(solution)/shard_map/ppermute | solution.py:596
  37.6 8.2 %collective-permute-done.4.rest_1_ = bf16[2,83,1024]{2,1,0:T(8,128)(2,1)} collective-permute-done((bf16[2,83,1024]{2,1,0:T(8,128)(2,1)}, bf16[2,83,1024]{2,1,0:T(8,128)(2,1)}, u32[]{:S(2)}, u32[]{:S(2)}) %collective-permute-start.4) | collective-permute-done | bytes 340000 | tf_op jit(solution)/shard_map/ppermute | solution.py:596
  46.4 1.4 collective-permute-done.5.rest_2_
  52.3 1.9 copy-done.34
  54.1 1.9 copy-done.36
  59.0 8.1 %shard_map.183 = (bf16[256,768]{1,0:T(8,128)(2,1)S(1)}, bf16[256,768]{1,0:T(8,128)(2,1)S(1)}, bf16[64,16,640]{2,1,0:T(8,128)(2,1)S(1)}, bf16[64,16,640]{2,1,0:T(8,128)(2,1)S(1)}, bf16[16,128]{1,0:T(8,128)(2,1)S(1)}) custom-call(s32[1]{0:T(128)} %bitcast.core, s32[1]{0:T(128)} %dynamic_slice.3.live_count, bf16[2,83,1024]{2,1,0:T(8,128)(2,1)} %get-tuple-element.50.mine, ...), custom_call_target="tpu_custom_call" | custom-call | flops 6000000000 | bytes 14938632 | tf_op jit(solution)/shard_map/pallas_call | solution.py:35
  67.4 2.7 %shard_map.184 = (bf16[2,256,1152]{2,1,0:T(8,128)(2,1)S(1)}, bf16[2,64,768]{2,1,0:T(8,128)(2,1)S(1)}, bf16[320,1152]{1,0:T(8,128)(2,1)S(1)}) custom-call(s32[1]{0:T(128)} %bitcast.core, bf16[256,2304]{1,0:T(8,128)(2,1)S(1)} %copy-done.20, bf16[64,1536]{1,0:T(8,128)(2,1)S(1)} %copy-done.44, s32[8,128]{1,0:T(8,128)S(1)} %copy-done.31, s32[1,128]{1,0:T(1,128)S(1)} %bitcast.12, ...), custom_call_target="tpu_custom_call" | custom-call | flops 2000000000 | bytes 3887620 | tf_op jit(solution)/shard_map/pallas_call | solution.py:35
  70.8 2.6 %shard_map.185 = (f32[2,768,128]{2,1,0:T(8,128)S(1)}, bf16[2,16,768]{2,1,0:T(8,128)(2,1)S(1)}, bf16[2,16,768]{2,1,0:T(8,128)(2,1)S(1)}, bf16[32,768]{1,0:T(8,128)(2,1)S(1)}) custom-call(bf16[2,128,768]{2,1,0:T(8,128)(2,1)S(1)} %copy-done.22, bf16[2,16,768]{2,1,0:T(8,128)(2,1)S(1)} %copy-done.27, bf16[2,16,768]{2,1,0:T(8,128)(2,1)S(1)} %copy-done.29, ...), custom_call_target="tpu_custom_call" | custom-call | flops 2000000000 | bytes 6832384 | tf_op jit(solution)/shard_map/pallas_call | solution.py:35
  74.3 2.6 %collective-permute-start.8 = (bf16[2,16,768]{2,1,0:T(8,128)(2,1)S(1)}, bf16[2,16,768]{2,1,0:T(8,128)(2,1)S(1)}, u32[]{:S(2)}, u32[]{:S(2)}) collective-permute-start(bf16[2,16,768]{2,1,0:T(8,128)(2,1)S(1)} %get-tuple-element.65), channel_id=1, source_target_pairs={{4,0},{8,4},{12,8},{16,12},{20,16},{24,20},{28,24},{32,28},{36,32}... | collective-permute-start | bytes 147464 | tf_op jit(solution)/shard_map/ppermute | solution.py:574
  76.9 3.4 %collective-permute-start.9 = (bf16[2,16,768]{2,1,0:T(8,128)(2,1)S(1)}, bf16[2,16,768]{2,1,0:T(8,128)(2,1)S(1)}, u32[]{:S(2)}, u32[]{:S(2)}) collective-permute-start(bf16[2,16,768]{2,1,0:T(8,128)(2,1)S(1)} %get-tuple-element.66), channel_id=1, source_target_pairs={{0,4},{4,8},{8,12},{12,16},{16,20},{20,24},{24,28},{28,32},{32,36}... | collective-permute-start | bytes 147464 | tf_op jit(solution)/shard_map/ppermute | solution.py:575
  80.4 2.8 %shard_map.186 = bf16[64,16,1536]{2,1,0:T(8,128)(2,1)S(1)} custom-call(s32[1]{0:T(128)} %bitcast.core, bf16[256,768]{1,0:T(8,128)(2,1)S(1)} %copy-done.3, bf16[64,768]{1,0:T(8,128)(2,1)S(1)} %copy-done.8, bf16[320,768]{1,0:T(8,128)(2,1)S(1)} %collective-permute-done.2.normed_theirs, bf16[2,256,1152]{2,1,0:T(8,128)(2,1)S(1)} %get-tuple-element.57.d_proj, ...), custom_call_target="tpu_custom_call" | custom-call | flops 2000000000 | bytes 8916996 | tf_op jit(solution)/shard_map/pallas_call | solution.py:35
  83.2 2.7 %collective-permute-done.9.from_prev = bf16[2,16,768]{2,1,0:T(8,128)(2,1)S(1)} collective-permute-done((bf16[2,16,768]{2,1,0:T(8,128)(2,1)S(1)}, bf16[2,16,768]{2,1,0:T(8,128)(2,1)S(1)}, u32[]{:S(2)}, u32[]{:S(2)}) %collective-permute-start.9) | collective-permute-done | bytes 49184 | tf_op jit(solution)/shard_map/ppermute | solution.py:575
  85.9 48.1 %all_to_all.10 = bf16[64,16,1536]{2,1,0:T(8,128)(2,1)S(1)} all-to-all(bf16[64,16,1536]{2,1,0:T(8,128)(2,1)S(1)} %shard_map.186), channel_id=1, replica_groups=mesh['space'=32,'zhi'=2,'core'=2] {'space','zhi'}, dimensions={0} | all-to-all | bytes 6291456 | tf_op jit(solution)/shard_map/all_to_all | solution.py:577
  134.8 46.1 %all_to_all.11.half = bf16[64,16,1536]{2,1,0:T(8,128)(2,1)S(1)} all-to-all(bf16[64,16,1536]{2,1,0:T(8,128)(2,1)S(1)} %bitcast.10), channel_id=1, replica_groups=mesh['space'=32,'zhi'=2,'core'=2] {'space','zhi'}, dimensions={0} | all-to-all | bytes 6291456 | tf_op jit(solution)/shard_map/all_to_all | solution.py:583
  184.5 6.3 %shard_map.188 = (f32[768,2304]{1,0:T(8,128)}, f32[768,768]{1,0:T(8,128)}, f32[768,768]{1,0:T(8,128)}, f32[83,768]{1,0:T(8,128)}, f32[32,768]{1,0:T(8,128)S(1)}, /*index=5*/f32[1,1]{1,0:T(1,128)}) custom-call(s32[1]{0:T(128)} %bitcast.core, bf16[64,16,1536]{2,1,0:T(8,128)(2,1)S(1)} %all_to_all.11.half), custom_call_target="tpu_custom_call" | custom-call | bytes 9000000 | tf_op jit(solution)/shard_map/pallas_call | solution.py:448
  190.8 11.2 %shard_map.189 = (f32[768,2304]{1,0:T(8,128)}, f32[768,768]{1,0:T(8,128)}, f32[768,768]{1,0:T(8,128)}, f32[83,768]{1,0:T(8,128)}, f32[32,768]{1,0:T(8,128)}, /*index=5*/f32[1,1]{1,0:T(1,128)}) custom-call(s32[1]{0:T(128)S(6)} %sub.3.core, ...), custom_call_target="tpu_custom_call", output_to_operand_aliasing={{0}: (2, {}), {1}: (3, {}), {2}: (4, {}), {3}: (5, {})} | custom-call | bytes 9000000 | tf_op jit(solution)/shard_map/pallas_call | solution.py:448
  (107 shorter events, 22.7 us)
Async XLA Ops:
  2.3 15.1 %copy-start.24 = (bf16[83,768]{1,0:T(8,128)(2,1)S(1)}, bf16[83,768]{1,0:T(8,128)(2,1)}, u32[]{:S(2)}) copy-start(bf16[83,768]{1,0:T(8,128)(2,1)} %rest_11_.1) | copy-start | bytes 382468
  2.3 15.1 %copy-start.30 = (s32[3,1024]{1,0:T(4,128)S(1)}, s32[3,1024]{1,0:T(4,128)}, u32[]{:S(2)}) copy-start(s32[3,1024]{1,0:T(4,128)} %dec_nodes.1) | copy-start | bytes 36868
  2.3 15.1 %copy-start.31 = (s32[8,128]{1,0:T(8,128)S(1)}, s32[8,128]{1,0:T(8,128)}, u32[]{:S(2)}) copy-start(s32[8,128]{1,0:T(8,128)} %nbr.3) | copy-start | bytes 12292
  2.3 15.2 %copy-start.32 = (s32[128]{0:T(128)S(1)}, s32[128]{0:T(128)}, u32[]{:S(2)}) copy-start(s32[128]{0:T(128)} %param.16) | copy-start | bytes 1540
  2.7 14.7 %collective-permute-start = (bf16[2,16,768]{2,1,0:T(8,128)(2,1)S(1)}, bf16[2,16,768]{2,1,0:T(8,128)(2,1)S(1)}, u32[]{:S(2)}, u32[]{:S(2)}) collective-permute-start(bf16[2,16,768]{2,1,0:T(8,128)(2,1)S(1)} %get-tuple-element.84), channel_id=1, source_target_pairs={{0,4},{4,8},{8,12},{12,16},{16,20},{20,24},{24,28},{28,32},{32,36}... | collective-permute-start | bytes 147464 | tf_op jit(solution)/shard_map/ppermute | solution.py:498
  6.2 11.3 %collective-permute-start.1 = (bf16[2,16,768]{2,1,0:T(8,128)(2,1)S(1)}, bf16[2,16,768]{2,1,0:T(8,128)(2,1)S(1)}, u32[]{:S(2)}, u32[]{:S(2)}) collective-permute-start(bf16[2,16,768]{2,1,0:T(8,128)(2,1)S(1)} %get-tuple-element.83), channel_id=1, source_target_pairs={{4,0},{8,4},{12,8},{16,12},{20,16},{24,20},{28,24},{32,28},{36,32}... | collective-permute-start | bytes 147464 | tf_op jit(solution)/shard_map/ppermute | solution.py:499
  17.4 9.5 %copy-start.19 = (bf16[256,2304]{1,0:T(8,128)(2,1)}, bf16[256,2304]{1,0:T(8,128)(2,1)S(1)}, u32[]{:S(2)}) copy-start(bf16[256,2304]{1,0:T(8,128)(2,1)S(1)} %get-tuple-element.47.proj) | copy-start | bytes 3538948
  17.4 9.5 %copy-start.21 = (bf16[2,128,768]{2,1,0:T(8,128)(2,1)}, bf16[2,128,768]{2,1,0:T(8,128)(2,1)S(1)}, u32[]{:S(2)}) copy-start(bf16[2,128,768]{2,1,0:T(8,128)(2,1)S(1)} %get-tuple-element.46.own) | copy-start | bytes 1179652
  17.4 9.5 %copy-start.26 = (bf16[2,16,768]{2,1,0:T(8,128)(2,1)}, bf16[2,16,768]{2,1,0:T(8,128)(2,1)S(1)}, u32[]{:S(2)}) copy-start(bf16[2,16,768]{2,1,0:T(8,128)(2,1)S(1)} %collective-permute-done.low) | copy-start | bytes 147460
  17.4 9.5 %copy-start.28 = (bf16[2,16,768]{2,1,0:T(8,128)(2,1)}, bf16[2,16,768]{2,1,0:T(8,128)(2,1)S(1)}, u32[]{:S(2)}) copy-start(bf16[2,16,768]{2,1,0:T(8,128)(2,1)S(1)} %collective-permute-done.1.high) | copy-start | bytes 147460
  20.6 25.2 %copy-start.45 = (s32[32]{0:T(128)S(1)}, s32[32]{0:T(128)}, u32[]{:S(2)}) copy-start(s32[32]{0:T(128)} %param.18) | copy-start | bytes 388
  33.8 12.0 %collective-permute-start.4 = (bf16[2,83,1024]{2,1,0:T(8,128)(2,1)}, bf16[2,83,1024]{2,1,0:T(8,128)(2,1)}, u32[]{:S(2)}, u32[]{:S(2)}) collective-permute-start(bf16[2,83,1024]{2,1,0:T(8,128)(2,1)} %get-tuple-element.50.mine), channel_id=1, source_target_pairs={{0,2},{2,0},{1,3},{3,1},{4,6},{6,4},{5,7},{7,5},{8,10},{10,8},{9,1... | collective-permute-start | bytes 1019912 | tf_op jit(solution)/shard_map/ppermute | solution.py:596
  37.6 8.8 %collective-permute-start.3 = (bf16[2,83,1024]{2,1,0:T(8,128)(2,1)}, bf16[2,83,1024]{2,1,0:T(8,128)(2,1)}, u32[]{:S(2)}, u32[]{:S(2)}) collective-permute-start(bf16[2,83,1024]{2,1,0:T(8,128)(2,1)} %get-tuple-element.50.mine), channel_id=1, source_target_pairs={{0,1},{1,0},{2,3},{3,2},{4,5},{5,4},{6,7},{7,6},{8,9},{9,8},{10,11... | collective-permute-start | bytes 1019912 | tf_op jit(solution)/shard_map/ppermute | solution.py:597
  45.8 2.0 collective-permute-start.5
  59.0 8.3 %copy-start.20 = (bf16[256,2304]{1,0:T(8,128)(2,1)S(1)}, bf16[256,2304]{1,0:T(8,128)(2,1)}, u32[]{:S(2)}) copy-start(bf16[256,2304]{1,0:T(8,128)(2,1)} %copy-done.19) | copy-start | bytes 3538948
  59.0 8.3 %copy-start.44 = (bf16[64,1536]{1,0:T(8,128)(2,1)S(1)}, bf16[64,1536]{1,0:T(8,128)(2,1)}, u32[]{:S(2)}) copy-start(bf16[64,1536]{1,0:T(8,128)(2,1)} %copy-done.43) | copy-start | bytes 589828
  67.1 13.3 %collective-permute-start.7 = (bf16[64,16,640]{2,1,0:T(8,128)(2,1)S(1)}, bf16[64,16,640]{2,1,0:T(8,128)(2,1)S(1)}, u32[]{:S(2)}, u32[]{:S(2)}) collective-permute-start(bf16[64,16,640]{2,1,0:T(8,128)(2,1)S(1)} %get-tuple-element.61), channel_id=1, source_target_pairs={{0,1},{1,0},{2,3},{3,2},{4,5},{5,4},{6,7},{7,6},{8,9},{9,8},{10,11... | collective-permute-start | bytes 3932168 | tf_op jit(solution)/shard_map/ppermute | solution.py:541
  67.3 3.5 %copy-start.10 = (f32[32,768]{1,0:T(8,128)S(1)}, f32[32,768]{1,0:T(8,128)}, u32[]{:S(2)}) copy-start(f32[32,768]{1,0:T(8,128)} %w_noise.5) | copy-start | bytes 294916
  70.1 10.3 %collective-permute-start.6 = (bf16[320,1152]{1,0:T(8,128)(2,1)S(1)}, bf16[320,1152]{1,0:T(8,128)(2,1)S(1)}, u32[]{:S(2)}, u32[]{:S(2)}) collective-permute-start(bf16[320,1152]{1,0:T(8,128)(2,1)S(1)} %get-tuple-element.59), channel_id=1, source_target_pairs={{0,1},{1,0},{2,3},{3,2},{4,5},{5,4},{6,7},{7,6},{8,9},{9,8},{10,11... | collective-permute-start | bytes 2211848 | tf_op jit(solution)/shard_map/ppermute | solution.py:553
  70.6 9.8 %collective-permute-start.2 = (bf16[320,768]{1,0:T(8,128)(2,1)S(1)}, bf16[320,768]{1,0:T(8,128)(2,1)S(1)}, u32[]{:S(2)}, u32[]{:S(2)}) collective-permute-start(bf16[320,768]{1,0:T(8,128)(2,1)S(1)} %pad_maximum_fusion), channel_id=1, source_target_pairs={{0,1},{1,0},{2,3},{3,2},{4,5},{5,4},{6,7},{7,6},{8,9},{9,8},{10,11... | collective-permute-start | bytes 1474568 | tf_op jit(solution)/shard_map/ppermute | solution.py:523
  74.3 8.9 %collective-permute-start.8 = (bf16[2,16,768]{2,1,0:T(8,128)(2,1)S(1)}, bf16[2,16,768]{2,1,0:T(8,128)(2,1)S(1)}, u32[]{:S(2)}, u32[]{:S(2)}) collective-permute-start(bf16[2,16,768]{2,1,0:T(8,128)(2,1)S(1)} %get-tuple-element.65), channel_id=1, source_target_pairs={{4,0},{8,4},{12,8},{16,12},{20,16},{24,20},{28,24},{32,28},{36,32}... | collective-permute-start | bytes 147464 | tf_op jit(solution)/shard_map/ppermute | solution.py:574
  76.9 9.0 %collective-permute-start.9 = (bf16[2,16,768]{2,1,0:T(8,128)(2,1)S(1)}, bf16[2,16,768]{2,1,0:T(8,128)(2,1)S(1)}, u32[]{:S(2)}, u32[]{:S(2)}) collective-permute-start(bf16[2,16,768]{2,1,0:T(8,128)(2,1)S(1)} %get-tuple-element.66), channel_id=1, source_target_pairs={{0,4},{4,8},{8,12},{12,16},{16,20},{20,24},{24,28},{28,32},{32,36}... | collective-permute-start | bytes 147464 | tf_op jit(solution)/shard_map/ppermute | solution.py:575
  134.7 47.4 %copy-start.12 = (s32[2,16]{1,0:T(2,128)S(1)}, s32[2,16]{1,0:T(2,128)}, u32[]{:S(2)}) copy-start(s32[2,16]{1,0:T(2,128)} %rows.3) | copy-start | bytes 388
  180.8 10.0 %collective-permute-start.10 = (bf16[64,16,1536]{2,1,0:T(8,128)(2,1)S(1)}, bf16[64,16,1536]{2,1,0:T(8,128)(2,1)}, u32[]{:S(2)}, u32[]{:S(2)}) collective-permute-start(bf16[64,16,1536]{2,1,0:T(8,128)(2,1)S(1)} %all_to_all.11.half), channel_id=1, source_target_pairs={{0,1},{1,0},{2,3},{3,2},{4,5},{5,4},{6,7},{7,6},{8,9},{9,8},{10,11... | collective-permute-start | bytes 9437192 | tf_op jit(solution)/shard_map/ppermute | solution.py:584
  (33 other events, 51.7 us)

commit v3 on v2

--- a/solution.py
+++ b/solution.py
@@ -9,7 +9,8 @@
 HEAD = 128
 TILE = 128
 GROUPS = 16
-BLOCKS = 4
+SPACE = ("x", "zlo", "y")
+HALF = 768
 SLOTS_A = 5
 SLOTS_B = 7
 CHUNKS = 4 * GROUPS
@@ -62,7 +63,11 @@
     return inverse * (d_hat - mean - hat * along)
 
 
-def send_body(latent, rows, sent):
+def depth_here():
+    return 2 * lax.axis_index("zhi") + lax.axis_index("zlo")
+
+
+def send_body(latent, rows, sent_up, sent_down):
     nodes = latent.shape[2]
     rim = rows.shape[1]
     both = jnp.concatenate([rows[0:1, :], rows[1:2, :]], axis=1)
@@ -70,8 +75,8 @@
     table = table.astype(F32).T.astype(BF16)
     for m in range(latent.shape[0]):
         picked = mm(table, latent[m], NT).astype(BF16)
-        sent[0, m] = picked[:rim]
-        sent[1, m] = picked[rim:]
+        sent_up[m] = picked[:rim]
+        sent_down[m] = picked[rim:]
 
 
 def local_body(latent, noise, w_noise, w_qkv, own, normed, proj):
@@ -109,8 +114,9 @@
 
 
 def forward_body(
-    own, proj, low, high, noise, w_noise, w_qkv, w_out, w_hid, w_pred, nbr, degree, dec_nodes,
-    normed_rim, proj_rim, attended, stored, hidden, slope, forecast, table,
+    own, normed, proj, low, high, noise, w_noise, w_qkv, w_out, w_hid, w_pred, nbr, degree,
+    dec_nodes,
+    normed_all, proj_rim, attended, stored, hidden, slope, forecast, table,
 ):
     members, nodes, width = own.shape
     rim = low.shape[1]
@@ -118,8 +124,10 @@
     for m in range(members):
         rows = jnp.concatenate([low[m], high[m]], axis=0).astype(F32)
         hat, _ = normalise(rows)
-        normed_rim[2 * rim * m : 2 * rim * (m + 1)] = (hat * gain[m : m + 1]).astype(BF16)
-    proj_rim[...] = mm(normed_rim[...], w_qkv[:, width:]).astype(BF16)
+        at = members * nodes + 2 * rim * m
+        normed_all[at : at + 2 * rim] = (hat * gain[m : m + 1]).astype(BF16)
+    normed_all[: members * nodes] = normed[...]
+    proj_rim[...] = mm(normed_all[members * nodes :], w_qkv[:, width:]).astype(BF16)
     mask = slot_mask(nbr, degree, nodes + 2 * rim)
     for m in range(members):
         here = slice(m * nodes, (m + 1) * nodes)
@@ -160,10 +168,12 @@
 
 
 def crps_body(
-    core, live_count, mine, *rest
+    counts, mine, *rest
 ):
     (*others, targets, hidden, slope, table, stored, attended, w_out, w_hid, w_pred,
      d_updated, d_attended, keep, send, loss, d_pre, d_cast, halves) = rest
+    live_count = counts[lax.axis_index(SPACE)]
+    core = lax.axis_index("core")
     members, channels, points = mine.shape
     total = members * (1 + len(others))
     block = 256
@@ -172,7 +182,7 @@
     losses = []
     for g in range(0, points, block):
         at = slice(g, g + block)
-        live = lax.broadcasted_iota(jnp.int32, (1, block), 1) + g < live_count[0]
+        live = lax.broadcasted_iota(jnp.int32, (1, block), 1) + g < live_count
         live = live.astype(F32)
         own = [mine[m, :, at].astype(F32) for m in range(members)]
         aim = targets[:, at]
@@ -235,8 +245,8 @@
                     column = c * half + TILE * column
                     piece = grad[16 * row : 16 * row + 16, column : column + TILE]
                 halves[c, chunk, :, lane : lane + TILE] = piece
-    keep[...] = halves[core[0]]
-    send[...] = halves[1 - core[0]]
+    keep[...] = halves[core]
+    send[...] = halves[1 - core]
 
 
 def tile_of_first(k, slot, grads):
@@ -250,7 +260,7 @@
 
 
 def attend_back_body(
-    core, proj, proj_rim, nbr, degree, d_attended,
+    proj, proj_rim, nbr, degree, d_attended,
     d_proj, d_rim, send, mask,
 ):
     nodes = nbr.shape[1]
@@ -285,8 +295,9 @@
                 d_proj[c, here, spot[k]] = d[rim : rim + nodes]
                 d_rim[c, hi, spot[k - 1]] = d[rim + nodes :]
     rows = members * nodes
-    send[:rows] = d_proj[1 - core[0]]
-    send[rows:, : 2 * part] = d_rim[1 - core[0]]
+    theirs = 1 - lax.axis_index("core")
+    send[:rows] = d_proj[theirs]
+    send[rows:, : 2 * part] = d_rim[theirs]
     send[rows:, 2 * part :] = jnp.zeros((2 * rim * members, part), BF16)
 
 
@@ -329,143 +340,206 @@
 
 
 def pack_body(
-    core, normed, normed_rim, normed_theirs, d_proj, d_rim, d_theirs, keep, came, g_noise, loss,
-    packed, g_half,
+    normed, normed_theirs, d_proj, d_rim, d_theirs, keep, came, g_noise, loss, plane, *rest
 ):
-    rows = normed.shape[0]
+    *stacks, g_half, stack = rest
+    core, depth = lax.axis_index("core"), depth_here()
+    rows = d_proj.shape[1]
     wide = 2 * d_proj.shape[2] // 3
     width = normed.shape[1]
-    mine = d_proj[core[0]]
-    rim = d_rim[core[0]]
+    mine = d_proj[core]
+    rim = d_rim[core]
     for r in range(0, width, 256):
         at = slice(r, r + 256)
-        total = mm(normed[:, at], mine, TN) + mm(normed_theirs[:rows, at], d_theirs[:rows], TN)
+        total = mm(normed[:rows, at], mine, TN) + mm(normed_theirs[:rows, at], d_theirs[:rows], TN)
         g_half[at, : wide // 2] = total[:, : wide // 2].astype(BF16)
-        edge = mm(normed_rim[:, at], rim, TN)
+        edge = mm(normed[rows:, at], rim, TN)
         edge = edge + mm(normed_theirs[rows:, at], d_theirs[rows:, :wide], TN)
         g_half[at, wide // 2 :] = (total[:, wide // 2 :] + edge).astype(BF16)
-    first = TILE * SLOTS_A
-    packed[:, :, :first] = (keep[...].astype(F32) + came[...].astype(F32)).astype(BF16)
     for k in range(GROUPS):
-        for slot in range(SLOTS_B * 4):
-            chunk, lane = 4 * k + slot // SLOTS_B, first + TILE * (slot % SLOTS_B)
-            if slot < 27:
-                row, column = 48 * k + 16 * (slot // 9), TILE * (slot % 9)
-                piece = g_half[row : row + 16, column : column + TILE]
-            elif k < 12:
-                row, column = 16 * (k // 6), TILE * (k % 6)
-                piece = g_noise[row : row + 16, column : column + TILE]
-            elif k == 12:
-                piece = loss[...]
-            else:
-                piece = jnp.zeros((16, TILE), BF16)
-            packed[chunk, :, lane : lane + TILE] = piece
-
-
-def sum_body(came, spread):
-    chips, chunks = came.shape[0], came.shape[1]
-    for j in range(chunks):
+        for sub in range(4):
+            level, spot = k // 4, 4 * (k % 4) + sub
+            first = keep[4 * k + sub].astype(F32) + came[4 * k + sub].astype(F32)
+            plane[spot, level, :, : TILE * SLOTS_A] = first.astype(BF16)
+            for j in range(SLOTS_B):
+                slot = SLOTS_B * sub + j
+                if slot < 27:
+                    row, column = 48 * k + 16 * (slot // 9), TILE * (slot % 9)
+                    piece = g_half[row : row + 16, column : column + TILE]
+                elif k < 12:
+                    row, column = 16 * (k // 6), TILE * (k % 6)
+                    piece = g_noise[row : row + 16, column : column + TILE]
+                elif k == 12:
+                    piece = loss[...]
+                else:
+                    piece = jnp.zeros((16, TILE), BF16)
+                lane = TILE * (SLOTS_A + j)
+                if lane < HALF:
+                    plane[spot, level, :, lane : lane + TILE] = piece
+                else:
+                    stack[level, spot, :, lane - HALF : lane - HALF + TILE] = piece
+    for shift in range(4):
+        stacks[shift][...] = stack[lax.rem(depth + shift, 4)]
+
+
+def first_sum_body(came, *rest):
+    depth = depth_here()
+    stacks, targets, (stack, column) = rest[:4], rest[4:8], rest[8:]
+    for j in range(came.shape[1]):
         total = came[0, j].astype(F32)
-        for i in range(1, chips):
+        for i in range(1, came.shape[0]):
             total = total + came[i, j].astype(F32)
-        total = total.astype(BF16)
-        for i in range(chips):
+        column[:, j] = total.astype(BF16)
+    for shift, target in enumerate(targets):
+        target[...] = column[lax.rem(depth + shift, 4)]
+    total = stacks[0][...].astype(F32)
+    for part in stacks[1:]:
+        total = total + part[...].astype(F32)
+    stack[...] = total.astype(BF16)
+
+
+def second_sum_body(one, two, three, four, came, column, spread):
+    total = one[...].astype(F32) + two[...].astype(F32)
+    total = total + three[...].astype(F32) + four[...].astype(F32)
+    column[...] = total.astype(BF16)
+    total = came[0].astype(F32)
+    for i in range(1, came.shape[0]):
+        total = total + came[i].astype(F32)
+    total = total.astype(BF16)
+    for i in range(came.shape[0]):
+        spread[i] = total
+
+
+def spread_body(one, two, three, four, spread, column):
+    depth = depth_here()
+    for shift, piece in enumerate((one, two, three, four)):
+        column[lax.rem(depth + (4 - shift), 4)] = piece[...]
+    for j in range(spread.shape[1]):
+        total = column[:, j]
+        for i in range(spread.shape[0]):
             spread[i, j] = total
 
 
-def unpack_body(
-    core, half, *rest
-):
-    (g_qkv, g_out, g_hid, g_pred, g_noise, loss, pred_rows) = rest[-7:]
-    before = rest[:-7]
-    r, section = pl.program_id(0), pl.program_id(1)
-    per_block = GROUPS // BLOCKS
-
-    def tile(group, slot, first=0, size=SLOTS_A):
-        lane = first + TILE * (slot % size)
-        return half[4 * group + slot // size, :, lane : lane + TILE].astype(F32)
-
-    for group in range(per_block):
-        for row in range(3):
-            at = slice(48 * group + 16 * row, 48 * group + 16 * row + 16)
-            for s in range(3):
-
-                @pl.when(section == s)
-                def _(group=group, row=row, at=at, s=s):
-                    for j in range(3):
-                        g_qkv[at, TILE * j : TILE * (j + 1)] = tile(
-                            group, 9 * row + 3 * s + j, TILE * SLOTS_A, SLOTS_B
-                        )
-
-    @pl.when(section == 0)
-    def _():
-        for group in range(per_block):
+def unpack_tiles(core, plane, stacks, targets, pred, noise, halves, sems):
+    wide = halves[1].shape[1]
+    depth = depth_here()
+    copies = []
+    total = None
+    for step in range(4):
+        level = lax.rem(depth + 4 - step, 4)
+        here = plane.at[:, level]
+
+        def tile(group, sub, j):
+            lane, spot = TILE * j, 4 * group + sub
+            if lane < HALF:
+                return here[spot, :, lane : lane + TILE].astype(F32)
+            return stacks[step][spot, :, lane - HALF : lane - HALF + TILE].astype(F32)
+
+        def first(group, slot):
+            return tile(group, slot // SLOTS_A, slot % SLOTS_A)
+
+        def second(group, slot):
+            return tile(group, slot // SLOTS_B, SLOTS_A + slot % SLOTS_B)
+
+        base = 192 * step
+        for group in range(4):
+            for slot in range(27):
+                row, column = base + 48 * group + 16 * (slot // 9), TILE * (slot % 9)
+                halves[0][row : row + 16, column : column + TILE] = second(group, slot)
             for slot in range(18):
-                target = (g_hid, g_out)[slot // 9]
-                row, column = 48 * group + 16 * (slot % 9 // 3), TILE * (slot % 3)
-                target[row : row + 16, column : column + TILE] = tile(group, slot)
-            k = per_block * r + group
+                row, column = base + 48 * group + 16 * (slot % 9 // 3), TILE * (slot % 3)
+                halves[1 + slot // 9][row : row + 16, column : column + TILE] = first(group, slot)
+            k = 4 * level + group
             for slot in (18, 19):
                 index = k + GROUPS * (slot - 18)
 
                 @pl.when(index < 18)
-                def _(slot=slot, index=index, group=group):
-                    row = pl.multiple_of(16 * (index // 3), 16)
-                    column = pl.multiple_of(TILE * (index % 3), TILE)
-                    pred_rows[pl.ds(row, 16), pl.ds(column, TILE)] = tile(group, slot)
-
-            spare = tile(group, 27, TILE * SLOTS_A, SLOTS_B)
+                def _():
+                    row = pl.multiple_of(16 * lax.div(index, 3), 16)
+                    column = pl.multiple_of(TILE * lax.rem(index, 3), TILE)
+                    pred[pl.ds(row, 16), pl.ds(column, TILE)] = first(group, slot)
+
+            spare = second(group, 27)
 
             @pl.when(k < 12)
-            def _(k=k, spare=spare):
-                row = pl.multiple_of(16 * (k // 6), 16)
-                column = pl.multiple_of(TILE * (k % 6), TILE)
-                here = (pl.ds(row, 16), pl.ds(column, TILE))
-                g_noise[here] = spare + before[-2][here] if before else spare
-
-            @pl.when(k == 12)
-            def _(spare=spare):
-                total = jnp.sum(spare, keepdims=True)
-                loss[...] = total + before[-1][...] if before else total
-
-        @pl.when(r == BLOCKS - 1)
-        def _():
-            g_pred[...] = pred_rows[: g_pred.shape[0]]
-
-
-def unpack(which, half, width, channels, before=()):
+            def _():
+                row = pl.multiple_of(16 * lax.div(k, 6), 16)
+                column = pl.multiple_of(TILE * lax.rem(k, 6), TILE)
+                noise[pl.ds(row, 16), pl.ds(column, TILE)] = spare
+
+            here_loss = jnp.where(k == 12, spare, 0.0)
+            total = here_loss if total is None else total + here_loss
+        rows = pl.ds(pl.multiple_of(192 * level, 16), 192)
+        for target, half, sections in ((0, 0, 3), (1, 1, 1), (2, 2, 1)):
+            for section in range(sections):
+                start = pl.multiple_of(2 * wide * section + wide * core, TILE)
+                copies.append(
+                    pltpu.make_async_copy(
+                        halves[half].at[base : base + 192, wide * section : wide * (section + 1)],
+                        targets[target].at[rows, pl.ds(start, wide)],
+                        sems.at[len(copies)],
+                    )
+                )
+                copies[-1].start()
+    return copies, jnp.sum(total, keepdims=True)
+
+
+def unpack_mine_body(
+    plane, one, two, three, four, g_qkv, g_hid, g_out, pred, noise, loss, *scratch
+):
+    *halves, sems = scratch
+    copies, total = unpack_tiles(
+        lax.axis_index("core"), plane, (one, two, three, four), (g_qkv, g_hid, g_out), pred, noise,
+        halves, sems,
+    )
+    loss[...] = total
+    for copy in copies:
+        copy.wait()
+
+
+def unpack_theirs_body(
+    plane, one, two, three, four, counts, _qkv, _hid, _out, pred_mine, noise_mine, loss_mine,
+    g_qkv, g_hid, g_out, g_pred, noise, mean, *scratch
+):
+    *halves, pred, sems = scratch
+    mine = lax.axis_index("core")
+    copies, total = unpack_tiles(
+        1 - mine, plane, (one, two, three, four), (g_qkv, g_hid, g_out), pred, noise, halves, sems
+    )
+    noise[...] = noise[...] + noise_mine[...]
+    channels, width = g_pred.shape
     wide = width // 2
-    rows = width // BLOCKS
-    const = lambda r, s, c: (0, 0)
-    spec = lambda shape, at: pl.BlockSpec(shape, at)
-    in_specs = [spec((CHUNKS // BLOCKS,) + half.shape[1:], lambda r, s, c: (r, 0, 0))]
+    for c in range(2):
+        own = pred_mine[:channels]
+        g_pred[:, c * wide : (c + 1) * wide] = jnp.where(mine == c, own, pred[:channels])
+    live = jnp.sum(counts[...].astype(F32), keepdims=True)
+    mean[...] = (total + loss_mine[...]) / (channels * live)
+    for copy in copies:
+        copy.wait()
+
+
+def unpack(plane, stacks, width, channels, counts=None, before=()):
+    wide = width // 2
+    big = ((width, 3 * width), (width, width), (width, width))
+    small = ((channels, width) if before else (96, wide), (32, width), (1, 1))
+    scratch = [pltpu.VMEM((width, n), F32) for n in (3 * wide, wide, wide)]
     if before:
-        in_specs += [pl.BlockSpec(memory_space=pl.ANY)] * 4
-        in_specs += [spec((32, width), const), spec((1, 1), const)]
-    shapes = (
-        (width, 3 * width), (width, width), (width, width), (channels, width), (32, width), (1, 1),
-    )
+        scratch.append(pltpu.VMEM((96, wide), F32))
+    scratch.append(pltpu.SemaphoreType.DMA((20,)))
+    anywhere = pl.BlockSpec(memory_space=pl.ANY)
+    args = (plane, *stacks)
+    if before:
+        args += (counts, *before)
     return pl.pallas_call(
-        unpack_body,
-        grid_spec=pltpu.PrefetchScalarGridSpec(
-            num_scalar_prefetch=1,
-            grid=(BLOCKS, 3),
-            in_specs=in_specs,
-            out_specs=[
-                spec((rows, wide), lambda r, s, c: (r, 2 * s + c[0])),
-                spec((rows, wide), lambda r, s, c: (r, c[0])),
-                spec((rows, wide), lambda r, s, c: (r, c[0])),
-                spec((channels, wide), lambda r, s, c: (0, c[0])),
-                spec((32, width), const),
-                spec((1, 1), const),
-            ],
-            scratch_shapes=[pltpu.VMEM((96, wide), F32)],
-        ),
-        out_shape=[jax.ShapeDtypeStruct(shape, F32) for shape in shapes],
-        input_output_aliases={2 + i: i for i in range(4)} if before else {},
-        compiler_params=pltpu.CompilerParams(vmem_limit_bytes=16 * MIB),
+        unpack_theirs_body if before else unpack_mine_body,
+        out_shape=[jax.ShapeDtypeStruct(shape, F32) for shape in big + small],
+        in_specs=[anywhere if 6 <= i < 9 else VMEM for i in range(len(args))],
+        out_specs=[anywhere] * 3 + [VMEM] * 3,
+        scratch_shapes=scratch,
+        input_output_aliases={6 + i: i for i in range(3)} if before else {},
+        compiler_params=pltpu.CompilerParams(vmem_limit_bytes=20 * MIB),
         cost_estimate=pl.CostEstimate(flops=0, bytes_accessed=9 * 10**6, transcendentals=0),
-    )(which, half, *before)
+    )(*args)
 
 
 def join_body(d_own, rows, from_next, from_prev, d_latent):
@@ -490,47 +564,47 @@
     rows = members * nodes
     rims = members * 2 * rim
     degree = degree[None, :]
-    size = lax.axis_size("space")
+    size = lax.axis_size(SPACE)
     up = [(i, i + 1) for i in range(size - 1)]
     down = [(i + 1, i) for i in range(size - 1)]
 
-    (sent,) = call(send_body, [((2, members, rim, width), BF16)], latent, send_rows)
-    low = lax.ppermute(sent[0], "space", up)
-    high = lax.ppermute(sent[1], "space", down)
+    sent_up, sent_down = call(
+        send_body, [((members, rim, width), BF16)] * 2, latent, send_rows
+    )
+    low = lax.ppermute(sent_up, SPACE, up)
+    high = lax.ppermute(sent_down, SPACE, down)
     own, normed, proj = call(
         local_body,
         [((members, nodes, width), BF16), ((rows, width), BF16), ((rows, 3 * width), BF16)],
         latent, member_noise, w_noise, w_qkv,
         flops=2 * rows * width * 3 * width,
     )
-    normed_rim, proj_rim, attended, stored, hidden, slope, forecast, table = call(
+    normed_all, proj_rim, attended, stored, hidden, slope, forecast, table = call(
         forward_body,
         [
-            ((rims, width), BF16), ((rims, 2 * width), BF16), ((rows, width), BF16),
+            ((rows + rims, width), BF16), ((rims, 2 * width), BF16), ((rows, width), BF16),
             ((rows, width), BF16), ((members, width, points), BF16),
             ((members, width, points), BF16), ((members, channels, points), BF16),
             ((nodes, points), BF16),
         ],
-        own, proj, low, high, member_noise, w_noise, w_qkv, w_out, w_hid, w_pred,
+        own, normed, proj, low, high, member_noise, w_noise, w_qkv, w_out, w_hid, w_pred,
         neighbours, degree, dec_nodes,
         flops=3 * 10**9,
     )
     gathered = gather_members(forecast)
     packed_shape = (CHUNKS, 16, TILE * (SLOTS_A + SLOTS_B))
     first_shape = (CHUNKS, 16, TILE * SLOTS_A)
-    core = lax.axis_index("core").astype(jnp.int32)[None]
     swap = [(0, 1), (1, 0)]
-    normed_theirs = lax.ppermute(jnp.concatenate([normed, normed_rim], axis=0), "core", swap)
-    live_count = lax.dynamic_slice_in_dim(counts, lax.axis_index("space"), 1)
+    normed_theirs = lax.ppermute(normed_all, "core", swap)
     d_updated, d_attended, keep, send, loss = call(
         crps_body,
         [
             ((rows, width), BF16), ((rows, width), BF16), (first_shape, BF16),
             (first_shape, BF16), ((16, TILE), BF16),
         ],
-        core, live_count, forecast, *gathered, targets, hidden, slope, table, stored, attended,
+        counts, forecast, *gathered, targets, hidden, slope, table, stored, attended,
         w_out, w_hid, w_pred,
-        smem=(0, 1),
+        smem=(0,),
         scratch=[
             pltpu.VMEM((members, width, points), BF16),
             pltpu.VMEM((members, channels, points), BF16),
@@ -545,8 +619,7 @@
             ((2, rows, 3 * width // 2), BF16), ((2, rims, width), BF16),
             ((rows + rims, 3 * width // 2), BF16),
         ],
-        core, proj, proj_rim, neighbours, degree, d_attended,
-        smem=(0,),
+        proj, proj_rim, neighbours, degree, d_attended,
         scratch=[pltpu.VMEM((nodes + 2 * rim, nodes), F32)],
         flops=2 * 10**9,
     )
@@ -560,35 +633,67 @@
         own, low, high, member_noise, w_noise, w_qkv, d_proj, d_rim, d_updated,
         flops=2 * 10**9,
     )
-    (packed,) = call(
+    planes, levels = ("x", "y"), ("zlo", "zhi")
+    spots = lax.axis_size(planes)
+    tile = (16, HALF)
+    chunk = (16 // spots,) + tile
+    ring = [2 * (z % 2) + z // 2 for z in range(4)]
+
+    def shifted(pieces):
+        moved = []
+        for shift, piece in enumerate(pieces, 1):
+            pairs = [(ring[z], ring[(z + shift) % 4]) for z in range(4)]
+            moved.append(lax.ppermute(piece, levels, pairs))
+        return moved
+
+    def swapped(a):
+        return lax.all_to_all(a, planes, 0, 0, tiled=True)
+
+    plane, *stacks = call(
         pack_body,
-        [(packed_shape, BF16)],
-        core, normed, normed_rim, normed_theirs, d_proj, d_rim, d_theirs, keep, came, g_noise,
-        loss,
-        smem=(0,),
-        scratch=[pltpu.VMEM((width, 3 * width // 2), BF16)],
+        [((16, 4) + tile, BF16)] + [((16,) + tile, BF16)] * 4,
+        normed_all, normed_theirs, d_proj, d_rim, d_theirs, keep, came, g_noise, loss,
+        scratch=[
+            pltpu.VMEM((width, 3 * width // 2), BF16), pltpu.VMEM((4, 16) + tile, BF16),
+        ],
         flops=2 * 10**9,
     )
-    chips = ("space", "zhi")
-    count = lax.axis_size(chips)
-    from_next = lax.ppermute(d_low, "space", down)
-    from_prev = lax.ppermute(d_high, "space", up)
-    packed, from_next, from_prev = lax.optimization_barrier((packed, from_next, from_prev))
-    parts = lax.all_to_all(packed, chips, 0, 0, tiled=True)
-    (spread,) = call(
-        sum_body,
-        [((count, CHUNKS // count) + packed_shape[1:], BF16)],
-        parts.reshape((count, CHUNKS // count) + packed_shape[1:]),
-    )
-    half = lax.all_to_all(spread.reshape(packed_shape), chips, 0, 0, tiled=True)
-    other = lax.ppermute(half, "core", swap)
+    from_next = lax.ppermute(d_low, SPACE, down)
+    from_prev = lax.ppermute(d_high, SPACE, up)
+    plane, from_next, from_prev = lax.optimization_barrier((plane, from_next, from_prev))
+    stacks = [stacks[0]] + shifted(stacks[1:])
+    plane = swapped(plane)
+    *columns, stack = call(
+        first_sum_body,
+        [(chunk, BF16)] * 4 + [((16,) + tile, BF16)],
+        plane.reshape((spots, 16 // spots, 4) + tile), *stacks,
+        scratch=[pltpu.VMEM((4,) + chunk, BF16)],
+    )
+    columns = [columns[0]] + shifted(columns[1:])
+    stack = swapped(stack)
+    column, stack = call(
+        second_sum_body,
+        [(chunk, BF16), ((spots,) + chunk, BF16)],
+        *columns, stack.reshape((spots,) + chunk),
+    )
+    columns = [column] + shifted([column] * 3)
+    stack = swapped(stack.reshape((16,) + tile))
+    (plane,) = call(
+        spread_body, [((spots, 16 // spots, 4) + tile, BF16)], *columns,
+        scratch=[pltpu.VMEM((4,) + chunk, BF16)],
+    )
+    stacks = [stack] + shifted([stack] * 3)
+    plane = swapped(plane.reshape((16, 4) + tile))
+    other_stacks = [lax.ppermute(a, "core", swap) for a in stacks]
+    other_plane = lax.ppermute(plane, "core", swap)
     (d_latent,) = call(
         join_body, [((members, width, nodes), F32)], d_own, send_rows, from_next, from_prev
     )
-    mine = unpack(core, half, width, channels)
-    g_qkv, g_out, g_hid, g_pred, g_noise, loss = unpack(1 - core, other, width, channels, mine)
-    mean = loss[0, 0] / (channels * jnp.sum(counts).astype(F32))
-    return mean, d_latent, g_qkv, g_out, g_noise, g_hid, g_pred
+    mine = unpack(plane, stacks, width, channels)
+    g_qkv, g_hid, g_out, g_pred, g_noise, mean = unpack(
+        other_plane, other_stacks, width, channels, counts[None, :], mine
+    )
+    return mean.reshape(()), d_latent, g_qkv, g_out, g_noise, g_hid, g_pred
 
 
 def gather_members(forecast):
@@ -599,14 +704,15 @@
 
 
 def solution(mesh):
-    space = mesh.shape["space"]
-    mesh = jax.sharding.Mesh(mesh.devices.reshape(space, 2, 2), ("space", "zhi", "core"))
-    member = ("zhi", "core")
+    axes = ("x", "zlo", "y", "zhi", "core")
+    side = 4 if mesh.shape["space"] == 32 else 1
+    mesh = jax.sharding.Mesh(mesh.devices.reshape(side, 2, side, 2, 2), axes)
+    member, space = ("zhi", "core"), SPACE
     in_specs = (
-        P(member, None, "space"), P(None, "space"), P(None, "space"), P("space"),
-        P(None, "space"), P(), P(None, "space"), P(member, None), P(), P(), P(), P(), P(),
-    )
-    out_specs = (P(), P(member, None, "space"), P(), P(), P(), P(), P())
+        P(member, None, space), P(None, space), P(None, space), P(space),
+        P(None, space), P(), P(None, space), P(member, None), P(), P(), P(), P(), P(),
+    )
+    out_specs = (P(), P(member, None, space), P(), P(), P(), P(), P())
     return jax.shard_map(
         on_device, mesh=mesh, in_specs=in_specs, out_specs=out_specs, check_vma=False
     )

time: 207 us -> 194 us (0.937)
  blocking collectives: 94.2 us -> 37.6 us
  waiting for transfers between devices: 12.3 us -> 52.2 us
  starting transfers between devices: 19.7 us -> 49.7 us
  local copies, waits for them, and re-layouts: 29.7 us -> 16.6 us
  Pallas kernels: 43.8 us -> 33.2 us
  between operations: 3.44 us -> 1.14 us
    all_to_all x2, blocking collectives: 94.2 us -> 37.6 us  [swapped(): return lax.all_to_all(a, planes, 0, 0, tiled=True)]
    ppermute x6 -> x22, waiting for transfers between devices: 2.75 us -> 42.7 us  [the longest x12 42.7 us: shifted(): moved.append(lax.ppermute(piece, levels, pairs))]
    ppermute x6 -> x22, starting transfers between devices: 15.1 us -> 31.5 us  [the longest x12 16.4 us: shifted(): moved.append(lax.ppermute(piece, levels, pairs))]
    all_to_all x0 -> x2, starting transfers between devices: none -> 13.6 us  [swapped(): return lax.all_to_all(a, planes, 0, 0, tiled=True)]
    unnamed x92 -> x66, local copies, waits for them, and re-layouts: 29.1 us -> 16.6 us
    pallas_call x2, Pallas kernels: 17.5 us -> 7.62 us  [unpack(): pl.pallas_call(unpack_theirs_body if before else unpack_mine_body, out_sh...]
    pallas_call x9 -> x11, Pallas kernels: 26.3 us -> 25.6 us  [call(): pl.pallas_call(body, out_shape=out_shape, in_specs=[SMEM if i in smem els...]
  transfers between devices with their start and end apart: 11 -> 29, of which waited for: 3 -> 13; matrix products, arithmetic and copies ran while one was open for 1% -> 0% of each run, Pallas kernels for 8% -> 8%
where the time goes in v3:
time: 194 us; the launch traced here: 190 us
  waiting for transfers between devices  52.2 us (27%)
  starting transfers between devices  49.7 us (26%)
  blocking collectives  37.6 us (19%)
  Pallas kernels  33.2 us (17%)
  local copies, waits for them, and re-layouts  16.6 us (9%)
    ppermute x12, waiting for transfers between devices, shifted(): moved.append(lax.ppermute(piece, levels, pairs))  42.7 us
    all_to_all x2, blocking collectives, swapped(): return lax.all_to_all(a, planes, 0, 0, tiled=True)  37.6 us
    pallas_call x11, Pallas kernels, call(): pl.pallas_call(body, out_shape=out_shape, in_specs=[SMEM if i in smem els...  25.6 us
    unnamed x66, local copies, waits for them, and re-layouts  16.6 us
    ppermute x12, starting transfers between devices, shifted(): moved.append(lax.ppermute(piece, levels, pairs))  16.4 us
    all_to_all x2, starting transfers between devices, swapped(): return lax.all_to_all(a, planes, 0, 0, tiled=True)  13.6 us
    ppermute x1, waiting for transfers between devices, gather_members(): far = lax.ppermute(forecast, 'zhi', swap)  7.85 us
    pallas_call x2, Pallas kernels, unpack(): pl.pallas_call(unpack_theirs_body if before else unpack_mine_body, out_sh...  7.62 us
  transfers between devices with their start and end apart: 29, of which 13 were waited for; matrix products, arithmetic and copies ran while one was open for 0% of the time, Pallas kernels for 8%

profile of v3, /device:TPU:2, one launch (start us, length us, event | category | flops | bytes accessed | tf_op | source)
XLA Modules:
  0.0 190.5 jit_solution(18152901398660553609)
XLA Ops:
  2.6 3.5 %collective-permute-start = (bf16[2,16,768]{2,1,0:T(8,128)(2,1)S(1)}, bf16[2,16,768]{2,1,0:T(8,128)(2,1)S(1)}, u32[]{:S(2)}, u32[]{:S(2)}) collective-permute-start(bf16[2,16,768]{2,1,0:T(8,128)(2,1)S(1)} %get-tuple-element.62), channel_id=1, source_target_pairs={{0,4},{4,8},{8,12},{12,16},{16,20},{20,24},{24,28},{28,32},{32,36}... | collective-permute-start | bytes 147464 | tf_op jit(solution)/shard_map/ppermute | solution.py:574
  6.1 5.4 %collective-permute-start.1 = (bf16[2,16,768]{2,1,0:T(8,128)(2,1)S(1)}, bf16[2,16,768]{2,1,0:T(8,128)(2,1)S(1)}, u32[]{:S(2)}, u32[]{:S(2)}) collective-permute-start(bf16[2,16,768]{2,1,0:T(8,128)(2,1)S(1)} %get-tuple-element.63), channel_id=1, source_target_pairs={{4,0},{8,4},{12,8},{16,12},{20,16},{24,20},{28,24},{32,28},{36,32}... | collective-permute-start | bytes 147464 | tf_op jit(solution)/shard_map/ppermute | solution.py:575
  19.7 5.6 %shard_map.182 = (bf16[320,768]{1,0:T(8,128)(2,1)S(1)}, bf16[64,1536]{1,0:T(8,128)(2,1)S(1)}, bf16[256,768]{1,0:T(8,128)(2,1)S(1)}, bf16[256,768]{1,0:T(8,128)(2...) custom-call(bf16[2,128,768]{2,1,0:T(8,128)(2,1)S(1)} %get-tuple-elem, ...), custom_call_target="tpu_custom_call" | custom-call | flops 3000000000 | bytes 16573696 | tf_op jit(solution)/shard_map/pallas_call | solution.py:36
  25.3 4.0 %collective-permute-start.4 = (bf16[2,83,1024]{2,1,0:T(8,128)(2,1)S(1)}, bf16[2,83,1024]{2,1,0:T(8,128)(2,1)S(1)}, u32[]{:S(2)}, u32[]{:S(2)}) collective-permute-start(bf16[2,83,1024]{2,1,0:T(8,128)(2,1)S(1)} %get-tuple-element.66.mine), channel_id=1, source_target_pairs={{0,2},{2,0},{1,3},{3,1},{4,6},{6,4},{5,7},{7,5},{8,10},{10,8},{9,1... | collective-permute-start | bytes 1019912 | tf_op jit(solution)/shard_map/ppermute | solution.py:701
  29.3 7.8 %collective-permute-done.4.rest_1_ = bf16[2,83,1024]{2,1,0:T(8,128)(2,1)S(1)} collective-permute-done((bf16[2,83,1024]{2,1,0:T(8,128)(2,1)S(1)}, bf16[2,83,1024]{2,1,0:T(8,128)(2,1)S(1)}, u32[]{:S(2)}, u32[]{:S(2)}) %collective-permute-start.4) | collective-permute-done | bytes 340000 | tf_op jit(solution)/shard_map/ppermute | solution.py:701
  38.8 7.0 %shard_map.183 = (bf16[256,768]{1,0:T(8,128)(2,1)S(1)}, bf16[256,768]{1,0:T(8,128)(2,1)S(1)}, bf16[64,16,640]{2,1,0:T(8,128)(2,1)S(1)}, bf16[64,16,640]{2,1,0:T(8,128)(2,1)S(1)}, bf16[16,128]{1,0:T(8,128)(2,1)S(1)}) custom-call(s32[32]{0:T(128)S(1)} %copy-done.18, bf16[2,83,1024]{2,1,0:T(8,128)(2,1)S(1)} %get-tuple-element.66.mine, ...), custom_call_target="tpu_custom_call" | custom-call | flops 6000000000 | bytes 14938752 | tf_op jit(solution)/shard_map/pallas_call | solution.py:36
  46.0 2.7 %shard_map.184 = (bf16[2,256,1152]{2,1,0:T(8,128)(2,1)S(1)}, bf16[2,64,768]{2,1,0:T(8,128)(2,1)S(1)}, bf16[320,1152]{1,0:T(8,128)(2,1)S(1)}) custom-call(bf16[256,2304]{1,0:T(8,128)(2,1)S(1)} %get-tuple-element.61.proj, bf16[64,1536]{1,0:T(8,128)(2,1)S(1)} %get-tuple-element.65.proj_rim, s32[8,128]{1,0:T(8,128)S(1)} %copy-done.31, s32[1,128]{1,0:T(1,128)S(1)} %bitcast.13, ...), custom_call_target="tpu_custom_call" | custom-call | flops 2000000000 | bytes 3887616 | tf_op jit(solution)/shard_map/pallas_call | solution.py:36
  51.9 2.6 %collective-permute-start.8 = (bf16[2,16,768]{2,1,0:T(8,128)(2,1)S(1)}, bf16[2,16,768]{2,1,0:T(8,128)(2,1)S(1)}, u32[]{:S(2)}, u32[]{:S(2)}) collective-permute-start(bf16[2,16,768]{2,1,0:T(8,128)(2,1)S(1)} %get-tuple-element.82), channel_id=1, source_target_pairs={{4,0},{8,4},{12,8},{16,12},{20,16},{24,20},{28,24},{32,28},{36,32}... | collective-permute-start | bytes 147464 | tf_op jit(solution)/shard_map/ppermute | solution.py:661
  54.5 3.5 %collective-permute-start.9 = (bf16[2,16,768]{2,1,0:T(8,128)(2,1)S(1)}, bf16[2,16,768]{2,1,0:T(8,128)(2,1)S(1)}, u32[]{:S(2)}, u32[]{:S(2)}) collective-permute-start(bf16[2,16,768]{2,1,0:T(8,128)(2,1)S(1)} %get-tuple-element.83), channel_id=1, source_target_pairs={{0,4},{4,8},{8,12},{12,16},{16,20},{20,24},{24,28},{28,32},{32,36}... | collective-permute-start | bytes 147464 | tf_op jit(solution)/shard_map/ppermute | solution.py:662
  58.0 3.7 %shard_map.186 = (bf16[16,4,16,768]{3,2,1,0:T(8,128)(2,1)}, bf16[16,16,768]{2,1,0:T(8,128)(2,1)S(1)}, bf16[16,16,768]{2,1,0:T(8,128)(2,1)}, bf16[16,16,768]{2,1,0:T(8,128)(2,1)S(1)}, bf16[16,16,768]{2,1,0:T(8,128)(2,1)S(1)}) custom-call(bf16[320,768]{1,0:T(8,128)(2,1)S(1)} %get-tuple-element.64.normed, ...), custom_call_target="tpu_custom_call" | custom-call | flops 2000000000 | bytes 8916992 | tf_op jit(solution)/shard_map/pallas_call | solution.py:36
  64.5 6.4 %all-to-all-start = ((bf16[16,4,16,768]{3,2,1,0:T(8,128)(2,1)}), bf16[16,4,16,768]{3,2,1,0:T(8,128)(2,1)S(1)}, u32[]{:S(2)}, u32[]{:S(2)}) async-start(bf16[16,4,16,768]{3,2,1,0:T(8,128)(2,1)} %get-tuple-element.84), calls=%async_computation | async-start | bytes 3145728 | tf_op jit(solution)/shard_map/all_to_all | solution.py:650
  73.1 3.6 %collective-permute-start.11 = (bf16[16,16,768]{2,1,0:T(8,128)(2,1)}, bf16[16,16,768]{2,1,0:T(8,128)(2,1)S(1)}, u32[]{:S(2)}, u32[]{:S(2)}) collective-permute-start(bf16[16,16,768]{2,1,0:T(8,128)(2,1)} %copy-done.24), channel_id=1, source_target_pairs={{0,2},{16,18},{2,0},{18,16},{1,3},{17,19},{3,1},{19,17},{4,6},{20,... | collective-permute-start | bytes 1179656 | tf_op jit(solution)/shard_map/ppermute | solution.py:646
  76.8 7.8 %collective-permute-done.10.rest_1_ = bf16[16,16,768]{2,1,0:T(8,128)(2,1)S(1)} collective-permute-done((bf16[16,16,768]{2,1,0:T(8,128)(2,1)}, bf16[16,16,768]{2,1,0:T(8,128)(2,1)S(1)}, u32[]{:S(2)}, u32[]{:S(2)}) %collective-permute-start.10) | collective-permute-done | bytes 393248 | tf_op jit(solution)/shard_map/ppermute | solution.py:646
  84.5 9.0 %collective-permute-done.11.rest_2_ = bf16[16,16,768]{2,1,0:T(8,128)(2,1)S(1)} collective-permute-done((bf16[16,16,768]{2,1,0:T(8,128)(2,1)}, bf16[16,16,768]{2,1,0:T(8,128)(2,1)S(1)}, u32[]{:S(2)}, u32[]{:S(2)}) %collective-permute-start.11) | collective-permute-done | bytes 393248 | tf_op jit(solution)/shard_map/ppermute | solution.py:646
  99.1 7.2 %all-to-all-start.1 = ((bf16[16,16,768]{2,1,0:T(8,128)(2,1)}), bf16[16,16,768]{2,1,0:T(8,128)(2,1)S(1)}, u32[]{:S(2)}, u32[]{:S(2)}) async-start(bf16[16,16,768]{2,1,0:T(8,128)(2,1)} %copy-done.5), calls=%async_computation.1 | async-start | bytes 786432 | tf_op jit(solution)/shard_map/all_to_all | solution.py:650
  107.0 2.9 %collective-permute-start.14 = (bf16[1,16,768]{2,1,0:T(8,128)(2,1)}, bf16[1,16,768]{2,1,0:T(8,128)(2,1)S(1)}, u32[]{:S(2)}, u32[]{:S(2)}) collective-permute-start(bf16[1,16,768]{2,1,0:T(8,128)(2,1)} %copy-done.28), channel_id=1, source_target_pairs={{0,2},{16,18},{2,0},{18,16},{1,3},{17,19},{3,1},{19,17},{4,6},{20,... | collective-permute-start | bytes 73736 | tf_op jit(solution)/shard_map/ppermute | solution.py:646
  114.8 2.7 %collective-permute-start.18 = (bf16[1,16,768]{2,1,0:T(8,128)(2,1)S(1)}, bf16[1,16,768]{2,1,0:T(8,128)(2,1)S(1)}, u32[]{:S(2)}, u32[]{:S(2)}) collective-permute-start(bf16[1,16,768]{2,1,0:T(8,128)(2,1)S(1)} %get-tuple-element.94.one), channel_id=1, source_target_pairs={{0,18},{16,0},{2,16},{18,2},{1,19},{17,1},{3,17},{19,3},{4,22},{20... | collective-permute-start | bytes 73736 | tf_op jit(solution)/shard_map/ppermute | solution.py:646
  119.0 3.8 %collective-permute-done.17.three = bf16[1,16,768]{2,1,0:T(8,128)(2,1)S(1)} collective-permute-done((bf16[1,16,768]{2,1,0:T(8,128)(2,1)S(1)}, bf16[1,16,768]{2,1,0:T(8,128)(2,1)S(1)}, u32[]{:S(2)}, u32[]{:S(2)}) %collective-permute-start.17) | collective-permute-done | bytes 24608 | tf_op jit(solution)/shard_map/ppermute | solution.py:646
  123.3 23.6 %all_to_all.20.plane = bf16[16,4,16,768]{3,2,1,0:T(8,128)(2,1)S(1)} all-to-all(bf16[16,4,16,768]{3,2,1,0:T(8,128)(2,1)S(1)} %bitcast.8), channel_id=1, replica_groups=mesh['x'=4,'zlo'=2,'y'=4,'zhi'=2,'core'=2] {'x','y'}, dimensions={0} | all-to-all | bytes 3145728 | tf_op jit(solution)/shard_map/all_to_all | solution.py:650
  146.9 14.0 %all_to_all.21.one = bf16[16,16,768]{2,1,0:T(8,128)(2,1)S(1)} all-to-all(bf16[16,16,768]{2,1,0:T(8,128)(2,1)S(1)} %bitcast.10), channel_id=1, replica_groups=mesh['x'=4,'zlo'=2,'y'=4,'zhi'=2,'core'=2] {'x','y'}, dimensions={0} | all-to-all | bytes 786432 | tf_op jit(solution)/shard_map/all_to_all | solution.py:650
  163.8 9.1 %collective-permute-done.25.four = bf16[16,16,768]{2,1,0:T(8,128)(2,1)S(1)} collective-permute-done((bf16[16,16,768]{2,1,0:T(8,128)(2,1)S(1)}, bf16[16,16,768]{2,1,0:T(8,128)(2,1)S(1)}, u32[]{:S(2)}, u32[]{:S(2)}) %collective-permute-start.25) | collective-permute-done | bytes 393248 | tf_op jit(solution)/shard_map/ppermute | solution.py:646
  175.3 6.0 %collective-permute-done.21.two = bf16[16,16,768]{2,1,0:T(8,128)(2,1)S(1)} collective-permute-done((bf16[16,16,768]{2,1,0:T(8,128)(2,1)S(1)}, bf16[16,16,768]{2,1,0:T(8,128)(2,1)S(1)}, u32[]{:S(2)}, u32[]{:S(2)}) %collective-permute-start.21) | collective-permute-done | bytes 393248 | tf_op jit(solution)/shard_map/ppermute | solution.py:646
  182.6 3.4 %shard_map.190 = (f32[768,2304]{1,0:T(8,128)}, f32[768,768]{1,0:T(8,128)}, f32[768,768]{1,0:T(8,128)}, f32[96,384]{1,0:T(8,128)S(1)}, f32[32,768]{1,0:T(8,128)S(1)}, /*index=5*/f32[1,1]{1,0:T(1,128)}) custom-call(bf16[16,4,16,768]{3,2,1,0:T(8,128)(2,1)S(1)} %all_to_all.20.plane, bf16[16,16,768]{2,1,0:T(8,128)(2,1)S(1)} %all_to_all.21.one, ...), custom_call_target="tpu_custom_call" | custom-call | bytes 9000000 | tf_op jit(solution)/shard_map/pallas_call | solution.py:533
  186.1 4.2 %shard_map.191 = (f32[768,2304]{1,0:T(8,128)}, f32[768,768]{1,0:T(8,128)}, f32[768,768]{1,0:T(8,128)}, f32[83,768]{1,0:T(8,128)}, f32[32,768]{1,0:T(8,128)}, /*index=5*/f32[1,1]{1,0:T(1,128)}) custom-call(bf16[16,4,16,768]{3,2,1,0:T(8,128)(2,1)S(1)} %collective-permute-done.19.plane, ...), custom_call_target="tpu_custom_call", output_to_operand_aliasing={{0}: (6, {}), {1}: (7, {}), {2}: (8, {})} | custom-call | bytes 9000000 | tf_op jit(solution)/shard_map/pallas_call | solution.py:533
  (115 shorter events, 39.8 us)
Async XLA Ops:
  2.6 14.0 %collective-permute-start = (bf16[2,16,768]{2,1,0:T(8,128)(2,1)S(1)}, bf16[2,16,768]{2,1,0:T(8,128)(2,1)S(1)}, u32[]{:S(2)}, u32[]{:S(2)}) collective-permute-start(bf16[2,16,768]{2,1,0:T(8,128)(2,1)S(1)} %get-tuple-element.62), channel_id=1, source_target_pairs={{0,4},{4,8},{8,12},{12,16},{16,20},{20,24},{24,28},{28,32},{32,36}... | collective-permute-start | bytes 147464 | tf_op jit(solution)/shard_map/ppermute | solution.py:574
  6.1 10.5 %collective-permute-start.1 = (bf16[2,16,768]{2,1,0:T(8,128)(2,1)S(1)}, bf16[2,16,768]{2,1,0:T(8,128)(2,1)S(1)}, u32[]{:S(2)}, u32[]{:S(2)}) collective-permute-start(bf16[2,16,768]{2,1,0:T(8,128)(2,1)S(1)} %get-tuple-element.63), channel_id=1, source_target_pairs={{4,0},{8,4},{12,8},{16,12},{20,16},{24,20},{28,24},{32,28},{36,32}... | collective-permute-start | bytes 147464 | tf_op jit(solution)/shard_map/ppermute | solution.py:575
  25.3 11.8 %collective-permute-start.4 = (bf16[2,83,1024]{2,1,0:T(8,128)(2,1)S(1)}, bf16[2,83,1024]{2,1,0:T(8,128)(2,1)S(1)}, u32[]{:S(2)}, u32[]{:S(2)}) collective-permute-start(bf16[2,83,1024]{2,1,0:T(8,128)(2,1)S(1)} %get-tuple-element.66.mine), channel_id=1, source_target_pairs={{0,2},{2,0},{1,3},{3,1},{4,6},{6,4},{5,7},{7,5},{8,10},{10,8},{9,1... | collective-permute-start | bytes 1019912 | tf_op jit(solution)/shard_map/ppermute | solution.py:701
  29.3 7.9 %collective-permute-start.3 = (bf16[2,83,1024]{2,1,0:T(8,128)(2,1)S(1)}, bf16[2,83,1024]{2,1,0:T(8,128)(2,1)S(1)}, u32[]{:S(2)}, u32[]{:S(2)}) collective-permute-start(bf16[2,83,1024]{2,1,0:T(8,128)(2,1)S(1)} %get-tuple-element.66.mine), channel_id=1, source_target_pairs={{0,1},{1,0},{2,3},{3,2},{4,5},{5,4},{6,7},{7,6},{8,9},{9,8},{10,11... | collective-permute-start | bytes 1019912 | tf_op jit(solution)/shard_map/ppermute | solution.py:702
  45.8 12.2 %collective-permute-start.7 = (bf16[64,16,640]{2,1,0:T(8,128)(2,1)S(1)}, bf16[64,16,640]{2,1,0:T(8,128)(2,1)S(1)}, u32[]{:S(2)}, u32[]{:S(2)}) collective-permute-start(bf16[64,16,640]{2,1,0:T(8,128)(2,1)S(1)} %get-tuple-element.77), channel_id=1, source_target_pairs={{0,1},{1,0},{2,3},{3,2},{4,5},{5,4},{6,7},{7,6},{8,9},{9,8},{10,11... | collective-permute-start | bytes 3932168 | tf_op jit(solution)/shard_map/ppermute | solution.py:615
  48.7 9.3 %collective-permute-start.6 = (bf16[320,1152]{1,0:T(8,128)(2,1)S(1)}, bf16[320,1152]{1,0:T(8,128)(2,1)S(1)}, u32[]{:S(2)}, u32[]{:S(2)}) collective-permute-start(bf16[320,1152]{1,0:T(8,128)(2,1)S(1)} %get-tuple-element.75), channel_id=1, source_target_pairs={{0,1},{1,0},{2,3},{3,2},{4,5},{5,4},{6,7},{7,6},{8,9},{9,8},{10,11... | collective-permute-start | bytes 2211848 | tf_op jit(solution)/shard_map/ppermute | solution.py:626
  49.2 8.8 %collective-permute-start.2 = (bf16[320,768]{1,0:T(8,128)(2,1)S(1)}, bf16[320,768]{1,0:T(8,128)(2,1)S(1)}, u32[]{:S(2)}, u32[]{:S(2)}) collective-permute-start(bf16[320,768]{1,0:T(8,128)(2,1)S(1)} %get-tuple-element.64.normed), channel_id=1, source_target_pairs={{0,1},{1,0},{2,3},{3,2},{4,5},{5,4},{6,7},{7,6},{8,9},{9,8},{10,11... | collective-permute-start | bytes 1474568 | tf_op jit(solution)/shard_map/ppermute | solution.py:598
  51.9 11.3 %collective-permute-start.8 = (bf16[2,16,768]{2,1,0:T(8,128)(2,1)S(1)}, bf16[2,16,768]{2,1,0:T(8,128)(2,1)S(1)}, u32[]{:S(2)}, u32[]{:S(2)}) collective-permute-start(bf16[2,16,768]{2,1,0:T(8,128)(2,1)S(1)} %get-tuple-element.82), channel_id=1, source_target_pairs={{4,0},{8,4},{12,8},{16,12},{20,16},{24,20},{28,24},{32,28},{36,32}... | collective-permute-start | bytes 147464 | tf_op jit(solution)/shard_map/ppermute | solution.py:661
  54.5 9.3 %collective-permute-start.9 = (bf16[2,16,768]{2,1,0:T(8,128)(2,1)S(1)}, bf16[2,16,768]{2,1,0:T(8,128)(2,1)S(1)}, u32[]{:S(2)}, u32[]{:S(2)}) collective-permute-start(bf16[2,16,768]{2,1,0:T(8,128)(2,1)S(1)} %get-tuple-element.83), channel_id=1, source_target_pairs={{0,4},{4,8},{8,12},{12,16},{16,20},{20,24},{24,28},{28,32},{32,36}... | collective-permute-start | bytes 147464 | tf_op jit(solution)/shard_map/ppermute | solution.py:662
  64.5 29.8 %all-to-all-start = ((bf16[16,4,16,768]{3,2,1,0:T(8,128)(2,1)}), bf16[16,4,16,768]{3,2,1,0:T(8,128)(2,1)S(1)}, u32[]{:S(2)}, u32[]{:S(2)}) async-start(bf16[16,4,16,768]{3,2,1,0:T(8,128)(2,1)} %get-tuple-element.84), calls=%async_computation | async-start | bytes 3145728 | tf_op jit(solution)/shard_map/all_to_all | solution.py:650
  70.9 13.6 %collective-permute-start.10 = (bf16[16,16,768]{2,1,0:T(8,128)(2,1)}, bf16[16,16,768]{2,1,0:T(8,128)(2,1)S(1)}, u32[]{:S(2)}, u32[]{:S(2)}) collective-permute-start(bf16[16,16,768]{2,1,0:T(8,128)(2,1)} %get-tuple-element.86), channel_id=1, source_target_pairs={{0,16},{16,2},{2,18},{18,0},{1,17},{17,3},{3,19},{19,1},{4,20},{20... | collective-permute-start | bytes 1179656 | tf_op jit(solution)/shard_map/ppermute | solution.py:646
  73.1 20.5 %collective-permute-start.11 = (bf16[16,16,768]{2,1,0:T(8,128)(2,1)}, bf16[16,16,768]{2,1,0:T(8,128)(2,1)S(1)}, u32[]{:S(2)}, u32[]{:S(2)}) collective-permute-start(bf16[16,16,768]{2,1,0:T(8,128)(2,1)} %copy-done.24), channel_id=1, source_target_pairs={{0,2},{16,18},{2,0},{18,16},{1,3},{17,19},{3,1},{19,17},{4,6},{20,... | collective-permute-start | bytes 1179656 | tf_op jit(solution)/shard_map/ppermute | solution.py:646
  76.7 16.9 %collective-permute-start.12 = (bf16[16,16,768]{2,1,0:T(8,128)(2,1)}, bf16[16,16,768]{2,1,0:T(8,128)(2,1)S(1)}, u32[]{:S(2)}, u32[]{:S(2)}) collective-permute-start(bf16[16,16,768]{2,1,0:T(8,128)(2,1)} %copy-done.23), channel_id=1, source_target_pairs={{0,18},{16,0},{2,16},{18,2},{1,19},{17,1},{3,17},{19,3},{4,22},{20... | collective-permute-start | bytes 1179656 | tf_op jit(solution)/shard_map/ppermute | solution.py:646
  99.1 14.9 %all-to-all-start.1 = ((bf16[16,16,768]{2,1,0:T(8,128)(2,1)}), bf16[16,16,768]{2,1,0:T(8,128)(2,1)S(1)}, u32[]{:S(2)}, u32[]{:S(2)}) async-start(bf16[16,16,768]{2,1,0:T(8,128)(2,1)} %copy-done.5), calls=%async_computation.1 | async-start | bytes 786432 | tf_op jit(solution)/shard_map/all_to_all | solution.py:650
  106.4 5.2 %collective-permute-start.13 = (bf16[1,16,768]{2,1,0:T(8,128)(2,1)}, bf16[1,16,768]{2,1,0:T(8,128)(2,1)S(1)}, u32[]{:S(2)}, u32[]{:S(2)}) collective-permute-start(bf16[1,16,768]{2,1,0:T(8,128)(2,1)} %copy-done.29), channel_id=1, source_target_pairs={{0,16},{16,2},{2,18},{18,0},{1,17},{17,3},{3,19},{19,1},{4,20},{20... | collective-permute-start | bytes 73736 | tf_op jit(solution)/shard_map/ppermute | solution.py:646
  107.0 5.5 %collective-permute-start.14 = (bf16[1,16,768]{2,1,0:T(8,128)(2,1)}, bf16[1,16,768]{2,1,0:T(8,128)(2,1)S(1)}, u32[]{:S(2)}, u32[]{:S(2)}) collective-permute-start(bf16[1,16,768]{2,1,0:T(8,128)(2,1)} %copy-done.28), channel_id=1, source_target_pairs={{0,2},{16,18},{2,0},{18,16},{1,3},{17,19},{3,1},{19,17},{4,6},{20,... | collective-permute-start | bytes 73736 | tf_op jit(solution)/shard_map/ppermute | solution.py:646
  117.5 5.3 %collective-permute-start.17 = (bf16[1,16,768]{2,1,0:T(8,128)(2,1)S(1)}, bf16[1,16,768]{2,1,0:T(8,128)(2,1)S(1)}, u32[]{:S(2)}, u32[]{:S(2)}) collective-permute-start(bf16[1,16,768]{2,1,0:T(8,128)(2,1)S(1)} %get-tuple-element.94.one), channel_id=1, source_target_pairs={{0,2},{16,18},{2,0},{18,16},{1,3},{17,19},{3,1},{19,17},{4,6},{20,... | collective-permute-start | bytes 73736 | tf_op jit(solution)/shard_map/ppermute | solution.py:646
  146.9 39.1 %collective-permute-start.19 = (bf16[16,4,16,768]{3,2,1,0:T(8,128)(2,1)S(1)}, bf16[16,4,16,768]{3,2,1,0:T(8,128)(2,1)S(1)}, u32[]{:S(2)}, u32[]{:S(2)}) collective-permute-start(bf16[16,4,16,768]{3,2,1,0:T(8,128)(2,1)S(1)} %all_to_all.20.plane), channel_id=1, source_target_pairs={{0,1},{1,0},{2,3},{3,2},{4,5},{5,4},{6,7},{7,6},{8,9},{9,8},{10,11... | collective-permute-start | bytes 4718600 | tf_op jit(solution)/shard_map/ppermute | solution.py:688
  160.9 12.1 %collective-permute-start.25 = (bf16[16,16,768]{2,1,0:T(8,128)(2,1)S(1)}, bf16[16,16,768]{2,1,0:T(8,128)(2,1)S(1)}, u32[]{:S(2)}, u32[]{:S(2)}) collective-permute-start(bf16[16,16,768]{2,1,0:T(8,128)(2,1)S(1)} %all_to_all.21.one), channel_id=1, source_target_pairs={{0,18},{16,0},{2,16},{18,2},{1,19},{17,1},{3,17},{19,3},{4,22},{20... | collective-permute-start | bytes 1179656 | tf_op jit(solution)/shard_map/ppermute | solution.py:646
  161.7 13.6 %collective-permute-start.23 = (bf16[16,16,768]{2,1,0:T(8,128)(2,1)S(1)}, bf16[16,16,768]{2,1,0:T(8,128)(2,1)S(1)}, u32[]{:S(2)}, u32[]{:S(2)}) collective-permute-start(bf16[16,16,768]{2,1,0:T(8,128)(2,1)S(1)} %all_to_all.21.one), channel_id=1, source_target_pairs={{0,2},{16,18},{2,0},{18,16},{1,3},{17,19},{3,1},{19,17},{4,6},{20,... | collective-permute-start | bytes 1179656 | tf_op jit(solution)/shard_map/ppermute | solution.py:646
  162.9 18.4 %collective-permute-start.21 = (bf16[16,16,768]{2,1,0:T(8,128)(2,1)S(1)}, bf16[16,16,768]{2,1,0:T(8,128)(2,1)S(1)}, u32[]{:S(2)}, u32[]{:S(2)}) collective-permute-start(bf16[16,16,768]{2,1,0:T(8,128)(2,1)S(1)} %all_to_all.21.one), channel_id=1, source_target_pairs={{0,16},{16,2},{2,18},{18,0},{1,17},{17,3},{3,19},{19,1},{4,20},{20... | collective-permute-start | bytes 1179656 | tf_op jit(solution)/shard_map/ppermute | solution.py:646
  163.8 22.2 %collective-permute-start.20 = (bf16[16,16,768]{2,1,0:T(8,128)(2,1)S(1)}, bf16[16,16,768]{2,1,0:T(8,128)(2,1)S(1)}, u32[]{:S(2)}, u32[]{:S(2)}) collective-permute-start(bf16[16,16,768]{2,1,0:T(8,128)(2,1)S(1)} %all_to_all.21.one), channel_id=1, source_target_pairs={{0,1},{1,0},{2,3},{3,2},{4,5},{5,4},{6,7},{7,6},{8,9},{9,8},{10,11... | collective-permute-start | bytes 1179656 | tf_op jit(solution)/shard_map/ppermute | solution.py:687
  172.9 13.1 %collective-permute-start.26 = (bf16[16,16,768]{2,1,0:T(8,128)(2,1)S(1)}, bf16[16,16,768]{2,1,0:T(8,128)(2,1)S(1)}, u32[]{:S(2)}, u32[]{:S(2)}) collective-permute-start(bf16[16,16,768]{2,1,0:T(8,128)(2,1)S(1)} %collective-permute-done.25.four), channel_id=1, source_target_pairs={{0,1},{1,0},{2,3},{3,2},{4,5},{5,4},{6,7},{7,6},{8,9},{9,8},{10,11... | collective-permute-start | bytes 1179656 | tf_op jit(solution)/shard_map/ppermute | solution.py:687
  175.3 10.7 %collective-permute-start.24 = (bf16[16,16,768]{2,1,0:T(8,128)(2,1)S(1)}, bf16[16,16,768]{2,1,0:T(8,128)(2,1)S(1)}, u32[]{:S(2)}, u32[]{:S(2)}) collective-permute-start(bf16[16,16,768]{2,1,0:T(8,128)(2,1)S(1)} %collective-permute-done.23.three), channel_id=1, source_target_pairs={{0,1},{1,0},{2,3},{3,2},{4,5},{5,4},{6,7},{7,6},{8,9},{9,8},{10,11... | collective-permute-start | bytes 1179656 | tf_op jit(solution)/shard_map/ppermute | solution.py:687
  (38 other events, 300.7 us)

commit v4 on v3

--- a/solution.py
+++ b/solution.py
@@ -1,3 +1,5 @@
+import functools
+
 import jax
 import jax.numpy as jnp
 from jax import lax
@@ -10,7 +12,8 @@
 TILE = 128
 GROUPS = 16
 SPACE = ("x", "zlo", "y")
-HALF = 768
+SPLIT = 896
+REST = 1536 - SPLIT
 SLOTS_A = 5
 SLOTS_B = 7
 CHUNKS = 4 * GROUPS
@@ -22,6 +25,7 @@
 TN = (((0,), (0,)), ((), ()))
 VMEM = pl.BlockSpec(memory_space=pltpu.VMEM)
 SMEM = pl.BlockSpec(memory_space=pltpu.SMEM)
+APART = pl.BlockSpec(memory_space=pltpu.HBM)
 MIB = 1024 * 1024
 
 
@@ -29,15 +33,23 @@
     return lax.dot_general(a, b, dims, preferred_element_type=F32)
 
 
-def call(body, out_shape, *args, smem=(), flops=0, scratch=(), vmem=16):
-    out_shape = [jax.ShapeDtypeStruct(s, d) for s, d in out_shape]
+def call(body, out_shape, *args, smem=(), apart=(), far=(), flops=0, scratch=(), vmem=16):
+    out_shape = [
+        pltpu.HBM(s, d) if i in far else jax.ShapeDtypeStruct(s, d)
+        for i, (s, d) in enumerate(out_shape)
+    ]
     size = sum(a.size * a.dtype.itemsize for a in args)
-    size += sum(o.size * o.dtype.itemsize for o in out_shape)
+    args = [
+        pltpu.with_memory_space_constraint(a, pltpu.HBM) if i in apart else a
+        for i, a in enumerate(args)
+    ]
     return pl.pallas_call(
         body,
         out_shape=out_shape,
-        in_specs=[SMEM if i in smem else VMEM for i in range(len(args))],
-        out_specs=[VMEM] * len(out_shape),
+        in_specs=[
+            SMEM if i in smem else APART if i in apart else VMEM for i in range(len(args))
+        ],
+        out_specs=[APART if i in far else VMEM for i in range(len(out_shape))],
         scratch_shapes=list(scratch),
         compiler_params=pltpu.CompilerParams(vmem_limit_bytes=vmem * MIB),
         cost_estimate=pl.CostEstimate(flops=flops, bytes_accessed=size, transcendentals=0),
@@ -67,7 +79,9 @@
     return 2 * lax.axis_index("zhi") + lax.axis_index("zlo")
 
 
-def send_body(latent, rows, sent_up, sent_down):
+def send_body(latent_far, rows_far, sent_up, sent_down, latent, rows, sems):
+    for copy in fetch((latent_far, rows_far), (latent, rows), sems):
+        copy.wait()
     nodes = latent.shape[2]
     rim = rows.shape[1]
     both = jnp.concatenate([rows[0:1, :], rows[1:2, :]], axis=1)
@@ -79,7 +93,28 @@
         sent_down[m] = picked[rim:]
 
 
-def local_body(latent, noise, w_noise, w_qkv, own, normed, proj):
+def fetch(sources, targets, sems):
+    copies = [
+        pltpu.make_async_copy(a, b, sems.at[i]) for i, (a, b) in enumerate(zip(sources, targets))
+    ]
+    for copy in copies:
+        copy.start()
+    return copies
+
+
+def local_body(
+    latent_far, noise_far, w_noise_far, w_qkv, own, normed, proj,
+    latent, noise, w_noise, held, total, sems,
+):
+    thirds = [slice(r, r + 256) for r in range(0, held.shape[0], 256)]
+    copies = fetch(
+        [latent_far, noise_far, w_noise_far] + [w_qkv.at[r] for r in thirds],
+        [latent, noise, w_noise] + [held.at[r] for r in thirds],
+        sems,
+    )
+    for copy in copies[:3]:
+        copy.wait()
+    copies = copies[3:]
     gain = gains(noise[...], w_noise[...])
     members, _, nodes = latent.shape
     for m in range(members):
@@ -87,7 +122,15 @@
         own[m] = rows.astype(BF16)
         hat, _ = normalise(rows)
         normed[m * nodes : (m + 1) * nodes] = (hat * gain[m : m + 1]).astype(BF16)
-    proj[...] = mm(normed[...], w_qkv[...]).astype(BF16)
+    for i, r in enumerate(thirds):
+        copies[i].wait()
+        part = mm(normed[:, r], held[r])
+        if i == 0:
+            total[...] = part
+        elif i < len(thirds) - 1:
+            total[...] = total[...] + part
+        else:
+            proj[...] = (total[...] + part).astype(BF16)
 
 
 def slot_mask(nbr, degree, rows):
@@ -117,7 +160,12 @@
     own, normed, proj, low, high, noise, w_noise, w_qkv, w_out, w_hid, w_pred, nbr, degree,
     dec_nodes,
     normed_all, proj_rim, attended, stored, hidden, slope, forecast, table,
+    held_qkv, held_out, held_hid, sems,
 ):
+    wide = own.shape[2]
+    copies = fetch(
+        (w_qkv.at[:, wide:], w_out, w_hid), (held_qkv, held_out, held_hid), sems
+    )
     members, nodes, width = own.shape
     rim = low.shape[1]
     gain = gains(noise[...], w_noise[...])
@@ -127,7 +175,8 @@
         at = members * nodes + 2 * rim * m
         normed_all[at : at + 2 * rim] = (hat * gain[m : m + 1]).astype(BF16)
     normed_all[: members * nodes] = normed[...]
-    proj_rim[...] = mm(normed_all[members * nodes :], w_qkv[:, width:]).astype(BF16)
+    copies[0].wait()
+    proj_rim[...] = mm(normed_all[members * nodes :], held_qkv[...]).astype(BF16)
     mask = slot_mask(nbr, degree, nodes + 2 * rim)
     for m in range(members):
         here = slice(m * nodes, (m + 1) * nodes)
@@ -141,12 +190,14 @@
             score = mm(key, proj[here, at[0]], NT) * HEAD**-0.5
             weight = (jax.nn.sigmoid(score) * mask).astype(BF16)
             attended[here, at[0]] = mm(weight, value, TN).astype(BF16)
-    branch = mm(attended[...], w_out[...])
+    copies[1].wait()
+    branch = mm(attended[...], held_out[...])
     for m in range(members):
         here = slice(m * nodes, (m + 1) * nodes)
         stored[here] = (own[m].astype(F32) + branch[here]).astype(BF16)
     table[...] = point_table(dec_nodes, nodes)
-    mixed = mm(stored[...], w_hid[...]).astype(BF16)
+    copies[2].wait()
+    mixed = mm(stored[...], held_hid[...]).astype(BF16)
     block = 256
     for m in range(members):
         part = mixed[m * nodes : (m + 1) * nodes]
@@ -339,30 +390,34 @@
     g_noise[...] = d_noise.astype(BF16)
 
 
+def pack_first_body(keep, came, *stacks):
+    depth = depth_here()
+    for shift, target in enumerate(stacks):
+        level = lax.rem(depth + shift, 4)
+        target[...] = (keep[level].astype(F32) + came[level].astype(F32)).astype(BF16)
+
+
 def pack_body(
-    normed, normed_theirs, d_proj, d_rim, d_theirs, keep, came, g_noise, loss, plane, *rest
+    normed, normed_theirs, d_proj, d_rim, d_theirs, g_noise, loss, plane_far, g_half, plane, sems
 ):
-    *stacks, g_half, stack = rest
-    core, depth = lax.axis_index("core"), depth_here()
+    copies = []
+    core = lax.axis_index("core")
     rows = d_proj.shape[1]
     wide = 2 * d_proj.shape[2] // 3
     width = normed.shape[1]
     mine = d_proj[core]
     rim = d_rim[core]
-    for r in range(0, width, 256):
-        at = slice(r, r + 256)
+    for r in range(0, width, 192):
+        at = slice(r, r + 192)
         total = mm(normed[:rows, at], mine, TN) + mm(normed_theirs[:rows, at], d_theirs[:rows], TN)
         g_half[at, : wide // 2] = total[:, : wide // 2].astype(BF16)
         edge = mm(normed[rows:, at], rim, TN)
         edge = edge + mm(normed_theirs[rows:, at], d_theirs[rows:, :wide], TN)
         g_half[at, wide // 2 :] = (total[:, wide // 2 :] + edge).astype(BF16)
-    for k in range(GROUPS):
-        for sub in range(4):
-            level, spot = k // 4, 4 * (k % 4) + sub
-            first = keep[4 * k + sub].astype(F32) + came[4 * k + sub].astype(F32)
-            plane[spot, level, :, : TILE * SLOTS_A] = first.astype(BF16)
-            for j in range(SLOTS_B):
-                slot = SLOTS_B * sub + j
+        level = r // 192
+        for k in range(4 * level, 4 * level + 4):
+            for slot in range(4 * SLOTS_B):
+                spot, lane = 4 * (k % 4) + slot // SLOTS_B, TILE * (slot % SLOTS_B)
                 if slot < 27:
                     row, column = 48 * k + 16 * (slot // 9), TILE * (slot % 9)
                     piece = g_half[row : row + 16, column : column + TILE]
@@ -373,18 +428,15 @@
                     piece = loss[...]
                 else:
                     piece = jnp.zeros((16, TILE), BF16)
-                lane = TILE * (SLOTS_A + j)
-                if lane < HALF:
-                    plane[spot, level, :, lane : lane + TILE] = piece
-                else:
-                    stack[level, spot, :, lane - HALF : lane - HALF + TILE] = piece
-    for shift in range(4):
-        stacks[shift][...] = stack[lax.rem(depth + shift, 4)]
-
-
-def first_sum_body(came, *rest):
+                plane[spot, level, :, lane : lane + TILE] = piece
+        copies += fetch([plane.at[:, level]], [plane_far.at[:, level]], sems.at[level : level + 1])
+    for copy in copies:
+        copy.wait()
+
+
+def sum_plane_body(came, *rest):
     depth = depth_here()
-    stacks, targets, (stack, column) = rest[:4], rest[4:8], rest[8:]
+    targets, column = rest[:4], rest[4]
     for j in range(came.shape[1]):
         total = came[0, j].astype(F32)
         for i in range(1, came.shape[0]):
@@ -392,10 +444,11 @@
         column[:, j] = total.astype(BF16)
     for shift, target in enumerate(targets):
         target[...] = column[lax.rem(depth + shift, 4)]
-    total = stacks[0][...].astype(F32)
-    for part in stacks[1:]:
-        total = total + part[...].astype(F32)
-    stack[...] = total.astype(BF16)
+
+
+def sum_stack_body(one, two, three, four, total):
+    part = one[...].astype(F32) + two[...].astype(F32)
+    total[...] = (part + three[...].astype(F32) + four[...].astype(F32)).astype(BF16)
 
 
 def second_sum_body(one, two, three, four, came, column, spread):
@@ -410,136 +463,143 @@
         spread[i] = total
 
 
-def spread_body(one, two, three, four, spread, column):
+def spread_body(one, two, three, four, spread, column, sems):
     depth = depth_here()
     for shift, piece in enumerate((one, two, three, four)):
         column[lax.rem(depth + (4 - shift), 4)] = piece[...]
-    for j in range(spread.shape[1]):
-        total = column[:, j]
-        for i in range(spread.shape[0]):
-            spread[i, j] = total
-
-
-def unpack_tiles(core, plane, stacks, targets, pred, noise, halves, sems):
-    wide = halves[1].shape[1]
-    depth = depth_here()
+    parts, spots = spread.shape[1], spread.shape[0]
+    sources = [column.at[:, j] for j in range(parts) for i in range(spots)]
+    targets = [spread.at[i, j] for j in range(parts) for i in range(spots)]
+    for copy in fetch(sources, targets, sems):
+        copy.wait()
+
+
+def unpack_first_body(*refs):
+    mine, theirs, (g_hid, g_out, g_pred, hid, out, pred, sems) = refs[:4], refs[4:8], refs[8:]
+    depth, core = depth_here(), lax.axis_index("core")
+    width = hid.shape[1]
     copies = []
-    total = None
     for step in range(4):
         level = lax.rem(depth + 4 - step, 4)
-        here = plane.at[:, level]
-
-        def tile(group, sub, j):
-            lane, spot = TILE * j, 4 * group + sub
-            if lane < HALF:
-                return here[spot, :, lane : lane + TILE].astype(F32)
-            return stacks[step][spot, :, lane - HALF : lane - HALF + TILE].astype(F32)
-
-        def first(group, slot):
-            return tile(group, slot // SLOTS_A, slot % SLOTS_A)
-
-        def second(group, slot):
-            return tile(group, slot // SLOTS_B, SLOTS_A + slot % SLOTS_B)
-
-        base = 192 * step
+        for side, which in ((mine, core), (theirs, 1 - core)):
+            start = which * (width // 2)
+
+            def column(j):
+                return pl.ds(pl.multiple_of(start + TILE * j, TILE), TILE)
+
+            for group in range(4):
+                k = 4 * level + group
+                for slot in range(4 * SLOTS_A):
+                    spot, lane = 4 * group + slot // SLOTS_A, TILE * (slot % SLOTS_A)
+                    piece = side[step][spot, :, lane : lane + TILE].astype(F32)
+                    if slot < 18:
+                        row = 192 * step + 48 * group + 16 * (slot % 9 // 3)
+                        (hid, out)[slot // 9][row : row + 16, column(slot % 3)] = piece
+                    else:
+                        index = k + GROUPS * (slot - 18)
+
+                        @pl.when(index < 18)
+                        def _():
+                            row = pl.multiple_of(16 * lax.div(index, 3), 16)
+                            pred[pl.ds(row, 16), column(lax.rem(index, 3))] = piece
+
+        base = slice(192 * step, 192 * step + 192)
+        rows = pl.ds(pl.multiple_of(192 * level, 16), 192)
+        copies += fetch(
+            (hid.at[base], out.at[base]), (g_hid.at[rows], g_out.at[rows]),
+            sems.at[2 * step : 2 * step + 2],
+        )
+    g_pred[...] = pred[: g_pred.shape[0]]
+    for copy in copies:
+        copy.wait()
+
+
+def unpack_plane(core, plane, g_qkv, noise, held, sems):
+    wide = held.shape[1] // 3
+    copies = []
+    total = jnp.zeros((16, TILE), F32)
+    for level in range(4):
         for group in range(4):
-            for slot in range(27):
-                row, column = base + 48 * group + 16 * (slot // 9), TILE * (slot % 9)
-                halves[0][row : row + 16, column : column + TILE] = second(group, slot)
-            for slot in range(18):
-                row, column = base + 48 * group + 16 * (slot % 9 // 3), TILE * (slot % 3)
-                halves[1 + slot // 9][row : row + 16, column : column + TILE] = first(group, slot)
             k = 4 * level + group
-            for slot in (18, 19):
-                index = k + GROUPS * (slot - 18)
-
-                @pl.when(index < 18)
-                def _():
-                    row = pl.multiple_of(16 * lax.div(index, 3), 16)
-                    column = pl.multiple_of(TILE * lax.rem(index, 3), TILE)
-                    pred[pl.ds(row, 16), pl.ds(column, TILE)] = first(group, slot)
-
-            spare = second(group, 27)
-
-            @pl.when(k < 12)
-            def _():
-                row = pl.multiple_of(16 * lax.div(k, 6), 16)
-                column = pl.multiple_of(TILE * lax.rem(k, 6), TILE)
-                noise[pl.ds(row, 16), pl.ds(column, TILE)] = spare
-
-            here_loss = jnp.where(k == 12, spare, 0.0)
-            total = here_loss if total is None else total + here_loss
-        rows = pl.ds(pl.multiple_of(192 * level, 16), 192)
-        for target, half, sections in ((0, 0, 3), (1, 1, 1), (2, 2, 1)):
-            for section in range(sections):
-                start = pl.multiple_of(2 * wide * section + wide * core, TILE)
-                copies.append(
-                    pltpu.make_async_copy(
-                        halves[half].at[base : base + 192, wide * section : wide * (section + 1)],
-                        targets[target].at[rows, pl.ds(start, wide)],
-                        sems.at[len(copies)],
-                    )
-                )
-                copies[-1].start()
+            for slot in range(4 * SLOTS_B):
+                spot, lane = 4 * group + slot // SLOTS_B, TILE * (slot % SLOTS_B)
+                if slot == 27 and k > 12:
+                    continue
+                piece = plane[spot, level, :, lane : lane + TILE].astype(F32)
+                if slot < 27:
+                    row, column = 48 * k + 16 * (slot // 9), TILE * (slot % 9)
+                    held[row : row + 16, column : column + TILE] = piece
+                elif k < 12:
+                    row, column = 16 * (k // 6), TILE * (k % 6)
+                    noise[row : row + 16, column : column + TILE] = piece
+                else:
+                    total = piece
+        base = slice(192 * level, 192 * level + 192)
+        for section in range(3):
+            start = pl.multiple_of(2 * wide * section + wide * core, TILE)
+            copies += fetch(
+                [held.at[base, wide * section : wide * (section + 1)]],
+                [g_qkv.at[base, pl.ds(start, wide)]],
+                sems.at[len(copies) : len(copies) + 1],
+            )
     return copies, jnp.sum(total, keepdims=True)
 
 
-def unpack_mine_body(
-    plane, one, two, three, four, g_qkv, g_hid, g_out, pred, noise, loss, *scratch
-):
-    *halves, sems = scratch
-    copies, total = unpack_tiles(
-        lax.axis_index("core"), plane, (one, two, three, four), (g_qkv, g_hid, g_out), pred, noise,
-        halves, sems,
-    )
+def unpack_mine_body(plane, g_qkv, noise, loss, held, sems):
+    copies, total = unpack_plane(lax.axis_index("core"), plane, g_qkv, noise, held, sems)
     loss[...] = total
     for copy in copies:
         copy.wait()
 
 
 def unpack_theirs_body(
-    plane, one, two, three, four, counts, _qkv, _hid, _out, pred_mine, noise_mine, loss_mine,
-    g_qkv, g_hid, g_out, g_pred, noise, mean, *scratch
+    plane, counts, _qkv, noise_mine, loss_mine, g_qkv, noise, mean, held, sems, channels
 ):
-    *halves, pred, sems = scratch
-    mine = lax.axis_index("core")
-    copies, total = unpack_tiles(
-        1 - mine, plane, (one, two, three, four), (g_qkv, g_hid, g_out), pred, noise, halves, sems
-    )
+    copies, total = unpack_plane(1 - lax.axis_index("core"), plane, g_qkv, noise, held, sems)
     noise[...] = noise[...] + noise_mine[...]
-    channels, width = g_pred.shape
-    wide = width // 2
-    for c in range(2):
-        own = pred_mine[:channels]
-        g_pred[:, c * wide : (c + 1) * wide] = jnp.where(mine == c, own, pred[:channels])
     live = jnp.sum(counts[...].astype(F32), keepdims=True)
     mean[...] = (total + loss_mine[...]) / (channels * live)
     for copy in copies:
         copy.wait()
 
 
-def unpack(plane, stacks, width, channels, counts=None, before=()):
-    wide = width // 2
-    big = ((width, 3 * width), (width, width), (width, width))
-    small = ((channels, width) if before else (96, wide), (32, width), (1, 1))
-    scratch = [pltpu.VMEM((width, n), F32) for n in (3 * wide, wide, wide)]
+def unpack(plane, width, channels=0, counts=None, before=()):
+    anywhere = pl.BlockSpec(memory_space=pl.ANY)
+    body = unpack_mine_body
+    args = (plane,)
     if before:
-        scratch.append(pltpu.VMEM((96, wide), F32))
-    scratch.append(pltpu.SemaphoreType.DMA((20,)))
+        body = functools.partial(unpack_theirs_body, channels=channels)
+        args += (counts, *before)
+    shapes = ((width, 3 * width), (32, width), (1, 1))
+    return pl.pallas_call(
+        body,
+        out_shape=[jax.ShapeDtypeStruct(shape, F32) for shape in shapes],
+        in_specs=[anywhere if i == 2 else VMEM for i in range(len(args))],
+        out_specs=[anywhere, VMEM, VMEM],
+        scratch_shapes=[
+            pltpu.VMEM((width, 3 * width // 2), F32), pltpu.SemaphoreType.DMA((12,)),
+        ],
+        input_output_aliases={2: 0} if before else {},
+        compiler_params=pltpu.CompilerParams(vmem_limit_bytes=16 * MIB),
+        cost_estimate=pl.CostEstimate(flops=0, bytes_accessed=6 * 10**6, transcendentals=0),
+    )(*args)
+
+
+def unpack_first(mine, theirs, width, channels):
+    shapes = ((width, width), (width, width), (channels, width))
     anywhere = pl.BlockSpec(memory_space=pl.ANY)
-    args = (plane, *stacks)
-    if before:
-        args += (counts, *before)
     return pl.pallas_call(
-        unpack_theirs_body if before else unpack_mine_body,
-        out_shape=[jax.ShapeDtypeStruct(shape, F32) for shape in big + small],
-        in_specs=[anywhere if 6 <= i < 9 else VMEM for i in range(len(args))],
-        out_specs=[anywhere] * 3 + [VMEM] * 3,
-        scratch_shapes=scratch,
-        input_output_aliases={6 + i: i for i in range(3)} if before else {},
-        compiler_params=pltpu.CompilerParams(vmem_limit_bytes=20 * MIB),
-        cost_estimate=pl.CostEstimate(flops=0, bytes_accessed=9 * 10**6, transcendentals=0),
-    )(*args)
+        unpack_first_body,
+        out_shape=[jax.ShapeDtypeStruct(shape, F32) for shape in shapes],
+        in_specs=[VMEM] * 8,
+        out_specs=[anywhere, anywhere, VMEM],
+        scratch_shapes=[
+            pltpu.VMEM((width, width), F32), pltpu.VMEM((width, width), F32),
+            pltpu.VMEM((96, width), F32), pltpu.SemaphoreType.DMA((8,)),
+        ],
+        compiler_params=pltpu.CompilerParams(vmem_limit_bytes=16 * MIB),
+        cost_estimate=pl.CostEstimate(flops=0, bytes_accessed=8 * 10**6, transcendentals=0),
+    )(*mine, *theirs)
 
 
 def join_body(d_own, rows, from_next, from_prev, d_latent):
@@ -569,7 +629,12 @@
     down = [(i + 1, i) for i in range(size - 1)]
 
     sent_up, sent_down = call(
-        send_body, [((members, rim, width), BF16)] * 2, latent, send_rows
+        send_body, [((members, rim, width), BF16)] * 2, latent, send_rows,
+        apart=(0, 1),
+        scratch=[
+            pltpu.VMEM(latent.shape, BF16), pltpu.VMEM(send_rows.shape, jnp.int32),
+            pltpu.SemaphoreType.DMA((2,)),
+        ],
     )
     low = lax.ppermute(sent_up, SPACE, up)
     high = lax.ppermute(sent_down, SPACE, down)
@@ -577,6 +642,13 @@
         local_body,
         [((members, nodes, width), BF16), ((rows, width), BF16), ((rows, 3 * width), BF16)],
         latent, member_noise, w_noise, w_qkv,
+        apart=(0, 1, 2, 3),
+        scratch=[
+            pltpu.VMEM(latent.shape, BF16), pltpu.VMEM(member_noise.shape, F32),
+            pltpu.VMEM(w_noise.shape, F32),
+            pltpu.VMEM((width, 3 * width), BF16), pltpu.VMEM((rows, 3 * width), F32),
+            pltpu.SemaphoreType.DMA((6,)),
+        ],
         flops=2 * rows * width * 3 * width,
     )
     normed_all, proj_rim, attended, stored, hidden, slope, forecast, table = call(
@@ -589,10 +661,30 @@
         ],
         own, normed, proj, low, high, member_noise, w_noise, w_qkv, w_out, w_hid, w_pred,
         neighbours, degree, dec_nodes,
+        apart=(7, 8, 9),
+        scratch=[
+            pltpu.VMEM((width, 2 * width), BF16), pltpu.VMEM((width, width), BF16),
+            pltpu.VMEM((width, width), BF16), pltpu.SemaphoreType.DMA((3,)),
+        ],
         flops=3 * 10**9,
     )
     gathered = gather_members(forecast)
-    packed_shape = (CHUNKS, 16, TILE * (SLOTS_A + SLOTS_B))
+    planes, levels = ("x", "y"), ("zlo", "zhi")
+    spots = lax.axis_size(planes)
+    tile, rest_tile = (16, SPLIT), (16, REST)
+    chunk, rest_chunk = (16 // spots,) + tile, (16 // spots,) + rest_tile
+    ring = [2 * (z % 2) + z // 2 for z in range(4)]
+
+    def shifted(pieces):
+        moved = []
+        for shift, piece in enumerate(pieces, 1):
+            pairs = [(ring[z], ring[(z + shift) % 4]) for z in range(4)]
+            moved.append(lax.ppermute(piece, levels, pairs))
+        return moved
+
+    def swapped(a):
+        return lax.all_to_all(a, planes, 0, 0, tiled=True)
+
     first_shape = (CHUNKS, 16, TILE * SLOTS_A)
     swap = [(0, 1), (1, 0)]
     normed_theirs = lax.ppermute(normed_all, "core", swap)
@@ -613,6 +705,11 @@
         flops=6 * 10**9,
     )
     came = lax.ppermute(send, "core", swap)
+    tall = (4, 16) + rest_tile
+    stacks = call(
+        pack_first_body, [((16,) + rest_tile, BF16)] * 4, keep.reshape(tall), came.reshape(tall)
+    )
+    stacks = [stacks[0]] + shifted(stacks[1:])
     d_proj, d_rim, d_send = call(
         attend_back_body,
         [
@@ -633,66 +730,55 @@
         own, low, high, member_noise, w_noise, w_qkv, d_proj, d_rim, d_updated,
         flops=2 * 10**9,
     )
-    planes, levels = ("x", "y"), ("zlo", "zhi")
-    spots = lax.axis_size(planes)
-    tile = (16, HALF)
-    chunk = (16 // spots,) + tile
-    ring = [2 * (z % 2) + z // 2 for z in range(4)]
-
-    def shifted(pieces):
-        moved = []
-        for shift, piece in enumerate(pieces, 1):
-            pairs = [(ring[z], ring[(z + shift) % 4]) for z in range(4)]
-            moved.append(lax.ppermute(piece, levels, pairs))
-        return moved
-
-    def swapped(a):
-        return lax.all_to_all(a, planes, 0, 0, tiled=True)
-
-    plane, *stacks = call(
+    (plane,) = call(
         pack_body,
-        [((16, 4) + tile, BF16)] + [((16,) + tile, BF16)] * 4,
-        normed_all, normed_theirs, d_proj, d_rim, d_theirs, keep, came, g_noise, loss,
+        [((16, 4) + tile, BF16)],
+        normed_all, normed_theirs, d_proj, d_rim, d_theirs, g_noise, loss,
         scratch=[
-            pltpu.VMEM((width, 3 * width // 2), BF16), pltpu.VMEM((4, 16) + tile, BF16),
-        ],
+            pltpu.VMEM((width, 3 * width // 2), BF16), pltpu.VMEM((16, 4) + tile, BF16),
+            pltpu.SemaphoreType.DMA((4,)),
+        ],
+        far=(0,),
         flops=2 * 10**9,
     )
+    plane, d_low, d_high = lax.optimization_barrier((plane, d_low, d_high))
     from_next = lax.ppermute(d_low, SPACE, down)
     from_prev = lax.ppermute(d_high, SPACE, up)
-    plane, from_next, from_prev = lax.optimization_barrier((plane, from_next, from_prev))
-    stacks = [stacks[0]] + shifted(stacks[1:])
     plane = swapped(plane)
-    *columns, stack = call(
-        first_sum_body,
-        [(chunk, BF16)] * 4 + [((16,) + tile, BF16)],
-        plane.reshape((spots, 16 // spots, 4) + tile), *stacks,
+    stacks, from_next, from_prev = lax.optimization_barrier((stacks, from_next, from_prev))
+    (stack,) = call(sum_stack_body, [((16,) + rest_tile, BF16)], *stacks)
+    columns = call(
+        sum_plane_body,
+        [(chunk, BF16)] * 4,
+        plane.reshape((spots, 16 // spots, 4) + tile),
         scratch=[pltpu.VMEM((4,) + chunk, BF16)],
     )
     columns = [columns[0]] + shifted(columns[1:])
     stack = swapped(stack)
     column, stack = call(
         second_sum_body,
-        [(chunk, BF16), ((spots,) + chunk, BF16)],
-        *columns, stack.reshape((spots,) + chunk),
+        [(chunk, BF16), ((spots,) + rest_chunk, BF16)],
+        *columns, stack.reshape((spots,) + rest_chunk),
     )
     columns = [column] + shifted([column] * 3)
-    stack = swapped(stack.reshape((16,) + tile))
+    stack = swapped(stack.reshape((16,) + rest_tile))
+    (d_latent,) = call(
+        join_body, [((members, width, nodes), F32)], d_own, send_rows, from_next, from_prev
+    )
+    columns, stack, d_latent = lax.optimization_barrier((columns, stack, d_latent))
     (plane,) = call(
         spread_body, [((spots, 16 // spots, 4) + tile, BF16)], *columns,
-        scratch=[pltpu.VMEM((4,) + chunk, BF16)],
+        far=(0,),
+        scratch=[pltpu.VMEM((4,) + chunk, BF16), pltpu.SemaphoreType.DMA((16,))],
     )
     stacks = [stack] + shifted([stack] * 3)
+    other_stacks = [lax.ppermute(a, "core", swap) for a in stacks]
+    g_hid, g_out, g_pred = unpack_first(stacks, other_stacks, width, channels)
     plane = swapped(plane.reshape((16, 4) + tile))
-    other_stacks = [lax.ppermute(a, "core", swap) for a in stacks]
+    plane, g_hid, g_out, g_pred = lax.optimization_barrier((plane, g_hid, g_out, g_pred))
     other_plane = lax.ppermute(plane, "core", swap)
-    (d_latent,) = call(
-        join_body, [((members, width, nodes), F32)], d_own, send_rows, from_next, from_prev
-    )
-    mine = unpack(plane, stacks, width, channels)
-    g_qkv, g_hid, g_out, g_pred, g_noise, mean = unpack(
-        other_plane, other_stacks, width, channels, counts[None, :], mine
-    )
+    mine = unpack(plane, width)
+    g_qkv, g_noise, mean = unpack(other_plane, width, channels, counts[None, :], mine)
     return mean.reshape(()), d_latent, g_qkv, g_out, g_noise, g_hid, g_pred
 
 

time: 194 us -> 153 us (0.79)
  blocking collectives: 37.6 us -> 0 us
  local copies, waits for them, and re-layouts: 16.6 us -> 0.09 us
  starting transfers between devices: 49.7 us -> 65.5 us
  waiting for transfers between devices: 52.2 us -> 43.2 us
  Pallas kernels: 33.2 us -> 41 us
    all_to_all x2 -> x0, blocking collectives: 37.6 us -> none  [swapped(): return lax.all_to_all(a, planes, 0, 0, tiled=True)]
    ppermute x12, waiting for transfers between devices: 42.7 us -> 16 us  [shifted(): moved.append(lax.ppermute(piece, levels, pairs))]
    unnamed x66 -> x30, local copies, waits for them, and re-layouts: 16.6 us -> 0.09 us
    all_to_all x2 -> x4, starting transfers between devices: 13.6 us -> 26.6 us  [swapped(): return lax.all_to_all(a, planes, 0, 0, tiled=True)]
    pallas_call x11 -> x13, Pallas kernels: 25.6 us -> 32.3 us  [call(): pl.pallas_call(body, out_shape=out_shape, in_specs=[SMEM if i in smem els...]
    ppermute x1, waiting for transfers between devices: 0.01 us -> 6.24 us  [on_device(): from_next = lax.ppermute(d_low, SPACE, down)]
    ppermute x1, waiting for transfers between devices: 0.01 us -> 3.24 us  [on_device(): came = lax.ppermute(send, 'core', swap)]
    ppermute x1, starting transfers between devices: 2.6 us -> 5.33 us  [on_device(): from_next = lax.ppermute(d_low, SPACE, down)]
  transfers between devices with their start and end apart: 29 -> 31, of which waited for: 13 -> 17; matrix products, arithmetic and copies ran while one was open for 0% -> 0% of each run, Pallas kernels for 8% -> 9%
where the time goes in v4:
time: 153 us; the launch traced here: 151 us
  starting transfers between devices  65.5 us (43%)
  waiting for transfers between devices  43.2 us (28%)
  Pallas kernels  41 us (27%)
    pallas_call x13, Pallas kernels, call(): pl.pallas_call(body, out_shape=out_shape, in_specs=[SMEM if i in smem els...  32.3 us
    all_to_all x4, starting transfers between devices, swapped(): return lax.all_to_all(a, planes, 0, 0, tiled=True)  26.6 us
    ppermute x12, starting transfers between devices, shifted(): moved.append(lax.ppermute(piece, levels, pairs))  18 us
    ppermute x12, waiting for transfers between devices, shifted(): moved.append(lax.ppermute(piece, levels, pairs))  16 us
    ppermute x1, waiting for transfers between devices, gather_members(): far = lax.ppermute(forecast, 'zhi', swap)  7.84 us
    ppermute x1, waiting for transfers between devices, on_device(): from_next = lax.ppermute(d_low, SPACE, down)  6.24 us
    pallas_call x2, Pallas kernels, unpack(): pl.pallas_call(body, out_shape=[jax.ShapeDtypeStruct(shape, F32) for shap...  5.6 us
    ppermute x1, starting transfers between devices, on_device(): high = lax.ppermute(sent_down, SPACE, down)  5.5 us
  transfers between devices with their start and end apart: 31, of which 17 were waited for; matrix products, arithmetic and copies ran while one was open for 0% of the time, Pallas kernels for 9%

profile of v4, /device:TPU:2, one launch (start us, length us, event | category | flops | bytes accessed | tf_op | source)
XLA Modules:
  0.0 151.0 jit_solution(5663622141217027540)
XLA Ops:
  2.0 3.5 %collective-permute-start = (bf16[2,16,768]{2,1,0:T(8,128)(2,1)S(1)}, bf16[2,16,768]{2,1,0:T(8,128)(2,1)S(1)}, u32[]{:S(2)}, u32[]{:S(2)}) collective-permute-start(bf16[2,16,768]{2,1,0:T(8,128)(2,1)S(1)} %get-tuple-element.73), channel_id=1, source_target_pairs={{0,4},{4,8},{8,12},{12,16},{16,20},{20,24},{24,28},{28,32},{32,36}... | collective-permute-start | bytes 147464 | tf_op jit(solution)/shard_map/ppermute | solution.py:639
  5.6 5.5 %collective-permute-start.1 = (bf16[2,16,768]{2,1,0:T(8,128)(2,1)S(1)}, bf16[2,16,768]{2,1,0:T(8,128)(2,1)S(1)}, u32[]{:S(2)}, u32[]{:S(2)}) collective-permute-start(bf16[2,16,768]{2,1,0:T(8,128)(2,1)S(1)} %get-tuple-element.74), channel_id=1, source_target_pairs={{4,0},{8,4},{12,8},{16,12},{20,16},{24,20},{28,24},{32,28},{36,32}... | collective-permute-start | bytes 147464 | tf_op jit(solution)/shard_map/ppermute | solution.py:640
  11.1 2.9 %shard_map.180 = (bf16[2,128,768]{2,1,0:T(8,128)(2,1)S(1)}, bf16[256,768]{1,0:T(8,128)(2,1)S(1)}, bf16[256,2304]{1,0:T(8,128)(2,1)S(1)}) custom-call(bf16[2,768,128]{2,1,0:T(8,128)(2,1)} %latent_far.3, f32[2,32]{1,0:T(2,128)} %noise.3, f32[32,768]{1,0:T(8,128)} %w_noise.3, bf16[768,2304]{1,0:T(8,128)(2,1)} %w_qkv.5), custom_call_target="tpu_custom_call" | custom-call | flops 905969664 | bytes 4030720 | tf_op jit(solution)/shard_map/pallas_call | solution.py:46
  14.1 7.9 %shard_map.182 = (bf16[320,768]{1,0:T(8,128)(2,1)S(1)}, bf16[64,1536]{1,0:T(8,128)(2,1)S(1)}, bf16[256,768]{1,0:T(8,128)(2,1)S(1)}, bf16[256,768]{1,0:T(8,128)(2...) custom-call(bf16[2,128,768]{2,1,0:T(8,128)(2,1)S(1)} %get-tuple-elem, ...), custom_call_target="tpu_custom_call" | custom-call | flops 3000000000 | bytes 8205568 | tf_op jit(solution)/shard_map/pallas_call | solution.py:46
  22.0 4.0 %collective-permute-start.4 = (bf16[2,83,1024]{2,1,0:T(8,128)(2,1)S(1)}, bf16[2,83,1024]{2,1,0:T(8,128)(2,1)S(1)}, u32[]{:S(2)}, u32[]{:S(2)}) collective-permute-start(bf16[2,83,1024]{2,1,0:T(8,128)(2,1)S(1)} %get-tuple-element.77.mine), channel_id=1, source_target_pairs={{0,2},{2,0},{1,3},{3,1},{4,6},{6,4},{5,7},{7,5},{8,10},{10,8},{9,1... | collective-permute-start | bytes 1019912 | tf_op jit(solution)/shard_map/ppermute | solution.py:787
  26.0 7.8 %collective-permute-done.4.rest_1_ = bf16[2,83,1024]{2,1,0:T(8,128)(2,1)S(1)} collective-permute-done((bf16[2,83,1024]{2,1,0:T(8,128)(2,1)S(1)}, bf16[2,83,1024]{2,1,0:T(8,128)(2,1)S(1)}, u32[]{:S(2)}, u32[]{:S(2)}) %collective-permute-start.4) | collective-permute-done | bytes 340000 | tf_op jit(solution)/shard_map/ppermute | solution.py:787
  35.5 6.9 %shard_map.183 = (bf16[256,768]{1,0:T(8,128)(2,1)S(1)}, bf16[256,768]{1,0:T(8,128)(2,1)S(1)}, bf16[64,16,640]{2,1,0:T(8,128)(2,1)S(1)}, bf16[64,16,640]{2,1,0:T(8,128)(2,1)S(1)}, bf16[16,128]{1,0:T(8,128)(2,1)S(1)}) custom-call(s32[32]{0:T(128)S(1)} %copy-done.6, bf16[2,83,1024]{2,1,0:T(8,128)(2,1)S(1)} %get-tuple-element.77.mine, ...), custom_call_target="tpu_custom_call" | custom-call | flops 6000000000 | bytes 11526784 | tf_op jit(solution)/shard_map/pallas_call | solution.py:46
  42.4 2.7 %shard_map.184 = (bf16[2,256,1152]{2,1,0:T(8,128)(2,1)S(1)}, bf16[2,64,768]{2,1,0:T(8,128)(2,1)S(1)}, bf16[320,1152]{1,0:T(8,128)(2,1)S(1)}) custom-call(bf16[256,2304]{1,0:T(8,128)(2,1)S(1)} %get-tuple-element.72.proj, bf16[64,1536]{1,0:T(8,128)(2,1)S(1)} %get-tuple-element.76.proj_rim, s32[8,128]{1,0:T(8,128)S(1)} %copy-done.13, s32[1,128]{1,0:T(1,128)S(1)} %bitcast.15, ...), custom_call_target="tpu_custom_call" | custom-call | flops 2000000000 | bytes 1774080 | tf_op jit(solution)/shard_map/pallas_call | solution.py:46
  48.4 3.0 %shard_map.186 = bf16[16,4,16,896]{3,2,1,0:T(8,128)(2,1)} custom-call(bf16[320,768]{1,0:T(8,128)(2,1)S(1)} %get-tuple-element.75.normed, bf16[320,768]{1,0:T(8,128)(2,1)S(1)} %collective-permute-done.2.normed_theirs, bf16[2,256,1152]{2,1,0:T(8,128)(2,1)S(1)} %get-tuple-element.84.d_proj, bf16[2,64,768]{2,1,0:T(8,128)(2,1)S(1)} %get-tuple-element.85.d_rim, ...), custom_call_target="tpu_custom_call" | custom-call | flops 2000000000 | bytes 3149824 | tf_op jit(solution)/shard_map/pallas_call | solution.py:46
  51.4 5.9 %all-to-all-start = ((bf16[16,4,16,896]{3,2,1,0:T(8,128)(2,1)}), bf16[16,4,16,896]{3,2,1,0:T(8,128)(2,1)S(1)}, u32[]{:S(2)}, u32[]{:S(2)}) async-start(bf16[16,4,16,896]{3,2,1,0:T(8,128)(2,1)} %shard_map.186), calls=%async_computation | async-start | bytes 3670016 | tf_op jit(solution)/shard_map/all_to_all | solution.py:686
  57.3 3.2 %collective-permute-done.10 = bf16[64,16,640]{2,1,0:T(8,128)(2,1)S(1)} collective-permute-done((bf16[64,16,640]{2,1,0:T(8,128)(2,1)}, bf16[64,16,640]{2,1,0:T(8,128)(2,1)S(1)}, u32[]{:S(2)}, u32[]{:S(2)}) %collective-permute-start.10) | collective-permute-done | bytes 1310752 | tf_op jit(solution)/shard_map/ppermute | solution.py:707
  62.2 3.9 %collective-permute-start.12 = (bf16[16,16,640]{2,1,0:T(8,128)(2,1)S(1)}, bf16[16,16,640]{2,1,0:T(8,128)(2,1)S(1)}, u32[]{:S(2)}, u32[]{:S(2)}) collective-permute-start(bf16[16,16,640]{2,1,0:T(8,128)(2,1)S(1)} %get-tuple-element.101), channel_id=1, source_target_pairs={{0,2},{16,18},{2,0},{18,16},{1,3},{17,19},{3,1},{19,17},{4,6},{20,... | collective-permute-start | bytes 983048 | tf_op jit(solution)/shard_map/ppermute | solution.py:682
  66.8 5.3 %collective-permute-start.14 = (bf16[2,16,768]{2,1,0:T(8,128)(2,1)S(1)}, bf16[2,16,768]{2,1,0:T(8,128)(2,1)S(1)}, u32[]{:S(2)}, u32[]{:S(2)}) collective-permute-start(bf16[2,16,768]{2,1,0:T(8,128)(2,1)S(1)} %get-tuple-element.103), channel_id=1, source_target_pairs={{4,0},{8,4},{12,8},{16,12},{20,16},{24,20},{28,24},{32,28},{36,32}... | collective-permute-start | bytes 147464 | tf_op jit(solution)/shard_map/ppermute | solution.py:745
  74.1 6.2 %collective-permute-done.14.from_next = bf16[2,16,768]{2,1,0:T(8,128)(2,1)S(1)} collective-permute-done((bf16[2,16,768]{2,1,0:T(8,128)(2,1)S(1)}, bf16[2,16,768]{2,1,0:T(8,128)(2,1)S(1)}, u32[]{:S(2)}, u32[]{:S(2)}) %collective-permute-start.14) | collective-permute-done | bytes 49184 | tf_op jit(solution)/shard_map/ppermute | solution.py:745
  83.8 6.4 %all-to-all-start.1 = ((bf16[16,16,640]{2,1,0:T(8,128)(2,1)}), bf16[16,16,640]{2,1,0:T(8,128)(2,1)S(1)}, u32[]{:S(2)}, u32[]{:S(2)}) async-start(bf16[16,16,640]{2,1,0:T(8,128)(2,1)} %shard_map.189), calls=%async_computation.1 | async-start | bytes 655360 | tf_op jit(solution)/shard_map/all_to_all | solution.py:686
  90.6 2.8 %collective-permute-start.7 = (bf16[1,16,896]{2,1,0:T(8,128)(2,1)S(1)}, bf16[1,16,896]{2,1,0:T(8,128)(2,1)S(1)}, u32[]{:S(2)}, u32[]{:S(2)}) collective-permute-start(bf16[1,16,896]{2,1,0:T(8,128)(2,1)S(1)} %get-tuple-element.94), channel_id=1, source_target_pairs={{0,16},{16,2},{2,18},{18,0},{1,17},{17,3},{3,19},{19,1},{4,20},{20... | collective-permute-start | bytes 86024 | tf_op jit(solution)/shard_map/ppermute | solution.py:682
  93.4 3.2 %collective-permute-start.8 = (bf16[1,16,896]{2,1,0:T(8,128)(2,1)S(1)}, bf16[1,16,896]{2,1,0:T(8,128)(2,1)S(1)}, u32[]{:S(2)}, u32[]{:S(2)}) collective-permute-start(bf16[1,16,896]{2,1,0:T(8,128)(2,1)S(1)} %get-tuple-element.95), channel_id=1, source_target_pairs={{0,2},{16,18},{2,0},{18,16},{1,3},{17,19},{3,1},{19,17},{4,6},{20,... | collective-permute-start | bytes 86024 | tf_op jit(solution)/shard_map/ppermute | solution.py:682
  101.2 7.2 %all-to-all-start.2 = ((bf16[16,16,640]{2,1,0:T(8,128)(2,1)}), bf16[16,16,640]{2,1,0:T(8,128)(2,1)S(1)}, u32[]{:S(2)}, u32[]{:S(2)}) async-start(bf16[16,16,640]{2,1,0:T(8,128)(2,1)} %bitcast.5), calls=%async_computation.2 | async-start | bytes 655360 | tf_op jit(solution)/shard_map/all_to_all | solution.py:686
  116.9 7.1 %all-to-all-start.3 = ((bf16[16,4,16,896]{3,2,1,0:T(8,128)(2,1)}), bf16[16,4,16,896]{3,2,1,0:T(8,128)(2,1)S(1)}, u32[]{:S(2)}, u32[]{:S(2)}) async-start(bf16[16,4,16,896]{3,2,1,0:T(8,128)(2,1)} %bitcast.16), calls=%async_computation.3 | async-start | bytes 3670016 | tf_op jit(solution)/shard_map/all_to_all | solution.py:686
  127.1 4.4 %collective-permute-done.21.refs_3_ = bf16[16,16,640]{2,1,0:T(8,128)(2,1)S(1)} collective-permute-done((bf16[16,16,640]{2,1,0:T(8,128)(2,1)S(1)}, bf16[16,16,640]{2,1,0:T(8,128)(2,1)S(1)}, u32[]{:S(2)}, u32[]{:S(2)}) %collective-permute-start.21) | collective-permute-done | bytes 327712 | tf_op jit(solution)/shard_map/ppermute | solution.py:682
  131.6 2.8 %collective-permute-done.20.refs_2_ = bf16[16,16,640]{2,1,0:T(8,128)(2,1)S(1)} collective-permute-done((bf16[16,16,640]{2,1,0:T(8,128)(2,1)S(1)}, bf16[16,16,640]{2,1,0:T(8,128)(2,1)S(1)}, u32[]{:S(2)}, u32[]{:S(2)}) %collective-permute-start.20) | collective-permute-done | bytes 327712 | tf_op jit(solution)/shard_map/ppermute | solution.py:682
  134.3 3.4 %collective-permute-done.19.refs_1_ = bf16[16,16,640]{2,1,0:T(8,128)(2,1)S(1)} collective-permute-done((bf16[16,16,640]{2,1,0:T(8,128)(2,1)S(1)}, bf16[16,16,640]{2,1,0:T(8,128)(2,1)S(1)}, u32[]{:S(2)}, u32[]{:S(2)}) %collective-permute-start.19) | collective-permute-done | bytes 327712 | tf_op jit(solution)/shard_map/ppermute | solution.py:682
  139.4 3.1 %shard_map.193 = (f32[768,768]{1,0:T(8,128)}, f32[768,768]{1,0:T(8,128)}, f32[83,768]{1,0:T(8,128)}) custom-call(bf16[16,16,640]{2,1,0:T(8,128)(2,1)S(1)} %all-to-all-done.2.refs_0_, bf16[16,16,640]{2,1,0:T(8,128)(2,1)S(1)} %collective-permute-done.19.refs_1_, bf16[16,16,640]{2,1,0:T(8,128)(2,1)S(1)} %collective-permute-done.20.refs_2_, ...), custom_call_target="tpu_custom_call" | custom-call | bytes 8000000 | tf_op jit(solution)/shard_map/pallas_call | solution.py:591
  147.6 3.1 %shard_map.195 = (f32[768,2304]{1,0:T(8,128)}, f32[32,768]{1,0:T(8,128)}, f32[1,1]{1,0:T(1,128)}) custom-call(bf16[16,4,16,896]{3,2,1,0:T(8,128)(2,1)S(1)} %collective-permute-done.26.plane, s32[1,32]{1,0:T(1,128)S(1)} %bitcast.13, f32[768,2304]{1,0:T(8,128)} %get-tuple-element.123._qkv, ...), custom_call_target="tpu_custom_call", output_to_operand_aliasing={{0}: (2, {})} | custom-call | bytes 6000000 | tf_op jit(solution)/shard_map/pallas_call | solution.py:574
  (84 shorter events, 37.4 us)
Async XLA Ops:
  2.0 12.0 %collective-permute-start = (bf16[2,16,768]{2,1,0:T(8,128)(2,1)S(1)}, bf16[2,16,768]{2,1,0:T(8,128)(2,1)S(1)}, u32[]{:S(2)}, u32[]{:S(2)}) collective-permute-start(bf16[2,16,768]{2,1,0:T(8,128)(2,1)S(1)} %get-tuple-element.73), channel_id=1, source_target_pairs={{0,4},{4,8},{8,12},{12,16},{16,20},{20,24},{24,28},{28,32},{32,36}... | collective-permute-start | bytes 147464 | tf_op jit(solution)/shard_map/ppermute | solution.py:639
  5.6 8.5 %collective-permute-start.1 = (bf16[2,16,768]{2,1,0:T(8,128)(2,1)S(1)}, bf16[2,16,768]{2,1,0:T(8,128)(2,1)S(1)}, u32[]{:S(2)}, u32[]{:S(2)}) collective-permute-start(bf16[2,16,768]{2,1,0:T(8,128)(2,1)S(1)} %get-tuple-element.74), channel_id=1, source_target_pairs={{4,0},{8,4},{12,8},{16,12},{20,16},{24,20},{28,24},{32,28},{36,32}... | collective-permute-start | bytes 147464 | tf_op jit(solution)/shard_map/ppermute | solution.py:640
  22.0 11.8 %collective-permute-start.4 = (bf16[2,83,1024]{2,1,0:T(8,128)(2,1)S(1)}, bf16[2,83,1024]{2,1,0:T(8,128)(2,1)S(1)}, u32[]{:S(2)}, u32[]{:S(2)}) collective-permute-start(bf16[2,83,1024]{2,1,0:T(8,128)(2,1)S(1)} %get-tuple-element.77.mine), channel_id=1, source_target_pairs={{0,2},{2,0},{1,3},{3,1},{4,6},{6,4},{5,7},{7,5},{8,10},{10,8},{9,1... | collective-permute-start | bytes 1019912 | tf_op jit(solution)/shard_map/ppermute | solution.py:787
  26.0 7.9 %collective-permute-start.3 = (bf16[2,83,1024]{2,1,0:T(8,128)(2,1)S(1)}, bf16[2,83,1024]{2,1,0:T(8,128)(2,1)S(1)}, u32[]{:S(2)}, u32[]{:S(2)}) collective-permute-start(bf16[2,83,1024]{2,1,0:T(8,128)(2,1)S(1)} %get-tuple-element.77.mine), channel_id=1, source_target_pairs={{0,1},{1,0},{2,3},{3,2},{4,5},{5,4},{6,7},{7,6},{8,9},{9,8},{10,11... | collective-permute-start | bytes 1019912 | tf_op jit(solution)/shard_map/ppermute | solution.py:788
  51.4 32.4 %all-to-all-start = ((bf16[16,4,16,896]{3,2,1,0:T(8,128)(2,1)}), bf16[16,4,16,896]{3,2,1,0:T(8,128)(2,1)S(1)}, u32[]{:S(2)}, u32[]{:S(2)}) async-start(bf16[16,4,16,896]{3,2,1,0:T(8,128)(2,1)} %shard_map.186), calls=%async_computation | async-start | bytes 3670016 | tf_op jit(solution)/shard_map/all_to_all | solution.py:686
  60.9 22.0 %collective-permute-start.11 = (bf16[16,16,640]{2,1,0:T(8,128)(2,1)S(1)}, bf16[16,16,640]{2,1,0:T(8,128)(2,1)S(1)}, u32[]{:S(2)}, u32[]{:S(2)}) collective-permute-start(bf16[16,16,640]{2,1,0:T(8,128)(2,1)S(1)} %get-tuple-element.100), channel_id=1, source_target_pairs={{0,16},{16,2},{2,18},{18,0},{1,17},{17,3},{3,19},{19,1},{4,20},{20... | collective-permute-start | bytes 983048 | tf_op jit(solution)/shard_map/ppermute | solution.py:682
  62.2 20.7 %collective-permute-start.12 = (bf16[16,16,640]{2,1,0:T(8,128)(2,1)S(1)}, bf16[16,16,640]{2,1,0:T(8,128)(2,1)S(1)}, u32[]{:S(2)}, u32[]{:S(2)}) collective-permute-start(bf16[16,16,640]{2,1,0:T(8,128)(2,1)S(1)} %get-tuple-element.101), channel_id=1, source_target_pairs={{0,2},{16,18},{2,0},{18,16},{1,3},{17,19},{3,1},{19,17},{4,6},{20,... | collective-permute-start | bytes 983048 | tf_op jit(solution)/shard_map/ppermute | solution.py:682
  66.1 16.8 %collective-permute-start.13 = (bf16[16,16,640]{2,1,0:T(8,128)(2,1)S(1)}, bf16[16,16,640]{2,1,0:T(8,128)(2,1)S(1)}, u32[]{:S(2)}, u32[]{:S(2)}) collective-permute-start(bf16[16,16,640]{2,1,0:T(8,128)(2,1)S(1)} %get-tuple-element.102), channel_id=1, source_target_pairs={{0,18},{16,0},{2,16},{18,2},{1,19},{17,1},{3,17},{19,3},{4,22},{20... | collective-permute-start | bytes 983048 | tf_op jit(solution)/shard_map/ppermute | solution.py:682
  66.8 13.5 %collective-permute-start.14 = (bf16[2,16,768]{2,1,0:T(8,128)(2,1)S(1)}, bf16[2,16,768]{2,1,0:T(8,128)(2,1)S(1)}, u32[]{:S(2)}, u32[]{:S(2)}) collective-permute-start(bf16[2,16,768]{2,1,0:T(8,128)(2,1)S(1)} %get-tuple-element.103), channel_id=1, source_target_pairs={{4,0},{8,4},{12,8},{16,12},{20,16},{24,20},{28,24},{32,28},{36,32}... | collective-permute-start | bytes 147464 | tf_op jit(solution)/shard_map/ppermute | solution.py:745
  72.1 10.8 %collective-permute-start.15 = (bf16[2,16,768]{2,1,0:T(8,128)(2,1)S(1)}, bf16[2,16,768]{2,1,0:T(8,128)(2,1)S(1)}, u32[]{:S(2)}, u32[]{:S(2)}) collective-permute-start(bf16[2,16,768]{2,1,0:T(8,128)(2,1)S(1)} %get-tuple-element.104), channel_id=1, source_target_pairs={{0,4},{4,8},{8,12},{12,16},{16,20},{20,24},{24,28},{28,32},{32,36}... | collective-permute-start | bytes 147464 | tf_op jit(solution)/shard_map/ppermute | solution.py:746
  83.8 13.9 %all-to-all-start.1 = ((bf16[16,16,640]{2,1,0:T(8,128)(2,1)}), bf16[16,16,640]{2,1,0:T(8,128)(2,1)S(1)}, u32[]{:S(2)}, u32[]{:S(2)}) async-start(bf16[16,16,640]{2,1,0:T(8,128)(2,1)} %shard_map.189), calls=%async_computation.1 | async-start | bytes 655360 | tf_op jit(solution)/shard_map/all_to_all | solution.py:686
  90.6 7.2 %collective-permute-start.7 = (bf16[1,16,896]{2,1,0:T(8,128)(2,1)S(1)}, bf16[1,16,896]{2,1,0:T(8,128)(2,1)S(1)}, u32[]{:S(2)}, u32[]{:S(2)}) collective-permute-start(bf16[1,16,896]{2,1,0:T(8,128)(2,1)S(1)} %get-tuple-element.94), channel_id=1, source_target_pairs={{0,16},{16,2},{2,18},{18,0},{1,17},{17,3},{3,19},{19,1},{4,20},{20... | collective-permute-start | bytes 86024 | tf_op jit(solution)/shard_map/ppermute | solution.py:682
  93.4 5.4 %collective-permute-start.8 = (bf16[1,16,896]{2,1,0:T(8,128)(2,1)S(1)}, bf16[1,16,896]{2,1,0:T(8,128)(2,1)S(1)}, u32[]{:S(2)}, u32[]{:S(2)}) collective-permute-start(bf16[1,16,896]{2,1,0:T(8,128)(2,1)S(1)} %get-tuple-element.95), channel_id=1, source_target_pairs={{0,2},{16,18},{2,0},{18,16},{1,3},{17,19},{3,1},{19,17},{4,6},{20,... | collective-permute-start | bytes 86024 | tf_op jit(solution)/shard_map/ppermute | solution.py:682
  96.6 3.9 %collective-permute-start.9 = (bf16[1,16,896]{2,1,0:T(8,128)(2,1)S(1)}, bf16[1,16,896]{2,1,0:T(8,128)(2,1)S(1)}, u32[]{:S(2)}, u32[]{:S(2)}) collective-permute-start(bf16[1,16,896]{2,1,0:T(8,128)(2,1)S(1)} %get-tuple-element.96), channel_id=1, source_target_pairs={{0,18},{16,0},{2,16},{18,2},{1,19},{17,1},{3,17},{19,3},{4,22},{20... | collective-permute-start | bytes 86024 | tf_op jit(solution)/shard_map/ppermute | solution.py:682
  101.2 14.2 %all-to-all-start.2 = ((bf16[16,16,640]{2,1,0:T(8,128)(2,1)}), bf16[16,16,640]{2,1,0:T(8,128)(2,1)S(1)}, u32[]{:S(2)}, u32[]{:S(2)}) async-start(bf16[16,16,640]{2,1,0:T(8,128)(2,1)} %bitcast.5), calls=%async_computation.2 | async-start | bytes 655360 | tf_op jit(solution)/shard_map/all_to_all | solution.py:686
  108.5 4.2 %collective-permute-start.18 = (bf16[1,16,896]{2,1,0:T(8,128)(2,1)S(1)}, bf16[1,16,896]{2,1,0:T(8,128)(2,1)S(1)}, u32[]{:S(2)}, u32[]{:S(2)}) collective-permute-start(bf16[1,16,896]{2,1,0:T(8,128)(2,1)S(1)} %get-tuple-element.114.one), channel_id=1, source_target_pairs={{0,18},{16,0},{2,16},{18,2},{1,19},{17,1},{3,17},{19,3},{4,22},{20... | collective-permute-start | bytes 86024 | tf_op jit(solution)/shard_map/ppermute | solution.py:682
  109.7 5.4 %collective-permute-start.17 = (bf16[1,16,896]{2,1,0:T(8,128)(2,1)S(1)}, bf16[1,16,896]{2,1,0:T(8,128)(2,1)S(1)}, u32[]{:S(2)}, u32[]{:S(2)}) collective-permute-start(bf16[1,16,896]{2,1,0:T(8,128)(2,1)S(1)} %get-tuple-element.114.one), channel_id=1, source_target_pairs={{0,2},{16,18},{2,0},{18,16},{1,3},{17,19},{3,1},{19,17},{4,6},{20,... | collective-permute-start | bytes 86024 | tf_op jit(solution)/shard_map/ppermute | solution.py:682
  110.3 5.1 %collective-permute-start.16 = (bf16[1,16,896]{2,1,0:T(8,128)(2,1)S(1)}, bf16[1,16,896]{2,1,0:T(8,128)(2,1)S(1)}, u32[]{:S(2)}, u32[]{:S(2)}) collective-permute-start(bf16[1,16,896]{2,1,0:T(8,128)(2,1)S(1)} %get-tuple-element.114.one), channel_id=1, source_target_pairs={{0,16},{16,2},{2,18},{18,0},{1,17},{17,3},{3,19},{19,1},{4,20},{20... | collective-permute-start | bytes 86024 | tf_op jit(solution)/shard_map/ppermute | solution.py:682
  116.9 27.0 %all-to-all-start.3 = ((bf16[16,4,16,896]{3,2,1,0:T(8,128)(2,1)}), bf16[16,4,16,896]{3,2,1,0:T(8,128)(2,1)S(1)}, u32[]{:S(2)}, u32[]{:S(2)}) async-start(bf16[16,4,16,896]{3,2,1,0:T(8,128)(2,1)} %bitcast.16), calls=%async_computation.3 | async-start | bytes 3670016 | tf_op jit(solution)/shard_map/all_to_all | solution.py:686
  124.0 7.6 %collective-permute-start.21 = (bf16[16,16,640]{2,1,0:T(8,128)(2,1)S(1)}, bf16[16,16,640]{2,1,0:T(8,128)(2,1)S(1)}, u32[]{:S(2)}, u32[]{:S(2)}) collective-permute-start(bf16[16,16,640]{2,1,0:T(8,128)(2,1)S(1)} %all-to-all-done.2.refs_0_), channel_id=1, source_target_pairs={{0,18},{16,0},{2,16},{18,2},{1,19},{17,1},{3,17},{19,3},{4,22},{20... | collective-permute-start | bytes 983048 | tf_op jit(solution)/shard_map/ppermute | solution.py:682
  125.7 8.7 %collective-permute-start.20 = (bf16[16,16,640]{2,1,0:T(8,128)(2,1)S(1)}, bf16[16,16,640]{2,1,0:T(8,128)(2,1)S(1)}, u32[]{:S(2)}, u32[]{:S(2)}) collective-permute-start(bf16[16,16,640]{2,1,0:T(8,128)(2,1)S(1)} %all-to-all-done.2.refs_0_), channel_id=1, source_target_pairs={{0,2},{16,18},{2,0},{18,16},{1,3},{17,19},{3,1},{19,17},{4,6},{20,... | collective-permute-start | bytes 983048 | tf_op jit(solution)/shard_map/ppermute | solution.py:682
  126.6 11.2 %collective-permute-start.19 = (bf16[16,16,640]{2,1,0:T(8,128)(2,1)S(1)}, bf16[16,16,640]{2,1,0:T(8,128)(2,1)S(1)}, u32[]{:S(2)}, u32[]{:S(2)}) collective-permute-start(bf16[16,16,640]{2,1,0:T(8,128)(2,1)S(1)} %all-to-all-done.2.refs_0_), channel_id=1, source_target_pairs={{0,16},{16,2},{2,18},{18,0},{1,17},{17,3},{3,19},{19,1},{4,20},{20... | collective-permute-start | bytes 983048 | tf_op jit(solution)/shard_map/ppermute | solution.py:682
  127.1 10.6 %collective-permute-start.22 = (bf16[16,16,640]{2,1,0:T(8,128)(2,1)S(1)}, bf16[16,16,640]{2,1,0:T(8,128)(2,1)S(1)}, u32[]{:S(2)}, u32[]{:S(2)}) collective-permute-start(bf16[16,16,640]{2,1,0:T(8,128)(2,1)S(1)} %all-to-all-done.2.refs_0_), channel_id=1, source_target_pairs={{0,1},{1,0},{2,3},{3,2},{4,5},{5,4},{6,7},{7,6},{8,9},{9,8},{10,11... | collective-permute-start | bytes 983048 | tf_op jit(solution)/shard_map/ppermute | solution.py:775
  131.6 6.2 %collective-permute-start.25 = (bf16[16,16,640]{2,1,0:T(8,128)(2,1)S(1)}, bf16[16,16,640]{2,1,0:T(8,128)(2,1)S(1)}, u32[]{:S(2)}, u32[]{:S(2)}) collective-permute-start(bf16[16,16,640]{2,1,0:T(8,128)(2,1)S(1)} %collective-permute-done.21.refs_3_), channel_id=1, source_target_pairs={{0,1},{1,0},{2,3},{3,2},{4,5},{5,4},{6,7},{7,6},{8,9},{9,8},{10,11... | collective-permute-start | bytes 983048 | tf_op jit(solution)/shard_map/ppermute | solution.py:775
  (22 other events, 224.3 us)

commit v5 on v4

--- a/solution.py
+++ b/solution.py
@@ -103,8 +103,8 @@
 
 
 def local_body(
-    latent_far, noise_far, w_noise_far, w_qkv, own, normed, proj,
-    latent, noise, w_noise, held, total, sems,
+    latent_far, noise_far, w_noise_far, w_qkv, own, normed, proj, held,
+    latent, noise, w_noise, total, sems,
 ):
     thirds = [slice(r, r + 256) for r in range(0, held.shape[0], 256)]
     copies = fetch(
@@ -160,12 +160,9 @@
     own, normed, proj, low, high, noise, w_noise, w_qkv, w_out, w_hid, w_pred, nbr, degree,
     dec_nodes,
     normed_all, proj_rim, attended, stored, hidden, slope, forecast, table,
-    held_qkv, held_out, held_hid, sems,
+    held_out, held_hid, sems,
 ):
-    wide = own.shape[2]
-    copies = fetch(
-        (w_qkv.at[:, wide:], w_out, w_hid), (held_qkv, held_out, held_hid), sems
-    )
+    copies = fetch((w_out, w_hid), (held_out, held_hid), sems)
     members, nodes, width = own.shape
     rim = low.shape[1]
     gain = gains(noise[...], w_noise[...])
@@ -175,8 +172,7 @@
         at = members * nodes + 2 * rim * m
         normed_all[at : at + 2 * rim] = (hat * gain[m : m + 1]).astype(BF16)
     normed_all[: members * nodes] = normed[...]
-    copies[0].wait()
-    proj_rim[...] = mm(normed_all[members * nodes :], held_qkv[...]).astype(BF16)
+    proj_rim[...] = mm(normed_all[members * nodes :], w_qkv[:, width:]).astype(BF16)
     mask = slot_mask(nbr, degree, nodes + 2 * rim)
     for m in range(members):
         here = slice(m * nodes, (m + 1) * nodes)
@@ -190,13 +186,13 @@
             score = mm(key, proj[here, at[0]], NT) * HEAD**-0.5
             weight = (jax.nn.sigmoid(score) * mask).astype(BF16)
             attended[here, at[0]] = mm(weight, value, TN).astype(BF16)
-    copies[1].wait()
+    copies[0].wait()
     branch = mm(attended[...], held_out[...])
     for m in range(members):
         here = slice(m * nodes, (m + 1) * nodes)
         stored[here] = (own[m].astype(F32) + branch[here]).astype(BF16)
     table[...] = point_table(dec_nodes, nodes)
-    copies[2].wait()
+    copies[1].wait()
     mixed = mm(stored[...], held_hid[...]).astype(BF16)
     block = 256
     for m in range(members):
@@ -638,16 +634,18 @@
     )
     low = lax.ppermute(sent_up, SPACE, up)
     high = lax.ppermute(sent_down, SPACE, down)
-    own, normed, proj = call(
+    own, normed, proj, held_qkv = call(
         local_body,
-        [((members, nodes, width), BF16), ((rows, width), BF16), ((rows, 3 * width), BF16)],
+        [
+            ((members, nodes, width), BF16), ((rows, width), BF16), ((rows, 3 * width), BF16),
+            (w_qkv.shape, BF16),
+        ],
         latent, member_noise, w_noise, w_qkv,
         apart=(0, 1, 2, 3),
         scratch=[
             pltpu.VMEM(latent.shape, BF16), pltpu.VMEM(member_noise.shape, F32),
             pltpu.VMEM(w_noise.shape, F32),
-            pltpu.VMEM((width, 3 * width), BF16), pltpu.VMEM((rows, 3 * width), F32),
-            pltpu.SemaphoreType.DMA((6,)),
+            pltpu.VMEM((rows, 3 * width), F32), pltpu.SemaphoreType.DMA((6,)),
         ],
         flops=2 * rows * width * 3 * width,
     )
@@ -659,12 +657,12 @@
             ((members, width, points), BF16), ((members, channels, points), BF16),
             ((nodes, points), BF16),
         ],
-        own, normed, proj, low, high, member_noise, w_noise, w_qkv, w_out, w_hid, w_pred,
+        own, normed, proj, low, high, member_noise, w_noise, held_qkv, w_out, w_hid, w_pred,
         neighbours, degree, dec_nodes,
-        apart=(7, 8, 9),
+        apart=(8, 9),
         scratch=[
-            pltpu.VMEM((width, 2 * width), BF16), pltpu.VMEM((width, width), BF16),
-            pltpu.VMEM((width, width), BF16), pltpu.SemaphoreType.DMA((3,)),
+            pltpu.VMEM((width, width), BF16), pltpu.VMEM((width, width), BF16),
+            pltpu.SemaphoreType.DMA((2,)),
         ],
         flops=3 * 10**9,
     )
@@ -727,7 +725,7 @@
             ((members, width, nodes), F32), ((members, rim, width), BF16),
             ((members, rim, width), BF16), ((32, width), BF16),
         ],
-        own, low, high, member_noise, w_noise, w_qkv, d_proj, d_rim, d_updated,
+        own, low, high, member_noise, w_noise, held_qkv, d_proj, d_rim, d_updated,
         flops=2 * 10**9,
     )
     (plane,) = call(

time: 153 us -> 152 us (level)
  no operation moved by 1% of the time
where the time goes in v5:
time: 152 us; the launch traced here: 150 us
  starting transfers between devices  65.5 us (43%)
  waiting for transfers between devices  43.2 us (28%)
  Pallas kernels  40 us (26%)
    pallas_call x13, Pallas kernels, call(): pl.pallas_call(body, out_shape=out_shape, in_specs=[SMEM if i in smem els...  31.4 us
    all_to_all x4, starting transfers between devices, swapped(): return lax.all_to_all(a, planes, 0, 0, tiled=True)  26.6 us
    ppermute x12, starting transfers between devices, shifted(): moved.append(lax.ppermute(piece, levels, pairs))  18.1 us
    ppermute x12, waiting for transfers between devices, shifted(): moved.append(lax.ppermute(piece, levels, pairs))  16 us
    ppermute x1, waiting for transfers between devices, gather_members(): far = lax.ppermute(forecast, 'zhi', swap)  7.84 us
    ppermute x1, waiting for transfers between devices, on_device(): from_next = lax.ppermute(d_low, SPACE, down)  6.22 us
    pallas_call x2, Pallas kernels, unpack(): pl.pallas_call(body, out_shape=[jax.ShapeDtypeStruct(shape, F32) for shap...  5.56 us
    ppermute x1, starting transfers between devices, on_device(): high = lax.ppermute(sent_down, SPACE, down)  5.5 us
  transfers between devices with their start and end apart: 31, of which 17 were waited for; matrix products, arithmetic and copies ran while one was open for 0% of the time, Pallas kernels for 9%

profile of v5, /device:TPU:2, one launch (start us, length us, event | category | flops | bytes accessed | tf_op | source)
XLA Modules:
  0.0 150.0 jit_solution(18124170612198870287)
XLA Ops:
  2.0 3.5 %collective-permute-start = (bf16[2,16,768]{2,1,0:T(8,128)(2,1)S(1)}, bf16[2,16,768]{2,1,0:T(8,128)(2,1)S(1)}, u32[]{:S(2)}, u32[]{:S(2)}) collective-permute-start(bf16[2,16,768]{2,1,0:T(8,128)(2,1)S(1)} %get-tuple-element.74), channel_id=1, source_target_pairs={{0,4},{4,8},{8,12},{12,16},{16,20},{20,24},{24,28},{28,32},{32,36}... | collective-permute-start | bytes 147464 | tf_op jit(solution)/shard_map/ppermute | solution.py:635
  5.6 5.5 %collective-permute-start.1 = (bf16[2,16,768]{2,1,0:T(8,128)(2,1)S(1)}, bf16[2,16,768]{2,1,0:T(8,128)(2,1)S(1)}, u32[]{:S(2)}, u32[]{:S(2)}) collective-permute-start(bf16[2,16,768]{2,1,0:T(8,128)(2,1)S(1)} %get-tuple-element.75), channel_id=1, source_target_pairs={{4,0},{8,4},{12,8},{16,12},{20,16},{24,20},{28,24},{32,28},{36,32}... | collective-permute-start | bytes 147464 | tf_op jit(solution)/shard_map/ppermute | solution.py:636
  11.1 2.9 %shard_map.180 = (bf16[2,128,768]{2,1,0:T(8,128)(2,1)S(1)}, bf16[256,768]{1,0:T(8,128)(2,1)S(1)}, bf16[256,2304]{1,0:T(8,128)(2,1)S(1)}, bf16[768,2304]{1,0:T(8,128)(2,1)S(1)}) custom-call(bf16[2,768,128]{2,1,0:T(8,128)(2,1)} %latent_far.3, f32[2,32]{1,0:T(2,128)} %noise.3, f32[32,768]{1,0:T(8,128)} %w_noise.3, bf16[768,2304]{1,0:T(8,128)(2,1)} %w_qkv.1), custom_call_target="tpu_custom_call" | custom-call | flops 905969664 | bytes 4030720 | tf_op jit(solution)/shard_map/pallas_call | solution.py:46
  14.1 7.0 %shard_map.182 = (bf16[320,768]{1,0:T(8,128)(2,1)S(1)}, bf16[64,1536]{1,0:T(8,128)(2,1)S(1)}, bf16[256,768]{1,0:T(8,128)(2,1)S(1)}, bf16[256,768]{1,0:T(8,128)(2...) custom-call(bf16[2,128,768]{2,1,0:T(8,128)(2,1)S(1)} %get-tuple-elem, ...), custom_call_target="tpu_custom_call" | custom-call | flops 3000000000 | bytes 8205568 | tf_op jit(solution)/shard_map/pallas_call | solution.py:46
  21.2 4.0 %collective-permute-start.4 = (bf16[2,83,1024]{2,1,0:T(8,128)(2,1)S(1)}, bf16[2,83,1024]{2,1,0:T(8,128)(2,1)S(1)}, u32[]{:S(2)}, u32[]{:S(2)}) collective-permute-start(bf16[2,83,1024]{2,1,0:T(8,128)(2,1)S(1)} %get-tuple-element.79.mine), channel_id=1, source_target_pairs={{0,2},{2,0},{1,3},{3,1},{4,6},{6,4},{5,7},{7,5},{8,10},{10,8},{9,1... | collective-permute-start | bytes 1019912 | tf_op jit(solution)/shard_map/ppermute | solution.py:785
  25.1 7.8 %collective-permute-done.4.rest_1_ = bf16[2,83,1024]{2,1,0:T(8,128)(2,1)S(1)} collective-permute-done((bf16[2,83,1024]{2,1,0:T(8,128)(2,1)S(1)}, bf16[2,83,1024]{2,1,0:T(8,128)(2,1)S(1)}, u32[]{:S(2)}, u32[]{:S(2)}) %collective-permute-start.4) | collective-permute-done | bytes 340000 | tf_op jit(solution)/shard_map/ppermute | solution.py:785
  34.7 6.8 %shard_map.183 = (bf16[256,768]{1,0:T(8,128)(2,1)S(1)}, bf16[256,768]{1,0:T(8,128)(2,1)S(1)}, bf16[64,16,640]{2,1,0:T(8,128)(2,1)S(1)}, bf16[64,16,640]{2,1,0:T(8,128)(2,1)S(1)}, bf16[16,128]{1,0:T(8,128)(2,1)S(1)}) custom-call(s32[32]{0:T(128)S(1)} %copy-done.5, bf16[2,83,1024]{2,1,0:T(8,128)(2,1)S(1)} %get-tuple-element.79.mine, ...), custom_call_target="tpu_custom_call" | custom-call | flops 6000000000 | bytes 11526784 | tf_op jit(solution)/shard_map/pallas_call | solution.py:46
  41.5 2.7 %shard_map.184 = (bf16[2,256,1152]{2,1,0:T(8,128)(2,1)S(1)}, bf16[2,64,768]{2,1,0:T(8,128)(2,1)S(1)}, bf16[320,1152]{1,0:T(8,128)(2,1)S(1)}) custom-call(bf16[256,2304]{1,0:T(8,128)(2,1)S(1)} %get-tuple-element.73.proj, bf16[64,1536]{1,0:T(8,128)(2,1)S(1)} %get-tuple-element.78.proj_rim, s32[8,128]{1,0:T(8,128)S(1)} %copy-done.12, s32[1,128]{1,0:T(1,128)S(1)} %bitcast.15, ...), custom_call_target="tpu_custom_call" | custom-call | flops 2000000000 | bytes 1774080 | tf_op jit(solution)/shard_map/pallas_call | solution.py:46
  47.4 3.1 %shard_map.186 = bf16[16,4,16,896]{3,2,1,0:T(8,128)(2,1)} custom-call(bf16[320,768]{1,0:T(8,128)(2,1)S(1)} %get-tuple-element.77.normed, bf16[320,768]{1,0:T(8,128)(2,1)S(1)} %collective-permute-done.2.normed_theirs, bf16[2,256,1152]{2,1,0:T(8,128)(2,1)S(1)} %get-tuple-element.86.d_proj, bf16[2,64,768]{2,1,0:T(8,128)(2,1)S(1)} %get-tuple-element.87.d_rim, ...), custom_call_target="tpu_custom_call" | custom-call | flops 2000000000 | bytes 3149824 | tf_op jit(solution)/shard_map/pallas_call | solution.py:46
  50.5 5.9 %all-to-all-start = ((bf16[16,4,16,896]{3,2,1,0:T(8,128)(2,1)}), bf16[16,4,16,896]{3,2,1,0:T(8,128)(2,1)S(1)}, u32[]{:S(2)}, u32[]{:S(2)}) async-start(bf16[16,4,16,896]{3,2,1,0:T(8,128)(2,1)} %shard_map.186), calls=%async_computation | async-start | bytes 3670016 | tf_op jit(solution)/shard_map/all_to_all | solution.py:684
  56.3 3.2 %collective-permute-done.10 = bf16[64,16,640]{2,1,0:T(8,128)(2,1)S(1)} collective-permute-done((bf16[64,16,640]{2,1,0:T(8,128)(2,1)}, bf16[64,16,640]{2,1,0:T(8,128)(2,1)S(1)}, u32[]{:S(2)}, u32[]{:S(2)}) %collective-permute-start.10) | collective-permute-done | bytes 1310752 | tf_op jit(solution)/shard_map/ppermute | solution.py:705
  61.3 3.8 %collective-permute-start.12 = (bf16[16,16,640]{2,1,0:T(8,128)(2,1)S(1)}, bf16[16,16,640]{2,1,0:T(8,128)(2,1)S(1)}, u32[]{:S(2)}, u32[]{:S(2)}) collective-permute-start(bf16[16,16,640]{2,1,0:T(8,128)(2,1)S(1)} %get-tuple-element.103), channel_id=1, source_target_pairs={{0,2},{16,18},{2,0},{18,16},{1,3},{17,19},{3,1},{19,17},{4,6},{20,... | collective-permute-start | bytes 983048 | tf_op jit(solution)/shard_map/ppermute | solution.py:680
  65.8 5.3 %collective-permute-start.14 = (bf16[2,16,768]{2,1,0:T(8,128)(2,1)S(1)}, bf16[2,16,768]{2,1,0:T(8,128)(2,1)S(1)}, u32[]{:S(2)}, u32[]{:S(2)}) collective-permute-start(bf16[2,16,768]{2,1,0:T(8,128)(2,1)S(1)} %get-tuple-element.105), channel_id=1, source_target_pairs={{4,0},{8,4},{12,8},{16,12},{20,16},{24,20},{28,24},{32,28},{36,32}... | collective-permute-start | bytes 147464 | tf_op jit(solution)/shard_map/ppermute | solution.py:743
  73.1 6.2 %collective-permute-done.14.from_next = bf16[2,16,768]{2,1,0:T(8,128)(2,1)S(1)} collective-permute-done((bf16[2,16,768]{2,1,0:T(8,128)(2,1)S(1)}, bf16[2,16,768]{2,1,0:T(8,128)(2,1)S(1)}, u32[]{:S(2)}, u32[]{:S(2)}) %collective-permute-start.14) | collective-permute-done | bytes 49184 | tf_op jit(solution)/shard_map/ppermute | solution.py:743
  82.8 6.4 %all-to-all-start.1 = ((bf16[16,16,640]{2,1,0:T(8,128)(2,1)}), bf16[16,16,640]{2,1,0:T(8,128)(2,1)S(1)}, u32[]{:S(2)}, u32[]{:S(2)}) async-start(bf16[16,16,640]{2,1,0:T(8,128)(2,1)} %shard_map.189), calls=%async_computation.1 | async-start | bytes 655360 | tf_op jit(solution)/shard_map/all_to_all | solution.py:684
  89.6 2.8 %collective-permute-start.7 = (bf16[1,16,896]{2,1,0:T(8,128)(2,1)S(1)}, bf16[1,16,896]{2,1,0:T(8,128)(2,1)S(1)}, u32[]{:S(2)}, u32[]{:S(2)}) collective-permute-start(bf16[1,16,896]{2,1,0:T(8,128)(2,1)S(1)} %get-tuple-element.96), channel_id=1, source_target_pairs={{0,16},{16,2},{2,18},{18,0},{1,17},{17,3},{3,19},{19,1},{4,20},{20... | collective-permute-start | bytes 86024 | tf_op jit(solution)/shard_map/ppermute | solution.py:680
  92.4 3.2 %collective-permute-start.8 = (bf16[1,16,896]{2,1,0:T(8,128)(2,1)S(1)}, bf16[1,16,896]{2,1,0:T(8,128)(2,1)S(1)}, u32[]{:S(2)}, u32[]{:S(2)}) collective-permute-start(bf16[1,16,896]{2,1,0:T(8,128)(2,1)S(1)} %get-tuple-element.97), channel_id=1, source_target_pairs={{0,2},{16,18},{2,0},{18,16},{1,3},{17,19},{3,1},{19,17},{4,6},{20,... | collective-permute-start | bytes 86024 | tf_op jit(solution)/shard_map/ppermute | solution.py:680
  100.3 7.2 %all-to-all-start.2 = ((bf16[16,16,640]{2,1,0:T(8,128)(2,1)}), bf16[16,16,640]{2,1,0:T(8,128)(2,1)S(1)}, u32[]{:S(2)}, u32[]{:S(2)}) async-start(bf16[16,16,640]{2,1,0:T(8,128)(2,1)} %bitcast.5), calls=%async_computation.2 | async-start | bytes 655360 | tf_op jit(solution)/shard_map/all_to_all | solution.py:684
  115.9 7.1 %all-to-all-start.3 = ((bf16[16,4,16,896]{3,2,1,0:T(8,128)(2,1)}), bf16[16,4,16,896]{3,2,1,0:T(8,128)(2,1)S(1)}, u32[]{:S(2)}, u32[]{:S(2)}) async-start(bf16[16,4,16,896]{3,2,1,0:T(8,128)(2,1)} %bitcast.16), calls=%async_computation.3 | async-start | bytes 3670016 | tf_op jit(solution)/shard_map/all_to_all | solution.py:684
  126.2 4.4 %collective-permute-done.21.refs_3_ = bf16[16,16,640]{2,1,0:T(8,128)(2,1)S(1)} collective-permute-done((bf16[16,16,640]{2,1,0:T(8,128)(2,1)S(1)}, bf16[16,16,640]{2,1,0:T(8,128)(2,1)S(1)}, u32[]{:S(2)}, u32[]{:S(2)}) %collective-permute-start.21) | collective-permute-done | bytes 327712 | tf_op jit(solution)/shard_map/ppermute | solution.py:680
  130.6 2.8 %collective-permute-done.20.refs_2_ = bf16[16,16,640]{2,1,0:T(8,128)(2,1)S(1)} collective-permute-done((bf16[16,16,640]{2,1,0:T(8,128)(2,1)S(1)}, bf16[16,16,640]{2,1,0:T(8,128)(2,1)S(1)}, u32[]{:S(2)}, u32[]{:S(2)}) %collective-permute-start.20) | collective-permute-done | bytes 327712 | tf_op jit(solution)/shard_map/ppermute | solution.py:680
  133.4 3.4 %collective-permute-done.19.refs_1_ = bf16[16,16,640]{2,1,0:T(8,128)(2,1)S(1)} collective-permute-done((bf16[16,16,640]{2,1,0:T(8,128)(2,1)S(1)}, bf16[16,16,640]{2,1,0:T(8,128)(2,1)S(1)}, u32[]{:S(2)}, u32[]{:S(2)}) %collective-permute-start.19) | collective-permute-done | bytes 327712 | tf_op jit(solution)/shard_map/ppermute | solution.py:680
  138.4 3.1 %shard_map.193 = (f32[768,768]{1,0:T(8,128)}, f32[768,768]{1,0:T(8,128)}, f32[83,768]{1,0:T(8,128)}) custom-call(bf16[16,16,640]{2,1,0:T(8,128)(2,1)S(1)} %all-to-all-done.2.refs_0_, bf16[16,16,640]{2,1,0:T(8,128)(2,1)S(1)} %collective-permute-done.19.refs_1_, bf16[16,16,640]{2,1,0:T(8,128)(2,1)S(1)} %collective-permute-done.20.refs_2_, ...), custom_call_target="tpu_custom_call" | custom-call | bytes 8000000 | tf_op jit(solution)/shard_map/pallas_call | solution.py:587
  146.7 3.1 %shard_map.195 = (f32[768,2304]{1,0:T(8,128)}, f32[32,768]{1,0:T(8,128)}, f32[1,1]{1,0:T(1,128)}) custom-call(bf16[16,4,16,896]{3,2,1,0:T(8,128)(2,1)S(1)} %collective-permute-done.26.plane, s32[1,32]{1,0:T(1,128)S(1)} %bitcast.13, f32[768,2304]{1,0:T(8,128)} %get-tuple-element.125._qkv, ...), custom_call_target="tpu_custom_call", output_to_operand_aliasing={{0}: (2, {})} | custom-call | bytes 6000000 | tf_op jit(solution)/shard_map/pallas_call | solution.py:570
  (82 shorter events, 37.4 us)
Async XLA Ops:
  2.0 12.0 %collective-permute-start = (bf16[2,16,768]{2,1,0:T(8,128)(2,1)S(1)}, bf16[2,16,768]{2,1,0:T(8,128)(2,1)S(1)}, u32[]{:S(2)}, u32[]{:S(2)}) collective-permute-start(bf16[2,16,768]{2,1,0:T(8,128)(2,1)S(1)} %get-tuple-element.74), channel_id=1, source_target_pairs={{0,4},{4,8},{8,12},{12,16},{16,20},{20,24},{24,28},{28,32},{32,36}... | collective-permute-start | bytes 147464 | tf_op jit(solution)/shard_map/ppermute | solution.py:635
  5.6 8.5 %collective-permute-start.1 = (bf16[2,16,768]{2,1,0:T(8,128)(2,1)S(1)}, bf16[2,16,768]{2,1,0:T(8,128)(2,1)S(1)}, u32[]{:S(2)}, u32[]{:S(2)}) collective-permute-start(bf16[2,16,768]{2,1,0:T(8,128)(2,1)S(1)} %get-tuple-element.75), channel_id=1, source_target_pairs={{4,0},{8,4},{12,8},{16,12},{20,16},{24,20},{28,24},{32,28},{36,32}... | collective-permute-start | bytes 147464 | tf_op jit(solution)/shard_map/ppermute | solution.py:636
  21.2 11.8 %collective-permute-start.4 = (bf16[2,83,1024]{2,1,0:T(8,128)(2,1)S(1)}, bf16[2,83,1024]{2,1,0:T(8,128)(2,1)S(1)}, u32[]{:S(2)}, u32[]{:S(2)}) collective-permute-start(bf16[2,83,1024]{2,1,0:T(8,128)(2,1)S(1)} %get-tuple-element.79.mine), channel_id=1, source_target_pairs={{0,2},{2,0},{1,3},{3,1},{4,6},{6,4},{5,7},{7,5},{8,10},{10,8},{9,1... | collective-permute-start | bytes 1019912 | tf_op jit(solution)/shard_map/ppermute | solution.py:785
  25.1 7.9 %collective-permute-start.3 = (bf16[2,83,1024]{2,1,0:T(8,128)(2,1)S(1)}, bf16[2,83,1024]{2,1,0:T(8,128)(2,1)S(1)}, u32[]{:S(2)}, u32[]{:S(2)}) collective-permute-start(bf16[2,83,1024]{2,1,0:T(8,128)(2,1)S(1)} %get-tuple-element.79.mine), channel_id=1, source_target_pairs={{0,1},{1,0},{2,3},{3,2},{4,5},{5,4},{6,7},{7,6},{8,9},{9,8},{10,11... | collective-permute-start | bytes 1019912 | tf_op jit(solution)/shard_map/ppermute | solution.py:786
  50.5 32.4 %all-to-all-start = ((bf16[16,4,16,896]{3,2,1,0:T(8,128)(2,1)}), bf16[16,4,16,896]{3,2,1,0:T(8,128)(2,1)S(1)}, u32[]{:S(2)}, u32[]{:S(2)}) async-start(bf16[16,4,16,896]{3,2,1,0:T(8,128)(2,1)} %shard_map.186), calls=%async_computation | async-start | bytes 3670016 | tf_op jit(solution)/shard_map/all_to_all | solution.py:684
  59.9 22.0 %collective-permute-start.11 = (bf16[16,16,640]{2,1,0:T(8,128)(2,1)S(1)}, bf16[16,16,640]{2,1,0:T(8,128)(2,1)S(1)}, u32[]{:S(2)}, u32[]{:S(2)}) collective-permute-start(bf16[16,16,640]{2,1,0:T(8,128)(2,1)S(1)} %get-tuple-element.102), channel_id=1, source_target_pairs={{0,16},{16,2},{2,18},{18,0},{1,17},{17,3},{3,19},{19,1},{4,20},{20... | collective-permute-start | bytes 983048 | tf_op jit(solution)/shard_map/ppermute | solution.py:680
  61.3 20.6 %collective-permute-start.12 = (bf16[16,16,640]{2,1,0:T(8,128)(2,1)S(1)}, bf16[16,16,640]{2,1,0:T(8,128)(2,1)S(1)}, u32[]{:S(2)}, u32[]{:S(2)}) collective-permute-start(bf16[16,16,640]{2,1,0:T(8,128)(2,1)S(1)} %get-tuple-element.103), channel_id=1, source_target_pairs={{0,2},{16,18},{2,0},{18,16},{1,3},{17,19},{3,1},{19,17},{4,6},{20,... | collective-permute-start | bytes 983048 | tf_op jit(solution)/shard_map/ppermute | solution.py:680
  65.1 16.8 %collective-permute-start.13 = (bf16[16,16,640]{2,1,0:T(8,128)(2,1)S(1)}, bf16[16,16,640]{2,1,0:T(8,128)(2,1)S(1)}, u32[]{:S(2)}, u32[]{:S(2)}) collective-permute-start(bf16[16,16,640]{2,1,0:T(8,128)(2,1)S(1)} %get-tuple-element.104), channel_id=1, source_target_pairs={{0,18},{16,0},{2,16},{18,2},{1,19},{17,1},{3,17},{19,3},{4,22},{20... | collective-permute-start | bytes 983048 | tf_op jit(solution)/shard_map/ppermute | solution.py:680
  65.8 13.5 %collective-permute-start.14 = (bf16[2,16,768]{2,1,0:T(8,128)(2,1)S(1)}, bf16[2,16,768]{2,1,0:T(8,128)(2,1)S(1)}, u32[]{:S(2)}, u32[]{:S(2)}) collective-permute-start(bf16[2,16,768]{2,1,0:T(8,128)(2,1)S(1)} %get-tuple-element.105), channel_id=1, source_target_pairs={{4,0},{8,4},{12,8},{16,12},{20,16},{24,20},{28,24},{32,28},{36,32}... | collective-permute-start | bytes 147464 | tf_op jit(solution)/shard_map/ppermute | solution.py:743
  71.2 10.7 %collective-permute-start.15 = (bf16[2,16,768]{2,1,0:T(8,128)(2,1)S(1)}, bf16[2,16,768]{2,1,0:T(8,128)(2,1)S(1)}, u32[]{:S(2)}, u32[]{:S(2)}) collective-permute-start(bf16[2,16,768]{2,1,0:T(8,128)(2,1)S(1)} %get-tuple-element.106), channel_id=1, source_target_pairs={{0,4},{4,8},{8,12},{12,16},{16,20},{20,24},{24,28},{28,32},{32,36}... | collective-permute-start | bytes 147464 | tf_op jit(solution)/shard_map/ppermute | solution.py:744
  82.8 13.9 %all-to-all-start.1 = ((bf16[16,16,640]{2,1,0:T(8,128)(2,1)}), bf16[16,16,640]{2,1,0:T(8,128)(2,1)S(1)}, u32[]{:S(2)}, u32[]{:S(2)}) async-start(bf16[16,16,640]{2,1,0:T(8,128)(2,1)} %shard_map.189), calls=%async_computation.1 | async-start | bytes 655360 | tf_op jit(solution)/shard_map/all_to_all | solution.py:684
  89.6 7.2 %collective-permute-start.7 = (bf16[1,16,896]{2,1,0:T(8,128)(2,1)S(1)}, bf16[1,16,896]{2,1,0:T(8,128)(2,1)S(1)}, u32[]{:S(2)}, u32[]{:S(2)}) collective-permute-start(bf16[1,16,896]{2,1,0:T(8,128)(2,1)S(1)} %get-tuple-element.96), channel_id=1, source_target_pairs={{0,16},{16,2},{2,18},{18,0},{1,17},{17,3},{3,19},{19,1},{4,20},{20... | collective-permute-start | bytes 86024 | tf_op jit(solution)/shard_map/ppermute | solution.py:680
  92.4 5.4 %collective-permute-start.8 = (bf16[1,16,896]{2,1,0:T(8,128)(2,1)S(1)}, bf16[1,16,896]{2,1,0:T(8,128)(2,1)S(1)}, u32[]{:S(2)}, u32[]{:S(2)}) collective-permute-start(bf16[1,16,896]{2,1,0:T(8,128)(2,1)S(1)} %get-tuple-element.97), channel_id=1, source_target_pairs={{0,2},{16,18},{2,0},{18,16},{1,3},{17,19},{3,1},{19,17},{4,6},{20,... | collective-permute-start | bytes 86024 | tf_op jit(solution)/shard_map/ppermute | solution.py:680
  95.6 3.9 %collective-permute-start.9 = (bf16[1,16,896]{2,1,0:T(8,128)(2,1)S(1)}, bf16[1,16,896]{2,1,0:T(8,128)(2,1)S(1)}, u32[]{:S(2)}, u32[]{:S(2)}) collective-permute-start(bf16[1,16,896]{2,1,0:T(8,128)(2,1)S(1)} %get-tuple-element.98), channel_id=1, source_target_pairs={{0,18},{16,0},{2,16},{18,2},{1,19},{17,1},{3,17},{19,3},{4,22},{20... | collective-permute-start | bytes 86024 | tf_op jit(solution)/shard_map/ppermute | solution.py:680
  100.3 14.2 %all-to-all-start.2 = ((bf16[16,16,640]{2,1,0:T(8,128)(2,1)}), bf16[16,16,640]{2,1,0:T(8,128)(2,1)S(1)}, u32[]{:S(2)}, u32[]{:S(2)}) async-start(bf16[16,16,640]{2,1,0:T(8,128)(2,1)} %bitcast.5), calls=%async_computation.2 | async-start | bytes 655360 | tf_op jit(solution)/shard_map/all_to_all | solution.py:684
  107.5 4.2 %collective-permute-start.18 = (bf16[1,16,896]{2,1,0:T(8,128)(2,1)S(1)}, bf16[1,16,896]{2,1,0:T(8,128)(2,1)S(1)}, u32[]{:S(2)}, u32[]{:S(2)}) collective-permute-start(bf16[1,16,896]{2,1,0:T(8,128)(2,1)S(1)} %get-tuple-element.116.one), channel_id=1, source_target_pairs={{0,18},{16,0},{2,16},{18,2},{1,19},{17,1},{3,17},{19,3},{4,22},{20... | collective-permute-start | bytes 86024 | tf_op jit(solution)/shard_map/ppermute | solution.py:680
  108.7 5.4 %collective-permute-start.17 = (bf16[1,16,896]{2,1,0:T(8,128)(2,1)S(1)}, bf16[1,16,896]{2,1,0:T(8,128)(2,1)S(1)}, u32[]{:S(2)}, u32[]{:S(2)}) collective-permute-start(bf16[1,16,896]{2,1,0:T(8,128)(2,1)S(1)} %get-tuple-element.116.one), channel_id=1, source_target_pairs={{0,2},{16,18},{2,0},{18,16},{1,3},{17,19},{3,1},{19,17},{4,6},{20,... | collective-permute-start | bytes 86024 | tf_op jit(solution)/shard_map/ppermute | solution.py:680
  109.3 5.1 %collective-permute-start.16 = (bf16[1,16,896]{2,1,0:T(8,128)(2,1)S(1)}, bf16[1,16,896]{2,1,0:T(8,128)(2,1)S(1)}, u32[]{:S(2)}, u32[]{:S(2)}) collective-permute-start(bf16[1,16,896]{2,1,0:T(8,128)(2,1)S(1)} %get-tuple-element.116.one), channel_id=1, source_target_pairs={{0,16},{16,2},{2,18},{18,0},{1,17},{17,3},{3,19},{19,1},{4,20},{20... | collective-permute-start | bytes 86024 | tf_op jit(solution)/shard_map/ppermute | solution.py:680
  115.9 27.0 %all-to-all-start.3 = ((bf16[16,4,16,896]{3,2,1,0:T(8,128)(2,1)}), bf16[16,4,16,896]{3,2,1,0:T(8,128)(2,1)S(1)}, u32[]{:S(2)}, u32[]{:S(2)}) async-start(bf16[16,4,16,896]{3,2,1,0:T(8,128)(2,1)} %bitcast.16), calls=%async_computation.3 | async-start | bytes 3670016 | tf_op jit(solution)/shard_map/all_to_all | solution.py:684
  123.0 7.6 %collective-permute-start.21 = (bf16[16,16,640]{2,1,0:T(8,128)(2,1)S(1)}, bf16[16,16,640]{2,1,0:T(8,128)(2,1)S(1)}, u32[]{:S(2)}, u32[]{:S(2)}) collective-permute-start(bf16[16,16,640]{2,1,0:T(8,128)(2,1)S(1)} %all-to-all-done.2.refs_0_), channel_id=1, source_target_pairs={{0,18},{16,0},{2,16},{18,2},{1,19},{17,1},{3,17},{19,3},{4,22},{20... | collective-permute-start | bytes 983048 | tf_op jit(solution)/shard_map/ppermute | solution.py:680
  124.7 8.7 %collective-permute-start.20 = (bf16[16,16,640]{2,1,0:T(8,128)(2,1)S(1)}, bf16[16,16,640]{2,1,0:T(8,128)(2,1)S(1)}, u32[]{:S(2)}, u32[]{:S(2)}) collective-permute-start(bf16[16,16,640]{2,1,0:T(8,128)(2,1)S(1)} %all-to-all-done.2.refs_0_), channel_id=1, source_target_pairs={{0,2},{16,18},{2,0},{18,16},{1,3},{17,19},{3,1},{19,17},{4,6},{20,... | collective-permute-start | bytes 983048 | tf_op jit(solution)/shard_map/ppermute | solution.py:680
  125.6 11.2 %collective-permute-start.19 = (bf16[16,16,640]{2,1,0:T(8,128)(2,1)S(1)}, bf16[16,16,640]{2,1,0:T(8,128)(2,1)S(1)}, u32[]{:S(2)}, u32[]{:S(2)}) collective-permute-start(bf16[16,16,640]{2,1,0:T(8,128)(2,1)S(1)} %all-to-all-done.2.refs_0_), channel_id=1, source_target_pairs={{0,16},{16,2},{2,18},{18,0},{1,17},{17,3},{3,19},{19,1},{4,20},{20... | collective-permute-start | bytes 983048 | tf_op jit(solution)/shard_map/ppermute | solution.py:680
  126.2 10.6 %collective-permute-start.22 = (bf16[16,16,640]{2,1,0:T(8,128)(2,1)S(1)}, bf16[16,16,640]{2,1,0:T(8,128)(2,1)S(1)}, u32[]{:S(2)}, u32[]{:S(2)}) collective-permute-start(bf16[16,16,640]{2,1,0:T(8,128)(2,1)S(1)} %all-to-all-done.2.refs_0_), channel_id=1, source_target_pairs={{0,1},{1,0},{2,3},{3,2},{4,5},{5,4},{6,7},{7,6},{8,9},{9,8},{10,11... | collective-permute-start | bytes 983048 | tf_op jit(solution)/shard_map/ppermute | solution.py:773
  130.6 6.2 %collective-permute-start.25 = (bf16[16,16,640]{2,1,0:T(8,128)(2,1)S(1)}, bf16[16,16,640]{2,1,0:T(8,128)(2,1)S(1)}, u32[]{:S(2)}, u32[]{:S(2)}) collective-permute-start(bf16[16,16,640]{2,1,0:T(8,128)(2,1)S(1)} %collective-permute-done.21.refs_3_), channel_id=1, source_target_pairs={{0,1},{1,0},{2,3},{3,2},{4,5},{5,4},{6,7},{7,6},{8,9},{9,8},{10,11... | collective-permute-start | bytes 983048 | tf_op jit(solution)/shard_map/ppermute | solution.py:773
  (21 other events, 217.6 us)

commit v6 on v5

--- a/solution.py
+++ b/solution.py
@@ -214,17 +214,52 @@
     return square * inverse - 0.5, v * inverse
 
 
+def crps_near_body(mine, near, targets, slopes, columns):
+    members, channels, points = mine.shape
+    total = 8
+    block = 256
+    scale = 0.5 / (total * (total - 1))
+    for g in range(0, points, block):
+        at = slice(g, g + block)
+        own = [mine[m, :, at].astype(F32) for m in range(members)]
+        aim = targets[:, at]
+        close = jnp.zeros((channels, block), F32)
+        apart = jnp.zeros((channels, block), F32)
+        first = []
+        grads = [jnp.zeros((channels, block), F32)] * members
+        for m in range(members):
+            value, grad = smooth(own[m] - aim)
+            close = close + value
+            first.append(grad)
+        for a in range(members):
+            for b in range(a + 1, members):
+                value, grad = smooth(own[a] - own[b])
+                apart = apart + 2.0 * value
+                grads[a] = grads[a] + grad
+                grads[b] = grads[b] - grad
+        for k in range(members):
+            theirs = near[k, :, at].astype(F32)
+            for m in range(members):
+                value, grad = smooth(own[m] - theirs)
+                apart = apart + value
+                grads[m] = grads[m] + grad
+        for m in range(members):
+            slopes[m, :, at] = first[m] * (1.0 / total) - grads[m] * (2.0 * scale)
+        columns[:, at] = jnp.sum(
+            close * (1.0 / total) - apart * scale, axis=0, keepdims=True
+        )
+
+
 def crps_body(
     counts, mine, *rest
 ):
-    (*others, targets, hidden, slope, table, stored, attended, w_out, w_hid, w_pred,
+    (*others, slopes, columns, hidden, slope, table, stored, attended, w_out, w_hid, w_pred,
      d_updated, d_attended, keep, send, loss, d_pre, d_cast, halves) = rest
     live_count = counts[lax.axis_index(SPACE)]
     core = lax.axis_index("core")
     members, channels, points = mine.shape
-    total = members * (1 + len(others))
+    total = 8
     block = 256
-    nodes = table.shape[0]
     scale = 0.5 / (total * (total - 1))
     losses = []
     for g in range(0, points, block):
@@ -232,32 +267,20 @@
         live = lax.broadcasted_iota(jnp.int32, (1, block), 1) + g < live_count
         live = live.astype(F32)
         own = [mine[m, :, at].astype(F32) for m in range(members)]
-        aim = targets[:, at]
-        near = jnp.zeros((channels, block), F32)
-        far = jnp.zeros((channels, block), F32)
-        slopes = []
-        for m in range(members):
-            value, grad = smooth(own[m] - aim)
-            near = near + value
-            slopes.append([grad, jnp.zeros((channels, block), F32)])
-        for a in range(members):
-            for b in range(a + 1, members):
-                value, grad = smooth(own[a] - own[b])
-                far = far + 2.0 * value
-                slopes[a][1] = slopes[a][1] + grad
-                slopes[b][1] = slopes[b][1] - grad
+        apart = jnp.zeros((channels, block), F32)
+        grads = [jnp.zeros((channels, block), F32)] * members
         for other in others:
             for k in range(members):
                 theirs = other[k, :, at].astype(F32)
                 for m in range(members):
                     value, grad = smooth(own[m] - theirs)
-                    far = far + value
-                    slopes[m][1] = slopes[m][1] + grad
+                    apart = apart + value
+                    grads[m] = grads[m] + grad
         for m in range(members):
-            grad = slopes[m][0] * (1.0 / total) - slopes[m][1] * (2.0 * scale)
+            grad = slopes[m, :, at] - grads[m] * (2.0 * scale)
             d_cast[m, :, at] = (grad * live).astype(BF16)
-        column = jnp.sum(near * (1.0 / total) - far * scale, axis=0, keepdims=True) * live
-        losses.append(column)
+        column = columns[:, at] - jnp.sum(apart, axis=0, keepdims=True) * scale
+        losses.append(column * live)
     for i in range(16):
         at = i % 2
         piece = losses[i // 2 % 4][:, TILE * at : TILE * (at + 1)]
@@ -666,7 +689,12 @@
         ],
         flops=3 * 10**9,
     )
-    gathered = gather_members(forecast)
+    near, *gathered = gather_members(forecast)
+    slopes, columns = call(
+        crps_near_body, [((members, channels, points), F32), ((1, points), F32)],
+        forecast, near, targets,
+        flops=10**8,
+    )
     planes, levels = ("x", "y"), ("zlo", "zhi")
     spots = lax.axis_size(planes)
     tile, rest_tile = (16, SPLIT), (16, REST)
@@ -692,7 +720,7 @@
             ((rows, width), BF16), ((rows, width), BF16), (first_shape, BF16),
             (first_shape, BF16), ((16, TILE), BF16),
         ],
-        counts, forecast, *gathered, targets, hidden, slope, table, stored, attended,
+        counts, forecast, *gathered, slopes, columns, hidden, slope, table, stored, attended,
         w_out, w_hid, w_pred,
         smem=(0,),
         scratch=[

time: 152 us -> 151 us (level)
    pallas_call x13 -> x14, Pallas kernels: 31.4 us -> 31.6 us  [call(): pl.pallas_call(body, out_shape=out_shape, in_specs=[SMEM if i in smem els...]
  transfers between devices with their start and end apart: 31 -> 31, of which waited for: 17 -> 17; matrix products, arithmetic and copies ran while one was open for 0% -> 0% of each run, Pallas kernels for 9% -> 10%
where the time goes in v6:
time: 151 us; the launch traced here: 149 us
  starting transfers between devices  65.5 us (43%)
  waiting for transfers between devices  42.3 us (28%)
  Pallas kernels  40.2 us (27%)
    pallas_call x14, Pallas kernels, call(): pl.pallas_call(body, out_shape=out_shape, in_specs=[SMEM if i in smem els...  31.6 us
    all_to_all x4, starting transfers between devices, swapped(): return lax.all_to_all(a, planes, 0, 0, tiled=True)  26.6 us
    ppermute x12, starting transfers between devices, shifted(): moved.append(lax.ppermute(piece, levels, pairs))  18.1 us
    ppermute x12, waiting for transfers between devices, shifted(): moved.append(lax.ppermute(piece, levels, pairs))  16 us
    ppermute x1, waiting for transfers between devices, gather_members(): far = lax.ppermute(forecast, 'zhi', swap)  7.85 us
    ppermute x1, waiting for transfers between devices, on_device(): from_next = lax.ppermute(d_low, SPACE, down)  6.22 us
    pallas_call x2, Pallas kernels, unpack(): pl.pallas_call(body, out_shape=[jax.ShapeDtypeStruct(shape, F32) for shap...  5.6 us
    ppermute x1, starting transfers between devices, on_device(): high = lax.ppermute(sent_down, SPACE, down)  5.5 us
  transfers between devices with their start and end apart: 31, of which 17 were waited for; matrix products, arithmetic and copies ran while one was open for 0% of the time, Pallas kernels for 10%

profile of v6, /device:TPU:2, one launch (start us, length us, event | category | flops | bytes accessed | tf_op | source)
XLA Modules:
  0.0 149.2 jit_solution(17793508333208738472)
XLA Ops:
  2.0 3.5 %collective-permute-start = (bf16[2,16,768]{2,1,0:T(8,128)(2,1)S(1)}, bf16[2,16,768]{2,1,0:T(8,128)(2,1)S(1)}, u32[]{:S(2)}, u32[]{:S(2)}) collective-permute-start(bf16[2,16,768]{2,1,0:T(8,128)(2,1)S(1)} %get-tuple-element.76), channel_id=1, source_target_pairs={{0,4},{4,8},{8,12},{12,16},{16,20},{20,24},{24,28},{28,32},{32,36}... | collective-permute-start | bytes 147464 | tf_op jit(solution)/shard_map/ppermute | solution.py:658
  5.6 5.5 %collective-permute-start.1 = (bf16[2,16,768]{2,1,0:T(8,128)(2,1)S(1)}, bf16[2,16,768]{2,1,0:T(8,128)(2,1)S(1)}, u32[]{:S(2)}, u32[]{:S(2)}) collective-permute-start(bf16[2,16,768]{2,1,0:T(8,128)(2,1)S(1)} %get-tuple-element.77), channel_id=1, source_target_pairs={{4,0},{8,4},{12,8},{16,12},{20,16},{24,20},{28,24},{32,28},{36,32}... | collective-permute-start | bytes 147464 | tf_op jit(solution)/shard_map/ppermute | solution.py:659
  11.1 2.9 %shard_map.180 = (bf16[2,128,768]{2,1,0:T(8,128)(2,1)S(1)}, bf16[256,768]{1,0:T(8,128)(2,1)S(1)}, bf16[256,2304]{1,0:T(8,128)(2,1)S(1)}, bf16[768,2304]{1,0:T(8,128)(2,1)S(1)}) custom-call(bf16[2,768,128]{2,1,0:T(8,128)(2,1)} %latent_far.3, f32[2,32]{1,0:T(2,128)} %noise.3, f32[32,768]{1,0:T(8,128)} %w_noise.3, bf16[768,2304]{1,0:T(8,128)(2,1)} %w_qkv.1), custom_call_target="tpu_custom_call" | custom-call | flops 905969664 | bytes 4030720 | tf_op jit(solution)/shard_map/pallas_call | solution.py:46
  14.1 7.0 %shard_map.182 = (bf16[320,768]{1,0:T(8,128)(2,1)S(1)}, bf16[64,1536]{1,0:T(8,128)(2,1)S(1)}, bf16[256,768]{1,0:T(8,128)(2,1)S(1)}, bf16[256,768]{1,0:T(8,128)(2...) custom-call(bf16[2,128,768]{2,1,0:T(8,128)(2,1)S(1)} %get-tuple-elem, ...), custom_call_target="tpu_custom_call" | custom-call | flops 3000000000 | bytes 8205568 | tf_op jit(solution)/shard_map/pallas_call | solution.py:46
  21.2 3.9 %collective-permute-start.3 = (bf16[2,83,1024]{2,1,0:T(8,128)(2,1)S(1)}, bf16[2,83,1024]{2,1,0:T(8,128)(2,1)S(1)}, u32[]{:S(2)}, u32[]{:S(2)}) collective-permute-start(bf16[2,83,1024]{2,1,0:T(8,128)(2,1)S(1)} %get-tuple-element.81.mine), channel_id=1, source_target_pairs={{0,2},{2,0},{1,3},{3,1},{4,6},{6,4},{5,7},{7,5},{8,10},{10,8},{9,1... | collective-permute-start | bytes 1019912 | tf_op jit(solution)/shard_map/ppermute | solution.py:813
  25.1 7.8 %collective-permute-done.3.rest_0_ = bf16[2,83,1024]{2,1,0:T(8,128)(2,1)S(1)} collective-permute-done((bf16[2,83,1024]{2,1,0:T(8,128)(2,1)S(1)}, bf16[2,83,1024]{2,1,0:T(8,128)(2,1)S(1)}, u32[]{:S(2)}, u32[]{:S(2)}) %collective-permute-start.3) | collective-permute-done | bytes 340000 | tf_op jit(solution)/shard_map/ppermute | solution.py:813
  34.7 6.0 %shard_map.184 = (bf16[256,768]{1,0:T(8,128)(2,1)S(1)}, bf16[256,768]{1,0:T(8,128)(2,1)S(1)}, bf16[64,16,640]{2,1,0:T(8,128)(2,1)S(1)}, bf16[64,16,640]{2,1,0:T(8,128)(2,1)S(1)}, bf16[16,128]{1,0:T(8,128)(2,1)S(1)}) custom-call(s32[32]{0:T(128)S(1)} %copy-done.6, bf16[2,83,1024]{2,1,0:T(8,128)(2,1)S(1)} %get-tuple-element.81.mine, ...), custom_call_target="tpu_custom_call" | custom-call | flops 6000000000 | bytes 11530880 | tf_op jit(solution)/shard_map/pallas_call | solution.py:46
  40.7 2.7 %shard_map.185 = (bf16[2,256,1152]{2,1,0:T(8,128)(2,1)S(1)}, bf16[2,64,768]{2,1,0:T(8,128)(2,1)S(1)}, bf16[320,1152]{1,0:T(8,128)(2,1)S(1)}) custom-call(bf16[256,2304]{1,0:T(8,128)(2,1)S(1)} %get-tuple-element.75.proj, bf16[64,1536]{1,0:T(8,128)(2,1)S(1)} %get-tuple-element.80.proj_rim, s32[8,128]{1,0:T(8,128)S(1)} %copy-done.12, s32[1,128]{1,0:T(1,128)S(1)} %bitcast.15, ...), custom_call_target="tpu_custom_call" | custom-call | flops 2000000000 | bytes 1774080 | tf_op jit(solution)/shard_map/pallas_call | solution.py:46
  46.6 3.0 %shard_map.187 = bf16[16,4,16,896]{3,2,1,0:T(8,128)(2,1)} custom-call(bf16[320,768]{1,0:T(8,128)(2,1)S(1)} %get-tuple-element.79.normed, bf16[320,768]{1,0:T(8,128)(2,1)S(1)} %collective-permute-done.2.normed_theirs, bf16[2,256,1152]{2,1,0:T(8,128)(2,1)S(1)} %get-tuple-element.90.d_proj, bf16[2,64,768]{2,1,0:T(8,128)(2,1)S(1)} %get-tuple-element.91.d_rim, ...), custom_call_target="tpu_custom_call" | custom-call | flops 2000000000 | bytes 3149824 | tf_op jit(solution)/shard_map/pallas_call | solution.py:46
  49.7 5.9 %all-to-all-start = ((bf16[16,4,16,896]{3,2,1,0:T(8,128)(2,1)}), bf16[16,4,16,896]{3,2,1,0:T(8,128)(2,1)S(1)}, u32[]{:S(2)}, u32[]{:S(2)}) async-start(bf16[16,4,16,896]{3,2,1,0:T(8,128)(2,1)} %shard_map.187), calls=%async_computation | async-start | bytes 3670016 | tf_op jit(solution)/shard_map/all_to_all | solution.py:712
  55.6 3.2 %collective-permute-done.10 = bf16[64,16,640]{2,1,0:T(8,128)(2,1)S(1)} collective-permute-done((bf16[64,16,640]{2,1,0:T(8,128)(2,1)}, bf16[64,16,640]{2,1,0:T(8,128)(2,1)S(1)}, u32[]{:S(2)}, u32[]{:S(2)}) %collective-permute-start.10) | collective-permute-done | bytes 1310752 | tf_op jit(solution)/shard_map/ppermute | solution.py:733
  60.5 3.9 %collective-permute-start.12 = (bf16[16,16,640]{2,1,0:T(8,128)(2,1)S(1)}, bf16[16,16,640]{2,1,0:T(8,128)(2,1)S(1)}, u32[]{:S(2)}, u32[]{:S(2)}) collective-permute-start(bf16[16,16,640]{2,1,0:T(8,128)(2,1)S(1)} %get-tuple-element.107), channel_id=1, source_target_pairs={{0,2},{16,18},{2,0},{18,16},{1,3},{17,19},{3,1},{19,17},{4,6},{20,... | collective-permute-start | bytes 983048 | tf_op jit(solution)/shard_map/ppermute | solution.py:708
  65.1 5.3 %collective-permute-start.14 = (bf16[2,16,768]{2,1,0:T(8,128)(2,1)S(1)}, bf16[2,16,768]{2,1,0:T(8,128)(2,1)S(1)}, u32[]{:S(2)}, u32[]{:S(2)}) collective-permute-start(bf16[2,16,768]{2,1,0:T(8,128)(2,1)S(1)} %get-tuple-element.109), channel_id=1, source_target_pairs={{4,0},{8,4},{12,8},{16,12},{20,16},{24,20},{28,24},{32,28},{36,32}... | collective-permute-start | bytes 147464 | tf_op jit(solution)/shard_map/ppermute | solution.py:771
  72.3 6.2 %collective-permute-done.14.from_next = bf16[2,16,768]{2,1,0:T(8,128)(2,1)S(1)} collective-permute-done((bf16[2,16,768]{2,1,0:T(8,128)(2,1)S(1)}, bf16[2,16,768]{2,1,0:T(8,128)(2,1)S(1)}, u32[]{:S(2)}, u32[]{:S(2)}) %collective-permute-start.14) | collective-permute-done | bytes 49184 | tf_op jit(solution)/shard_map/ppermute | solution.py:771
  82.1 6.4 %all-to-all-start.1 = ((bf16[16,16,640]{2,1,0:T(8,128)(2,1)}), bf16[16,16,640]{2,1,0:T(8,128)(2,1)S(1)}, u32[]{:S(2)}, u32[]{:S(2)}) async-start(bf16[16,16,640]{2,1,0:T(8,128)(2,1)} %shard_map.190), calls=%async_computation.1 | async-start | bytes 655360 | tf_op jit(solution)/shard_map/all_to_all | solution.py:712
  88.8 2.8 %collective-permute-start.7 = (bf16[1,16,896]{2,1,0:T(8,128)(2,1)S(1)}, bf16[1,16,896]{2,1,0:T(8,128)(2,1)S(1)}, u32[]{:S(2)}, u32[]{:S(2)}) collective-permute-start(bf16[1,16,896]{2,1,0:T(8,128)(2,1)S(1)} %get-tuple-element.100), channel_id=1, source_target_pairs={{0,16},{16,2},{2,18},{18,0},{1,17},{17,3},{3,19},{19,1},{4,20},{20... | collective-permute-start | bytes 86024 | tf_op jit(solution)/shard_map/ppermute | solution.py:708
  91.6 3.2 %collective-permute-start.8 = (bf16[1,16,896]{2,1,0:T(8,128)(2,1)S(1)}, bf16[1,16,896]{2,1,0:T(8,128)(2,1)S(1)}, u32[]{:S(2)}, u32[]{:S(2)}) collective-permute-start(bf16[1,16,896]{2,1,0:T(8,128)(2,1)S(1)} %get-tuple-element.101), channel_id=1, source_target_pairs={{0,2},{16,18},{2,0},{18,16},{1,3},{17,19},{3,1},{19,17},{4,6},{20,... | collective-permute-start | bytes 86024 | tf_op jit(solution)/shard_map/ppermute | solution.py:708
  99.5 7.2 %all-to-all-start.2 = ((bf16[16,16,640]{2,1,0:T(8,128)(2,1)}), bf16[16,16,640]{2,1,0:T(8,128)(2,1)S(1)}, u32[]{:S(2)}, u32[]{:S(2)}) async-start(bf16[16,16,640]{2,1,0:T(8,128)(2,1)} %bitcast.5), calls=%async_computation.2 | async-start | bytes 655360 | tf_op jit(solution)/shard_map/all_to_all | solution.py:712
  115.1 7.1 %all-to-all-start.3 = ((bf16[16,4,16,896]{3,2,1,0:T(8,128)(2,1)}), bf16[16,4,16,896]{3,2,1,0:T(8,128)(2,1)S(1)}, u32[]{:S(2)}, u32[]{:S(2)}) async-start(bf16[16,4,16,896]{3,2,1,0:T(8,128)(2,1)} %bitcast.16), calls=%async_computation.3 | async-start | bytes 3670016 | tf_op jit(solution)/shard_map/all_to_all | solution.py:712
  125.4 4.4 %collective-permute-done.21.refs_3_ = bf16[16,16,640]{2,1,0:T(8,128)(2,1)S(1)} collective-permute-done((bf16[16,16,640]{2,1,0:T(8,128)(2,1)S(1)}, bf16[16,16,640]{2,1,0:T(8,128)(2,1)S(1)}, u32[]{:S(2)}, u32[]{:S(2)}) %collective-permute-start.21) | collective-permute-done | bytes 327712 | tf_op jit(solution)/shard_map/ppermute | solution.py:708
  129.8 2.8 %collective-permute-done.20.refs_2_ = bf16[16,16,640]{2,1,0:T(8,128)(2,1)S(1)} collective-permute-done((bf16[16,16,640]{2,1,0:T(8,128)(2,1)S(1)}, bf16[16,16,640]{2,1,0:T(8,128)(2,1)S(1)}, u32[]{:S(2)}, u32[]{:S(2)}) %collective-permute-start.20) | collective-permute-done | bytes 327712 | tf_op jit(solution)/shard_map/ppermute | solution.py:708
  132.6 3.4 %collective-permute-done.19.refs_1_ = bf16[16,16,640]{2,1,0:T(8,128)(2,1)S(1)} collective-permute-done((bf16[16,16,640]{2,1,0:T(8,128)(2,1)S(1)}, bf16[16,16,640]{2,1,0:T(8,128)(2,1)S(1)}, u32[]{:S(2)}, u32[]{:S(2)}) %collective-permute-start.19) | collective-permute-done | bytes 327712 | tf_op jit(solution)/shard_map/ppermute | solution.py:708
  137.7 3.1 %shard_map.194 = (f32[768,768]{1,0:T(8,128)}, f32[768,768]{1,0:T(8,128)}, f32[83,768]{1,0:T(8,128)}) custom-call(bf16[16,16,640]{2,1,0:T(8,128)(2,1)S(1)} %all-to-all-done.2.refs_0_, bf16[16,16,640]{2,1,0:T(8,128)(2,1)S(1)} %collective-permute-done.19.refs_1_, bf16[16,16,640]{2,1,0:T(8,128)(2,1)S(1)} %collective-permute-done.20.refs_2_, ...), custom_call_target="tpu_custom_call" | custom-call | bytes 8000000 | tf_op jit(solution)/shard_map/pallas_call | solution.py:610
  145.9 3.1 %shard_map.196 = (f32[768,2304]{1,0:T(8,128)}, f32[32,768]{1,0:T(8,128)}, f32[1,1]{1,0:T(1,128)}) custom-call(bf16[16,4,16,896]{3,2,1,0:T(8,128)(2,1)S(1)} %collective-permute-done.26.plane, s32[1,32]{1,0:T(1,128)S(1)} %bitcast.13, f32[768,2304]{1,0:T(8,128)} %get-tuple-element.129._qkv, ...), custom_call_target="tpu_custom_call", output_to_operand_aliasing={{0}: (2, {})} | custom-call | bytes 6000000 | tf_op jit(solution)/shard_map/pallas_call | solution.py:593
  (83 shorter events, 37.4 us)
Async XLA Ops:
  2.0 12.0 %collective-permute-start = (bf16[2,16,768]{2,1,0:T(8,128)(2,1)S(1)}, bf16[2,16,768]{2,1,0:T(8,128)(2,1)S(1)}, u32[]{:S(2)}, u32[]{:S(2)}) collective-permute-start(bf16[2,16,768]{2,1,0:T(8,128)(2,1)S(1)} %get-tuple-element.76), channel_id=1, source_target_pairs={{0,4},{4,8},{8,12},{12,16},{16,20},{20,24},{24,28},{28,32},{32,36}... | collective-permute-start | bytes 147464 | tf_op jit(solution)/shard_map/ppermute | solution.py:658
  5.6 8.5 %collective-permute-start.1 = (bf16[2,16,768]{2,1,0:T(8,128)(2,1)S(1)}, bf16[2,16,768]{2,1,0:T(8,128)(2,1)S(1)}, u32[]{:S(2)}, u32[]{:S(2)}) collective-permute-start(bf16[2,16,768]{2,1,0:T(8,128)(2,1)S(1)} %get-tuple-element.77), channel_id=1, source_target_pairs={{4,0},{8,4},{12,8},{16,12},{20,16},{24,20},{28,24},{32,28},{36,32}... | collective-permute-start | bytes 147464 | tf_op jit(solution)/shard_map/ppermute | solution.py:659
  21.2 11.8 %collective-permute-start.3 = (bf16[2,83,1024]{2,1,0:T(8,128)(2,1)S(1)}, bf16[2,83,1024]{2,1,0:T(8,128)(2,1)S(1)}, u32[]{:S(2)}, u32[]{:S(2)}) collective-permute-start(bf16[2,83,1024]{2,1,0:T(8,128)(2,1)S(1)} %get-tuple-element.81.mine), channel_id=1, source_target_pairs={{0,2},{2,0},{1,3},{3,1},{4,6},{6,4},{5,7},{7,5},{8,10},{10,8},{9,1... | collective-permute-start | bytes 1019912 | tf_op jit(solution)/shard_map/ppermute | solution.py:813
  25.1 7.9 %collective-permute-start.5 = (bf16[2,83,1024]{2,1,0:T(8,128)(2,1)S(1)}, bf16[2,83,1024]{2,1,0:T(8,128)(2,1)S(1)}, u32[]{:S(2)}, u32[]{:S(2)}) collective-permute-start(bf16[2,83,1024]{2,1,0:T(8,128)(2,1)S(1)} %get-tuple-element.81.mine), channel_id=1, source_target_pairs={{0,1},{1,0},{2,3},{3,2},{4,5},{5,4},{6,7},{7,6},{8,9},{9,8},{10,11... | collective-permute-start | bytes 1019912 | tf_op jit(solution)/shard_map/ppermute | solution.py:814
  49.7 32.4 %all-to-all-start = ((bf16[16,4,16,896]{3,2,1,0:T(8,128)(2,1)}), bf16[16,4,16,896]{3,2,1,0:T(8,128)(2,1)S(1)}, u32[]{:S(2)}, u32[]{:S(2)}) async-start(bf16[16,4,16,896]{3,2,1,0:T(8,128)(2,1)} %shard_map.187), calls=%async_computation | async-start | bytes 3670016 | tf_op jit(solution)/shard_map/all_to_all | solution.py:712
  59.1 22.0 %collective-permute-start.11 = (bf16[16,16,640]{2,1,0:T(8,128)(2,1)S(1)}, bf16[16,16,640]{2,1,0:T(8,128)(2,1)S(1)}, u32[]{:S(2)}, u32[]{:S(2)}) collective-permute-start(bf16[16,16,640]{2,1,0:T(8,128)(2,1)S(1)} %get-tuple-element.106), channel_id=1, source_target_pairs={{0,16},{16,2},{2,18},{18,0},{1,17},{17,3},{3,19},{19,1},{4,20},{20... | collective-permute-start | bytes 983048 | tf_op jit(solution)/shard_map/ppermute | solution.py:708
  60.5 20.6 %collective-permute-start.12 = (bf16[16,16,640]{2,1,0:T(8,128)(2,1)S(1)}, bf16[16,16,640]{2,1,0:T(8,128)(2,1)S(1)}, u32[]{:S(2)}, u32[]{:S(2)}) collective-permute-start(bf16[16,16,640]{2,1,0:T(8,128)(2,1)S(1)} %get-tuple-element.107), channel_id=1, source_target_pairs={{0,2},{16,18},{2,0},{18,16},{1,3},{17,19},{3,1},{19,17},{4,6},{20,... | collective-permute-start | bytes 983048 | tf_op jit(solution)/shard_map/ppermute | solution.py:708
  64.4 16.8 %collective-permute-start.13 = (bf16[16,16,640]{2,1,0:T(8,128)(2,1)S(1)}, bf16[16,16,640]{2,1,0:T(8,128)(2,1)S(1)}, u32[]{:S(2)}, u32[]{:S(2)}) collective-permute-start(bf16[16,16,640]{2,1,0:T(8,128)(2,1)S(1)} %get-tuple-element.108), channel_id=1, source_target_pairs={{0,18},{16,0},{2,16},{18,2},{1,19},{17,1},{3,17},{19,3},{4,22},{20... | collective-permute-start | bytes 983048 | tf_op jit(solution)/shard_map/ppermute | solution.py:708
  65.1 13.5 %collective-permute-start.14 = (bf16[2,16,768]{2,1,0:T(8,128)(2,1)S(1)}, bf16[2,16,768]{2,1,0:T(8,128)(2,1)S(1)}, u32[]{:S(2)}, u32[]{:S(2)}) collective-permute-start(bf16[2,16,768]{2,1,0:T(8,128)(2,1)S(1)} %get-tuple-element.109), channel_id=1, source_target_pairs={{4,0},{8,4},{12,8},{16,12},{20,16},{24,20},{28,24},{32,28},{36,32}... | collective-permute-start | bytes 147464 | tf_op jit(solution)/shard_map/ppermute | solution.py:771
  70.4 10.7 %collective-permute-start.15 = (bf16[2,16,768]{2,1,0:T(8,128)(2,1)S(1)}, bf16[2,16,768]{2,1,0:T(8,128)(2,1)S(1)}, u32[]{:S(2)}, u32[]{:S(2)}) collective-permute-start(bf16[2,16,768]{2,1,0:T(8,128)(2,1)S(1)} %get-tuple-element.110), channel_id=1, source_target_pairs={{0,4},{4,8},{8,12},{12,16},{16,20},{20,24},{24,28},{28,32},{32,36}... | collective-permute-start | bytes 147464 | tf_op jit(solution)/shard_map/ppermute | solution.py:772
  82.1 13.9 %all-to-all-start.1 = ((bf16[16,16,640]{2,1,0:T(8,128)(2,1)}), bf16[16,16,640]{2,1,0:T(8,128)(2,1)S(1)}, u32[]{:S(2)}, u32[]{:S(2)}) async-start(bf16[16,16,640]{2,1,0:T(8,128)(2,1)} %shard_map.190), calls=%async_computation.1 | async-start | bytes 655360 | tf_op jit(solution)/shard_map/all_to_all | solution.py:712
  88.8 7.2 %collective-permute-start.7 = (bf16[1,16,896]{2,1,0:T(8,128)(2,1)S(1)}, bf16[1,16,896]{2,1,0:T(8,128)(2,1)S(1)}, u32[]{:S(2)}, u32[]{:S(2)}) collective-permute-start(bf16[1,16,896]{2,1,0:T(8,128)(2,1)S(1)} %get-tuple-element.100), channel_id=1, source_target_pairs={{0,16},{16,2},{2,18},{18,0},{1,17},{17,3},{3,19},{19,1},{4,20},{20... | collective-permute-start | bytes 86024 | tf_op jit(solution)/shard_map/ppermute | solution.py:708
  91.6 5.4 %collective-permute-start.8 = (bf16[1,16,896]{2,1,0:T(8,128)(2,1)S(1)}, bf16[1,16,896]{2,1,0:T(8,128)(2,1)S(1)}, u32[]{:S(2)}, u32[]{:S(2)}) collective-permute-start(bf16[1,16,896]{2,1,0:T(8,128)(2,1)S(1)} %get-tuple-element.101), channel_id=1, source_target_pairs={{0,2},{16,18},{2,0},{18,16},{1,3},{17,19},{3,1},{19,17},{4,6},{20,... | collective-permute-start | bytes 86024 | tf_op jit(solution)/shard_map/ppermute | solution.py:708
  94.9 3.9 %collective-permute-start.9 = (bf16[1,16,896]{2,1,0:T(8,128)(2,1)S(1)}, bf16[1,16,896]{2,1,0:T(8,128)(2,1)S(1)}, u32[]{:S(2)}, u32[]{:S(2)}) collective-permute-start(bf16[1,16,896]{2,1,0:T(8,128)(2,1)S(1)} %get-tuple-element.102), channel_id=1, source_target_pairs={{0,18},{16,0},{2,16},{18,2},{1,19},{17,1},{3,17},{19,3},{4,22},{20... | collective-permute-start | bytes 86024 | tf_op jit(solution)/shard_map/ppermute | solution.py:708
  99.5 14.2 %all-to-all-start.2 = ((bf16[16,16,640]{2,1,0:T(8,128)(2,1)}), bf16[16,16,640]{2,1,0:T(8,128)(2,1)S(1)}, u32[]{:S(2)}, u32[]{:S(2)}) async-start(bf16[16,16,640]{2,1,0:T(8,128)(2,1)} %bitcast.5), calls=%async_computation.2 | async-start | bytes 655360 | tf_op jit(solution)/shard_map/all_to_all | solution.py:712
  106.7 4.2 %collective-permute-start.18 = (bf16[1,16,896]{2,1,0:T(8,128)(2,1)S(1)}, bf16[1,16,896]{2,1,0:T(8,128)(2,1)S(1)}, u32[]{:S(2)}, u32[]{:S(2)}) collective-permute-start(bf16[1,16,896]{2,1,0:T(8,128)(2,1)S(1)} %get-tuple-element.120.one), channel_id=1, source_target_pairs={{0,18},{16,0},{2,16},{18,2},{1,19},{17,1},{3,17},{19,3},{4,22},{20... | collective-permute-start | bytes 86024 | tf_op jit(solution)/shard_map/ppermute | solution.py:708
  108.0 5.4 %collective-permute-start.17 = (bf16[1,16,896]{2,1,0:T(8,128)(2,1)S(1)}, bf16[1,16,896]{2,1,0:T(8,128)(2,1)S(1)}, u32[]{:S(2)}, u32[]{:S(2)}) collective-permute-start(bf16[1,16,896]{2,1,0:T(8,128)(2,1)S(1)} %get-tuple-element.120.one), channel_id=1, source_target_pairs={{0,2},{16,18},{2,0},{18,16},{1,3},{17,19},{3,1},{19,17},{4,6},{20,... | collective-permute-start | bytes 86024 | tf_op jit(solution)/shard_map/ppermute | solution.py:708
  108.5 5.1 %collective-permute-start.16 = (bf16[1,16,896]{2,1,0:T(8,128)(2,1)S(1)}, bf16[1,16,896]{2,1,0:T(8,128)(2,1)S(1)}, u32[]{:S(2)}, u32[]{:S(2)}) collective-permute-start(bf16[1,16,896]{2,1,0:T(8,128)(2,1)S(1)} %get-tuple-element.120.one), channel_id=1, source_target_pairs={{0,16},{16,2},{2,18},{18,0},{1,17},{17,3},{3,19},{19,1},{4,20},{20... | collective-permute-start | bytes 86024 | tf_op jit(solution)/shard_map/ppermute | solution.py:708
  115.1 27.0 %all-to-all-start.3 = ((bf16[16,4,16,896]{3,2,1,0:T(8,128)(2,1)}), bf16[16,4,16,896]{3,2,1,0:T(8,128)(2,1)S(1)}, u32[]{:S(2)}, u32[]{:S(2)}) async-start(bf16[16,4,16,896]{3,2,1,0:T(8,128)(2,1)} %bitcast.16), calls=%async_computation.3 | async-start | bytes 3670016 | tf_op jit(solution)/shard_map/all_to_all | solution.py:712
  122.3 7.6 %collective-permute-start.21 = (bf16[16,16,640]{2,1,0:T(8,128)(2,1)S(1)}, bf16[16,16,640]{2,1,0:T(8,128)(2,1)S(1)}, u32[]{:S(2)}, u32[]{:S(2)}) collective-permute-start(bf16[16,16,640]{2,1,0:T(8,128)(2,1)S(1)} %all-to-all-done.2.refs_0_), channel_id=1, source_target_pairs={{0,18},{16,0},{2,16},{18,2},{1,19},{17,1},{3,17},{19,3},{4,22},{20... | collective-permute-start | bytes 983048 | tf_op jit(solution)/shard_map/ppermute | solution.py:708
  123.9 8.7 %collective-permute-start.20 = (bf16[16,16,640]{2,1,0:T(8,128)(2,1)S(1)}, bf16[16,16,640]{2,1,0:T(8,128)(2,1)S(1)}, u32[]{:S(2)}, u32[]{:S(2)}) collective-permute-start(bf16[16,16,640]{2,1,0:T(8,128)(2,1)S(1)} %all-to-all-done.2.refs_0_), channel_id=1, source_target_pairs={{0,2},{16,18},{2,0},{18,16},{1,3},{17,19},{3,1},{19,17},{4,6},{20,... | collective-permute-start | bytes 983048 | tf_op jit(solution)/shard_map/ppermute | solution.py:708
  124.8 11.2 %collective-permute-start.19 = (bf16[16,16,640]{2,1,0:T(8,128)(2,1)S(1)}, bf16[16,16,640]{2,1,0:T(8,128)(2,1)S(1)}, u32[]{:S(2)}, u32[]{:S(2)}) collective-permute-start(bf16[16,16,640]{2,1,0:T(8,128)(2,1)S(1)} %all-to-all-done.2.refs_0_), channel_id=1, source_target_pairs={{0,16},{16,2},{2,18},{18,0},{1,17},{17,3},{3,19},{19,1},{4,20},{20... | collective-permute-start | bytes 983048 | tf_op jit(solution)/shard_map/ppermute | solution.py:708
  125.4 10.6 %collective-permute-start.22 = (bf16[16,16,640]{2,1,0:T(8,128)(2,1)S(1)}, bf16[16,16,640]{2,1,0:T(8,128)(2,1)S(1)}, u32[]{:S(2)}, u32[]{:S(2)}) collective-permute-start(bf16[16,16,640]{2,1,0:T(8,128)(2,1)S(1)} %all-to-all-done.2.refs_0_), channel_id=1, source_target_pairs={{0,1},{1,0},{2,3},{3,2},{4,5},{5,4},{6,7},{7,6},{8,9},{9,8},{10,11... | collective-permute-start | bytes 983048 | tf_op jit(solution)/shard_map/ppermute | solution.py:801
  129.8 6.2 %collective-permute-start.25 = (bf16[16,16,640]{2,1,0:T(8,128)(2,1)S(1)}, bf16[16,16,640]{2,1,0:T(8,128)(2,1)S(1)}, u32[]{:S(2)}, u32[]{:S(2)}) collective-permute-start(bf16[16,16,640]{2,1,0:T(8,128)(2,1)S(1)} %collective-permute-done.21.refs_3_), channel_id=1, source_target_pairs={{0,1},{1,0},{2,3},{3,2},{4,5},{5,4},{6,7},{7,6},{8,9},{9,8},{10,11... | collective-permute-start | bytes 983048 | tf_op jit(solution)/shard_map/ppermute | solution.py:801
  (21 other events, 215.8 us)

commit v7 on v6

--- a/solution.py
+++ b/solution.py
@@ -553,14 +553,16 @@
                     noise[row : row + 16, column : column + TILE] = piece
                 else:
                     total = piece
-        base = slice(192 * level, 192 * level + 192)
-        for section in range(3):
-            start = pl.multiple_of(2 * wide * section + wide * core, TILE)
-            copies += fetch(
-                [held.at[base, wide * section : wide * (section + 1)]],
-                [g_qkv.at[base, pl.ds(start, wide)]],
-                sems.at[len(copies) : len(copies) + 1],
-            )
+            if group % 2 == 0:
+                continue
+            base = slice(48 * k - 48, 48 * k + 48)
+            for section in range(3):
+                start = pl.multiple_of(2 * wide * section + wide * core, TILE)
+                copies += fetch(
+                    [held.at[base, wide * section : wide * (section + 1)]],
+                    [g_qkv.at[base, pl.ds(start, wide)]],
+                    sems.at[len(copies) : len(copies) + 1],
+                )
     return copies, jnp.sum(total, keepdims=True)
 
 
@@ -596,7 +598,7 @@
         in_specs=[anywhere if i == 2 else VMEM for i in range(len(args))],
         out_specs=[anywhere, VMEM, VMEM],
         scratch_shapes=[
-            pltpu.VMEM((width, 3 * width // 2), F32), pltpu.SemaphoreType.DMA((12,)),
+            pltpu.VMEM((width, 3 * width // 2), F32), pltpu.SemaphoreType.DMA((24,)),
         ],
         input_output_aliases={2: 0} if before else {},
         compiler_params=pltpu.CompilerParams(vmem_limit_bytes=16 * MIB),

time: 151 us -> 151 us (level)
  no operation moved by 1% of the time
where the time goes in v7:
time: 151 us; the launch traced here: 149 us
  starting transfers between devices  65.5 us (43%)
  waiting for transfers between devices  42.2 us (28%)
  Pallas kernels  40.4 us (27%)
    pallas_call x14, Pallas kernels, call(): pl.pallas_call(body, out_shape=out_shape, in_specs=[SMEM if i in smem els...  31.6 us
    all_to_all x4, starting transfers between devices, swapped(): return lax.all_to_all(a, planes, 0, 0, tiled=True)  26.6 us
    ppermute x12, starting transfers between devices, shifted(): moved.append(lax.ppermute(piece, levels, pairs))  18.1 us
    ppermute x12, waiting for transfers between devices, shifted(): moved.append(lax.ppermute(piece, levels, pairs))  16 us
    ppermute x1, waiting for transfers between devices, gather_members(): far = lax.ppermute(forecast, 'zhi', swap)  7.85 us
    ppermute x1, waiting for transfers between devices, on_device(): from_next = lax.ppermute(d_low, SPACE, down)  6.22 us
    pallas_call x2, Pallas kernels, unpack(): pl.pallas_call(body, out_shape=[jax.ShapeDtypeStruct(shape, F32) for shap...  5.75 us
    ppermute x1, starting transfers between devices, on_device(): high = lax.ppermute(sent_down, SPACE, down)  5.5 us
  transfers between devices with their start and end apart: 31, of which 17 were waited for; matrix products, arithmetic and copies ran while one was open for 0% of the time, Pallas kernels for 10%

profile of v7, /device:TPU:2, one launch (start us, length us, event | category | flops | bytes accessed | tf_op | source)
XLA Modules:
  0.0 149.3 jit_solution(13404761925771434829)
XLA Ops:
  2.0 3.5 %collective-permute-start = (bf16[2,16,768]{2,1,0:T(8,128)(2,1)S(1)}, bf16[2,16,768]{2,1,0:T(8,128)(2,1)S(1)}, u32[]{:S(2)}, u32[]{:S(2)}) collective-permute-start(bf16[2,16,768]{2,1,0:T(8,128)(2,1)S(1)} %get-tuple-element.76), channel_id=1, source_target_pairs={{0,4},{4,8},{8,12},{12,16},{16,20},{20,24},{24,28},{28,32},{32,36}... | collective-permute-start | bytes 147464 | tf_op jit(solution)/shard_map/ppermute | solution.py:660
  5.6 5.5 %collective-permute-start.1 = (bf16[2,16,768]{2,1,0:T(8,128)(2,1)S(1)}, bf16[2,16,768]{2,1,0:T(8,128)(2,1)S(1)}, u32[]{:S(2)}, u32[]{:S(2)}) collective-permute-start(bf16[2,16,768]{2,1,0:T(8,128)(2,1)S(1)} %get-tuple-element.77), channel_id=1, source_target_pairs={{4,0},{8,4},{12,8},{16,12},{20,16},{24,20},{28,24},{32,28},{36,32}... | collective-permute-start | bytes 147464 | tf_op jit(solution)/shard_map/ppermute | solution.py:661
  11.1 2.9 %shard_map.180 = (bf16[2,128,768]{2,1,0:T(8,128)(2,1)S(1)}, bf16[256,768]{1,0:T(8,128)(2,1)S(1)}, bf16[256,2304]{1,0:T(8,128)(2,1)S(1)}, bf16[768,2304]{1,0:T(8,128)(2,1)S(1)}) custom-call(bf16[2,768,128]{2,1,0:T(8,128)(2,1)} %latent_far.3, f32[2,32]{1,0:T(2,128)} %noise.3, f32[32,768]{1,0:T(8,128)} %w_noise.3, bf16[768,2304]{1,0:T(8,128)(2,1)} %w_qkv.1), custom_call_target="tpu_custom_call" | custom-call | flops 905969664 | bytes 4030720 | tf_op jit(solution)/shard_map/pallas_call | solution.py:46
  14.1 7.0 %shard_map.182 = (bf16[320,768]{1,0:T(8,128)(2,1)S(1)}, bf16[64,1536]{1,0:T(8,128)(2,1)S(1)}, bf16[256,768]{1,0:T(8,128)(2,1)S(1)}, bf16[256,768]{1,0:T(8,128)(2...) custom-call(bf16[2,128,768]{2,1,0:T(8,128)(2,1)S(1)} %get-tuple-elem, ...), custom_call_target="tpu_custom_call" | custom-call | flops 3000000000 | bytes 8205568 | tf_op jit(solution)/shard_map/pallas_call | solution.py:46
  21.2 3.9 %collective-permute-start.3 = (bf16[2,83,1024]{2,1,0:T(8,128)(2,1)S(1)}, bf16[2,83,1024]{2,1,0:T(8,128)(2,1)S(1)}, u32[]{:S(2)}, u32[]{:S(2)}) collective-permute-start(bf16[2,83,1024]{2,1,0:T(8,128)(2,1)S(1)} %get-tuple-element.81.mine), channel_id=1, source_target_pairs={{0,2},{2,0},{1,3},{3,1},{4,6},{6,4},{5,7},{7,5},{8,10},{10,8},{9,1... | collective-permute-start | bytes 1019912 | tf_op jit(solution)/shard_map/ppermute | solution.py:815
  25.1 7.8 %collective-permute-done.3.rest_0_ = bf16[2,83,1024]{2,1,0:T(8,128)(2,1)S(1)} collective-permute-done((bf16[2,83,1024]{2,1,0:T(8,128)(2,1)S(1)}, bf16[2,83,1024]{2,1,0:T(8,128)(2,1)S(1)}, u32[]{:S(2)}, u32[]{:S(2)}) %collective-permute-start.3) | collective-permute-done | bytes 340000 | tf_op jit(solution)/shard_map/ppermute | solution.py:815
  34.7 6.0 %shard_map.184 = (bf16[256,768]{1,0:T(8,128)(2,1)S(1)}, bf16[256,768]{1,0:T(8,128)(2,1)S(1)}, bf16[64,16,640]{2,1,0:T(8,128)(2,1)S(1)}, bf16[64,16,640]{2,1,0:T(8,128)(2,1)S(1)}, bf16[16,128]{1,0:T(8,128)(2,1)S(1)}) custom-call(s32[32]{0:T(128)S(1)} %copy-done.6, bf16[2,83,1024]{2,1,0:T(8,128)(2,1)S(1)} %get-tuple-element.81.mine, ...), custom_call_target="tpu_custom_call" | custom-call | flops 6000000000 | bytes 11530880 | tf_op jit(solution)/shard_map/pallas_call | solution.py:46
  40.7 2.7 %shard_map.185 = (bf16[2,256,1152]{2,1,0:T(8,128)(2,1)S(1)}, bf16[2,64,768]{2,1,0:T(8,128)(2,1)S(1)}, bf16[320,1152]{1,0:T(8,128)(2,1)S(1)}) custom-call(bf16[256,2304]{1,0:T(8,128)(2,1)S(1)} %get-tuple-element.75.proj, bf16[64,1536]{1,0:T(8,128)(2,1)S(1)} %get-tuple-element.80.proj_rim, s32[8,128]{1,0:T(8,128)S(1)} %copy-done.12, s32[1,128]{1,0:T(1,128)S(1)} %bitcast.15, ...), custom_call_target="tpu_custom_call" | custom-call | flops 2000000000 | bytes 1774080 | tf_op jit(solution)/shard_map/pallas_call | solution.py:46
  46.6 3.0 %shard_map.187 = bf16[16,4,16,896]{3,2,1,0:T(8,128)(2,1)} custom-call(bf16[320,768]{1,0:T(8,128)(2,1)S(1)} %get-tuple-element.79.normed, bf16[320,768]{1,0:T(8,128)(2,1)S(1)} %collective-permute-done.2.normed_theirs, bf16[2,256,1152]{2,1,0:T(8,128)(2,1)S(1)} %get-tuple-element.90.d_proj, bf16[2,64,768]{2,1,0:T(8,128)(2,1)S(1)} %get-tuple-element.91.d_rim, ...), custom_call_target="tpu_custom_call" | custom-call | flops 2000000000 | bytes 3149824 | tf_op jit(solution)/shard_map/pallas_call | solution.py:46
  49.7 5.9 %all-to-all-start = ((bf16[16,4,16,896]{3,2,1,0:T(8,128)(2,1)}), bf16[16,4,16,896]{3,2,1,0:T(8,128)(2,1)S(1)}, u32[]{:S(2)}, u32[]{:S(2)}) async-start(bf16[16,4,16,896]{3,2,1,0:T(8,128)(2,1)} %shard_map.187), calls=%async_computation | async-start | bytes 3670016 | tf_op jit(solution)/shard_map/all_to_all | solution.py:714
  55.6 3.2 %collective-permute-done.10 = bf16[64,16,640]{2,1,0:T(8,128)(2,1)S(1)} collective-permute-done((bf16[64,16,640]{2,1,0:T(8,128)(2,1)}, bf16[64,16,640]{2,1,0:T(8,128)(2,1)S(1)}, u32[]{:S(2)}, u32[]{:S(2)}) %collective-permute-start.10) | collective-permute-done | bytes 1310752 | tf_op jit(solution)/shard_map/ppermute | solution.py:735
  60.5 3.9 %collective-permute-start.12 = (bf16[16,16,640]{2,1,0:T(8,128)(2,1)S(1)}, bf16[16,16,640]{2,1,0:T(8,128)(2,1)S(1)}, u32[]{:S(2)}, u32[]{:S(2)}) collective-permute-start(bf16[16,16,640]{2,1,0:T(8,128)(2,1)S(1)} %get-tuple-element.107), channel_id=1, source_target_pairs={{0,2},{16,18},{2,0},{18,16},{1,3},{17,19},{3,1},{19,17},{4,6},{20,... | collective-permute-start | bytes 983048 | tf_op jit(solution)/shard_map/ppermute | solution.py:710
  65.1 5.3 %collective-permute-start.14 = (bf16[2,16,768]{2,1,0:T(8,128)(2,1)S(1)}, bf16[2,16,768]{2,1,0:T(8,128)(2,1)S(1)}, u32[]{:S(2)}, u32[]{:S(2)}) collective-permute-start(bf16[2,16,768]{2,1,0:T(8,128)(2,1)S(1)} %get-tuple-element.109), channel_id=1, source_target_pairs={{4,0},{8,4},{12,8},{16,12},{20,16},{24,20},{28,24},{32,28},{36,32}... | collective-permute-start | bytes 147464 | tf_op jit(solution)/shard_map/ppermute | solution.py:773
  72.3 6.2 %collective-permute-done.14.from_next = bf16[2,16,768]{2,1,0:T(8,128)(2,1)S(1)} collective-permute-done((bf16[2,16,768]{2,1,0:T(8,128)(2,1)S(1)}, bf16[2,16,768]{2,1,0:T(8,128)(2,1)S(1)}, u32[]{:S(2)}, u32[]{:S(2)}) %collective-permute-start.14) | collective-permute-done | bytes 49184 | tf_op jit(solution)/shard_map/ppermute | solution.py:773
  82.1 6.4 %all-to-all-start.1 = ((bf16[16,16,640]{2,1,0:T(8,128)(2,1)}), bf16[16,16,640]{2,1,0:T(8,128)(2,1)S(1)}, u32[]{:S(2)}, u32[]{:S(2)}) async-start(bf16[16,16,640]{2,1,0:T(8,128)(2,1)} %shard_map.190), calls=%async_computation.1 | async-start | bytes 655360 | tf_op jit(solution)/shard_map/all_to_all | solution.py:714
  88.8 2.8 %collective-permute-start.7 = (bf16[1,16,896]{2,1,0:T(8,128)(2,1)S(1)}, bf16[1,16,896]{2,1,0:T(8,128)(2,1)S(1)}, u32[]{:S(2)}, u32[]{:S(2)}) collective-permute-start(bf16[1,16,896]{2,1,0:T(8,128)(2,1)S(1)} %get-tuple-element.100), channel_id=1, source_target_pairs={{0,16},{16,2},{2,18},{18,0},{1,17},{17,3},{3,19},{19,1},{4,20},{20... | collective-permute-start | bytes 86024 | tf_op jit(solution)/shard_map/ppermute | solution.py:710
  91.6 3.2 %collective-permute-start.8 = (bf16[1,16,896]{2,1,0:T(8,128)(2,1)S(1)}, bf16[1,16,896]{2,1,0:T(8,128)(2,1)S(1)}, u32[]{:S(2)}, u32[]{:S(2)}) collective-permute-start(bf16[1,16,896]{2,1,0:T(8,128)(2,1)S(1)} %get-tuple-element.101), channel_id=1, source_target_pairs={{0,2},{16,18},{2,0},{18,16},{1,3},{17,19},{3,1},{19,17},{4,6},{20,... | collective-permute-start | bytes 86024 | tf_op jit(solution)/shard_map/ppermute | solution.py:710
  99.5 7.2 %all-to-all-start.2 = ((bf16[16,16,640]{2,1,0:T(8,128)(2,1)}), bf16[16,16,640]{2,1,0:T(8,128)(2,1)S(1)}, u32[]{:S(2)}, u32[]{:S(2)}) async-start(bf16[16,16,640]{2,1,0:T(8,128)(2,1)} %bitcast.5), calls=%async_computation.2 | async-start | bytes 655360 | tf_op jit(solution)/shard_map/all_to_all | solution.py:714
  115.1 7.1 %all-to-all-start.3 = ((bf16[16,4,16,896]{3,2,1,0:T(8,128)(2,1)}), bf16[16,4,16,896]{3,2,1,0:T(8,128)(2,1)S(1)}, u32[]{:S(2)}, u32[]{:S(2)}) async-start(bf16[16,4,16,896]{3,2,1,0:T(8,128)(2,1)} %bitcast.16), calls=%async_computation.3 | async-start | bytes 3670016 | tf_op jit(solution)/shard_map/all_to_all | solution.py:714
  125.4 4.4 %collective-permute-done.21.refs_3_ = bf16[16,16,640]{2,1,0:T(8,128)(2,1)S(1)} collective-permute-done((bf16[16,16,640]{2,1,0:T(8,128)(2,1)S(1)}, bf16[16,16,640]{2,1,0:T(8,128)(2,1)S(1)}, u32[]{:S(2)}, u32[]{:S(2)}) %collective-permute-start.21) | collective-permute-done | bytes 327712 | tf_op jit(solution)/shard_map/ppermute | solution.py:710
  129.8 2.8 %collective-permute-done.20.refs_2_ = bf16[16,16,640]{2,1,0:T(8,128)(2,1)S(1)} collective-permute-done((bf16[16,16,640]{2,1,0:T(8,128)(2,1)S(1)}, bf16[16,16,640]{2,1,0:T(8,128)(2,1)S(1)}, u32[]{:S(2)}, u32[]{:S(2)}) %collective-permute-start.20) | collective-permute-done | bytes 327712 | tf_op jit(solution)/shard_map/ppermute | solution.py:710
  132.6 3.4 %collective-permute-done.19.refs_1_ = bf16[16,16,640]{2,1,0:T(8,128)(2,1)S(1)} collective-permute-done((bf16[16,16,640]{2,1,0:T(8,128)(2,1)S(1)}, bf16[16,16,640]{2,1,0:T(8,128)(2,1)S(1)}, u32[]{:S(2)}, u32[]{:S(2)}) %collective-permute-start.19) | collective-permute-done | bytes 327712 | tf_op jit(solution)/shard_map/ppermute | solution.py:710
  137.7 3.1 %shard_map.194 = (f32[768,768]{1,0:T(8,128)}, f32[768,768]{1,0:T(8,128)}, f32[83,768]{1,0:T(8,128)}) custom-call(bf16[16,16,640]{2,1,0:T(8,128)(2,1)S(1)} %all-to-all-done.2.refs_0_, bf16[16,16,640]{2,1,0:T(8,128)(2,1)S(1)} %collective-permute-done.19.refs_1_, bf16[16,16,640]{2,1,0:T(8,128)(2,1)S(1)} %collective-permute-done.20.refs_2_, ...), custom_call_target="tpu_custom_call" | custom-call | bytes 8000000 | tf_op jit(solution)/shard_map/pallas_call | solution.py:612
  145.9 3.2 %shard_map.196 = (f32[768,2304]{1,0:T(8,128)}, f32[32,768]{1,0:T(8,128)}, f32[1,1]{1,0:T(1,128)}) custom-call(bf16[16,4,16,896]{3,2,1,0:T(8,128)(2,1)S(1)} %collective-permute-done.26.plane, s32[1,32]{1,0:T(1,128)S(1)} %bitcast.13, f32[768,2304]{1,0:T(8,128)} %get-tuple-element.129._qkv, ...), custom_call_target="tpu_custom_call", output_to_operand_aliasing={{0}: (2, {})} | custom-call | bytes 6000000 | tf_op jit(solution)/shard_map/pallas_call | solution.py:595
  (83 shorter events, 37.4 us)
Async XLA Ops:
  2.0 12.0 %collective-permute-start = (bf16[2,16,768]{2,1,0:T(8,128)(2,1)S(1)}, bf16[2,16,768]{2,1,0:T(8,128)(2,1)S(1)}, u32[]{:S(2)}, u32[]{:S(2)}) collective-permute-start(bf16[2,16,768]{2,1,0:T(8,128)(2,1)S(1)} %get-tuple-element.76), channel_id=1, source_target_pairs={{0,4},{4,8},{8,12},{12,16},{16,20},{20,24},{24,28},{28,32},{32,36}... | collective-permute-start | bytes 147464 | tf_op jit(solution)/shard_map/ppermute | solution.py:660
  5.6 8.5 %collective-permute-start.1 = (bf16[2,16,768]{2,1,0:T(8,128)(2,1)S(1)}, bf16[2,16,768]{2,1,0:T(8,128)(2,1)S(1)}, u32[]{:S(2)}, u32[]{:S(2)}) collective-permute-start(bf16[2,16,768]{2,1,0:T(8,128)(2,1)S(1)} %get-tuple-element.77), channel_id=1, source_target_pairs={{4,0},{8,4},{12,8},{16,12},{20,16},{24,20},{28,24},{32,28},{36,32}... | collective-permute-start | bytes 147464 | tf_op jit(solution)/shard_map/ppermute | solution.py:661
  21.2 11.8 %collective-permute-start.3 = (bf16[2,83,1024]{2,1,0:T(8,128)(2,1)S(1)}, bf16[2,83,1024]{2,1,0:T(8,128)(2,1)S(1)}, u32[]{:S(2)}, u32[]{:S(2)}) collective-permute-start(bf16[2,83,1024]{2,1,0:T(8,128)(2,1)S(1)} %get-tuple-element.81.mine), channel_id=1, source_target_pairs={{0,2},{2,0},{1,3},{3,1},{4,6},{6,4},{5,7},{7,5},{8,10},{10,8},{9,1... | collective-permute-start | bytes 1019912 | tf_op jit(solution)/shard_map/ppermute | solution.py:815
  25.1 7.9 %collective-permute-start.5 = (bf16[2,83,1024]{2,1,0:T(8,128)(2,1)S(1)}, bf16[2,83,1024]{2,1,0:T(8,128)(2,1)S(1)}, u32[]{:S(2)}, u32[]{:S(2)}) collective-permute-start(bf16[2,83,1024]{2,1,0:T(8,128)(2,1)S(1)} %get-tuple-element.81.mine), channel_id=1, source_target_pairs={{0,1},{1,0},{2,3},{3,2},{4,5},{5,4},{6,7},{7,6},{8,9},{9,8},{10,11... | collective-permute-start | bytes 1019912 | tf_op jit(solution)/shard_map/ppermute | solution.py:816
  49.7 32.4 %all-to-all-start = ((bf16[16,4,16,896]{3,2,1,0:T(8,128)(2,1)}), bf16[16,4,16,896]{3,2,1,0:T(8,128)(2,1)S(1)}, u32[]{:S(2)}, u32[]{:S(2)}) async-start(bf16[16,4,16,896]{3,2,1,0:T(8,128)(2,1)} %shard_map.187), calls=%async_computation | async-start | bytes 3670016 | tf_op jit(solution)/shard_map/all_to_all | solution.py:714
  59.1 22.0 %collective-permute-start.11 = (bf16[16,16,640]{2,1,0:T(8,128)(2,1)S(1)}, bf16[16,16,640]{2,1,0:T(8,128)(2,1)S(1)}, u32[]{:S(2)}, u32[]{:S(2)}) collective-permute-start(bf16[16,16,640]{2,1,0:T(8,128)(2,1)S(1)} %get-tuple-element.106), channel_id=1, source_target_pairs={{0,16},{16,2},{2,18},{18,0},{1,17},{17,3},{3,19},{19,1},{4,20},{20... | collective-permute-start | bytes 983048 | tf_op jit(solution)/shard_map/ppermute | solution.py:710
  60.5 20.6 %collective-permute-start.12 = (bf16[16,16,640]{2,1,0:T(8,128)(2,1)S(1)}, bf16[16,16,640]{2,1,0:T(8,128)(2,1)S(1)}, u32[]{:S(2)}, u32[]{:S(2)}) collective-permute-start(bf16[16,16,640]{2,1,0:T(8,128)(2,1)S(1)} %get-tuple-element.107), channel_id=1, source_target_pairs={{0,2},{16,18},{2,0},{18,16},{1,3},{17,19},{3,1},{19,17},{4,6},{20,... | collective-permute-start | bytes 983048 | tf_op jit(solution)/shard_map/ppermute | solution.py:710
  64.4 16.8 %collective-permute-start.13 = (bf16[16,16,640]{2,1,0:T(8,128)(2,1)S(1)}, bf16[16,16,640]{2,1,0:T(8,128)(2,1)S(1)}, u32[]{:S(2)}, u32[]{:S(2)}) collective-permute-start(bf16[16,16,640]{2,1,0:T(8,128)(2,1)S(1)} %get-tuple-element.108), channel_id=1, source_target_pairs={{0,18},{16,0},{2,16},{18,2},{1,19},{17,1},{3,17},{19,3},{4,22},{20... | collective-permute-start | bytes 983048 | tf_op jit(solution)/shard_map/ppermute | solution.py:710
  65.1 13.5 %collective-permute-start.14 = (bf16[2,16,768]{2,1,0:T(8,128)(2,1)S(1)}, bf16[2,16,768]{2,1,0:T(8,128)(2,1)S(1)}, u32[]{:S(2)}, u32[]{:S(2)}) collective-permute-start(bf16[2,16,768]{2,1,0:T(8,128)(2,1)S(1)} %get-tuple-element.109), channel_id=1, source_target_pairs={{4,0},{8,4},{12,8},{16,12},{20,16},{24,20},{28,24},{32,28},{36,32}... | collective-permute-start | bytes 147464 | tf_op jit(solution)/shard_map/ppermute | solution.py:773
  70.4 10.7 %collective-permute-start.15 = (bf16[2,16,768]{2,1,0:T(8,128)(2,1)S(1)}, bf16[2,16,768]{2,1,0:T(8,128)(2,1)S(1)}, u32[]{:S(2)}, u32[]{:S(2)}) collective-permute-start(bf16[2,16,768]{2,1,0:T(8,128)(2,1)S(1)} %get-tuple-element.110), channel_id=1, source_target_pairs={{0,4},{4,8},{8,12},{12,16},{16,20},{20,24},{24,28},{28,32},{32,36}... | collective-permute-start | bytes 147464 | tf_op jit(solution)/shard_map/ppermute | solution.py:774
  82.1 13.9 %all-to-all-start.1 = ((bf16[16,16,640]{2,1,0:T(8,128)(2,1)}), bf16[16,16,640]{2,1,0:T(8,128)(2,1)S(1)}, u32[]{:S(2)}, u32[]{:S(2)}) async-start(bf16[16,16,640]{2,1,0:T(8,128)(2,1)} %shard_map.190), calls=%async_computation.1 | async-start | bytes 655360 | tf_op jit(solution)/shard_map/all_to_all | solution.py:714
  88.8 7.2 %collective-permute-start.7 = (bf16[1,16,896]{2,1,0:T(8,128)(2,1)S(1)}, bf16[1,16,896]{2,1,0:T(8,128)(2,1)S(1)}, u32[]{:S(2)}, u32[]{:S(2)}) collective-permute-start(bf16[1,16,896]{2,1,0:T(8,128)(2,1)S(1)} %get-tuple-element.100), channel_id=1, source_target_pairs={{0,16},{16,2},{2,18},{18,0},{1,17},{17,3},{3,19},{19,1},{4,20},{20... | collective-permute-start | bytes 86024 | tf_op jit(solution)/shard_map/ppermute | solution.py:710
  91.6 5.4 %collective-permute-start.8 = (bf16[1,16,896]{2,1,0:T(8,128)(2,1)S(1)}, bf16[1,16,896]{2,1,0:T(8,128)(2,1)S(1)}, u32[]{:S(2)}, u32[]{:S(2)}) collective-permute-start(bf16[1,16,896]{2,1,0:T(8,128)(2,1)S(1)} %get-tuple-element.101), channel_id=1, source_target_pairs={{0,2},{16,18},{2,0},{18,16},{1,3},{17,19},{3,1},{19,17},{4,6},{20,... | collective-permute-start | bytes 86024 | tf_op jit(solution)/shard_map/ppermute | solution.py:710
  94.9 3.9 %collective-permute-start.9 = (bf16[1,16,896]{2,1,0:T(8,128)(2,1)S(1)}, bf16[1,16,896]{2,1,0:T(8,128)(2,1)S(1)}, u32[]{:S(2)}, u32[]{:S(2)}) collective-permute-start(bf16[1,16,896]{2,1,0:T(8,128)(2,1)S(1)} %get-tuple-element.102), channel_id=1, source_target_pairs={{0,18},{16,0},{2,16},{18,2},{1,19},{17,1},{3,17},{19,3},{4,22},{20... | collective-permute-start | bytes 86024 | tf_op jit(solution)/shard_map/ppermute | solution.py:710
  99.5 14.2 %all-to-all-start.2 = ((bf16[16,16,640]{2,1,0:T(8,128)(2,1)}), bf16[16,16,640]{2,1,0:T(8,128)(2,1)S(1)}, u32[]{:S(2)}, u32[]{:S(2)}) async-start(bf16[16,16,640]{2,1,0:T(8,128)(2,1)} %bitcast.5), calls=%async_computation.2 | async-start | bytes 655360 | tf_op jit(solution)/shard_map/all_to_all | solution.py:714
  106.7 4.2 %collective-permute-start.18 = (bf16[1,16,896]{2,1,0:T(8,128)(2,1)S(1)}, bf16[1,16,896]{2,1,0:T(8,128)(2,1)S(1)}, u32[]{:S(2)}, u32[]{:S(2)}) collective-permute-start(bf16[1,16,896]{2,1,0:T(8,128)(2,1)S(1)} %get-tuple-element.120.one), channel_id=1, source_target_pairs={{0,18},{16,0},{2,16},{18,2},{1,19},{17,1},{3,17},{19,3},{4,22},{20... | collective-permute-start | bytes 86024 | tf_op jit(solution)/shard_map/ppermute | solution.py:710
  108.0 5.4 %collective-permute-start.17 = (bf16[1,16,896]{2,1,0:T(8,128)(2,1)S(1)}, bf16[1,16,896]{2,1,0:T(8,128)(2,1)S(1)}, u32[]{:S(2)}, u32[]{:S(2)}) collective-permute-start(bf16[1,16,896]{2,1,0:T(8,128)(2,1)S(1)} %get-tuple-element.120.one), channel_id=1, source_target_pairs={{0,2},{16,18},{2,0},{18,16},{1,3},{17,19},{3,1},{19,17},{4,6},{20,... | collective-permute-start | bytes 86024 | tf_op jit(solution)/shard_map/ppermute | solution.py:710
  108.5 5.1 %collective-permute-start.16 = (bf16[1,16,896]{2,1,0:T(8,128)(2,1)S(1)}, bf16[1,16,896]{2,1,0:T(8,128)(2,1)S(1)}, u32[]{:S(2)}, u32[]{:S(2)}) collective-permute-start(bf16[1,16,896]{2,1,0:T(8,128)(2,1)S(1)} %get-tuple-element.120.one), channel_id=1, source_target_pairs={{0,16},{16,2},{2,18},{18,0},{1,17},{17,3},{3,19},{19,1},{4,20},{20... | collective-permute-start | bytes 86024 | tf_op jit(solution)/shard_map/ppermute | solution.py:710
  115.1 27.0 %all-to-all-start.3 = ((bf16[16,4,16,896]{3,2,1,0:T(8,128)(2,1)}), bf16[16,4,16,896]{3,2,1,0:T(8,128)(2,1)S(1)}, u32[]{:S(2)}, u32[]{:S(2)}) async-start(bf16[16,4,16,896]{3,2,1,0:T(8,128)(2,1)} %bitcast.16), calls=%async_computation.3 | async-start | bytes 3670016 | tf_op jit(solution)/shard_map/all_to_all | solution.py:714
  122.3 7.6 %collective-permute-start.21 = (bf16[16,16,640]{2,1,0:T(8,128)(2,1)S(1)}, bf16[16,16,640]{2,1,0:T(8,128)(2,1)S(1)}, u32[]{:S(2)}, u32[]{:S(2)}) collective-permute-start(bf16[16,16,640]{2,1,0:T(8,128)(2,1)S(1)} %all-to-all-done.2.refs_0_), channel_id=1, source_target_pairs={{0,18},{16,0},{2,16},{18,2},{1,19},{17,1},{3,17},{19,3},{4,22},{20... | collective-permute-start | bytes 983048 | tf_op jit(solution)/shard_map/ppermute | solution.py:710
  123.9 8.7 %collective-permute-start.20 = (bf16[16,16,640]{2,1,0:T(8,128)(2,1)S(1)}, bf16[16,16,640]{2,1,0:T(8,128)(2,1)S(1)}, u32[]{:S(2)}, u32[]{:S(2)}) collective-permute-start(bf16[16,16,640]{2,1,0:T(8,128)(2,1)S(1)} %all-to-all-done.2.refs_0_), channel_id=1, source_target_pairs={{0,2},{16,18},{2,0},{18,16},{1,3},{17,19},{3,1},{19,17},{4,6},{20,... | collective-permute-start | bytes 983048 | tf_op jit(solution)/shard_map/ppermute | solution.py:710
  124.8 11.2 %collective-permute-start.19 = (bf16[16,16,640]{2,1,0:T(8,128)(2,1)S(1)}, bf16[16,16,640]{2,1,0:T(8,128)(2,1)S(1)}, u32[]{:S(2)}, u32[]{:S(2)}) collective-permute-start(bf16[16,16,640]{2,1,0:T(8,128)(2,1)S(1)} %all-to-all-done.2.refs_0_), channel_id=1, source_target_pairs={{0,16},{16,2},{2,18},{18,0},{1,17},{17,3},{3,19},{19,1},{4,20},{20... | collective-permute-start | bytes 983048 | tf_op jit(solution)/shard_map/ppermute | solution.py:710
  125.4 10.6 %collective-permute-start.22 = (bf16[16,16,640]{2,1,0:T(8,128)(2,1)S(1)}, bf16[16,16,640]{2,1,0:T(8,128)(2,1)S(1)}, u32[]{:S(2)}, u32[]{:S(2)}) collective-permute-start(bf16[16,16,640]{2,1,0:T(8,128)(2,1)S(1)} %all-to-all-done.2.refs_0_), channel_id=1, source_target_pairs={{0,1},{1,0},{2,3},{3,2},{4,5},{5,4},{6,7},{7,6},{8,9},{9,8},{10,11... | collective-permute-start | bytes 983048 | tf_op jit(solution)/shard_map/ppermute | solution.py:803
  129.8 6.2 %collective-permute-start.25 = (bf16[16,16,640]{2,1,0:T(8,128)(2,1)S(1)}, bf16[16,16,640]{2,1,0:T(8,128)(2,1)S(1)}, u32[]{:S(2)}, u32[]{:S(2)}) collective-permute-start(bf16[16,16,640]{2,1,0:T(8,128)(2,1)S(1)} %collective-permute-done.21.refs_3_), channel_id=1, source_target_pairs={{0,1},{1,0},{2,3},{3,2},{4,5},{5,4},{6,7},{7,6},{8,9},{9,8},{10,11... | collective-permute-start | bytes 983048 | tf_op jit(solution)/shard_map/ppermute | solution.py:803
  (21 other events, 215.8 us)
